TPU v7x, 32 devices: a whole 2x2x4 slice. The times are simulated.
32 devices in a mesh: pb: 8 (over y, x, core), ka: 4 (over z).
Axes of the slice: x: 2, y: 2, z: 4, core: 2. Of those that a mesh axis runs over, the one named last changes fastest.
Arguments:
- tokens: bfloat16 [32768, 768], P(('pb', 'ka')), may hold values from -6 to 6
- sequence_ids: int32 [32768], P(('pb', 'ka')), may hold values from 0 to 31, as said below
- sequence_offsets: int32 [32768], P(('pb', 'ka')), may hold values from 0 to 2047, as said below
- signed_norm_gain: bfloat16 [768], replicated, may hold values from 0.099609375 to 1.8984375
- signed_norm_bias: bfloat16 [768], replicated, may hold values from -1.75 to 1.75
- signed_query: bfloat16 [768, 768], replicated, may hold values from -0.21875 to 0.21875
- signed_key: bfloat16 [768, 768], replicated, may hold values from -0.21875 to 0.21875
- signed_value: bfloat16 [768, 768], replicated, may hold values from -0.21875 to 0.21875
- signed_out: bfloat16 [768, 768], replicated, may hold values from -1.75 to 1.75
- signed_mlp_gain: bfloat16 [768], replicated, may hold values from 0.099609375 to 1.8984375
- signed_mlp_bias: bfloat16 [768], replicated, may hold values from -1.75 to 1.75
- signed_up: bfloat16 [768, 3072], replicated, may hold values from -0.21875 to 0.21875
- signed_up_bias: bfloat16 [3072], replicated, may hold values from -3 to 3
- signed_down: bfloat16 [3072, 768], replicated, may hold values from -0.109375 to 0.109375
- signed_down_bias: bfloat16 [768], replicated, may hold values from -1.75 to 1.75
- plain_norm_gain: bfloat16 [768], replicated, may hold values from 0.099609375 to 1.8984375
- plain_norm_bias: bfloat16 [768], replicated, may hold values from -1.75 to 1.75
- plain_query: bfloat16 [768, 768], replicated, may hold values from -0.21875 to 0.21875
- plain_key: bfloat16 [768, 768], replicated, may hold values from -0.21875 to 0.21875
- plain_value: bfloat16 [768, 768], replicated, may hold values from -0.21875 to 0.21875
- plain_out: bfloat16 [768, 768], replicated, may hold values from -1.75 to 1.75
- plain_mlp_gain: bfloat16 [768], replicated, may hold values from 0.099609375 to 1.8984375
- plain_mlp_bias: bfloat16 [768], replicated, may hold values from -1.75 to 1.75
- plain_up: bfloat16 [768, 3072], replicated, may hold values from -0.21875 to 0.21875
- plain_up_bias: bfloat16 [3072], replicated, may hold values from -3 to 3
- plain_down: bfloat16 [3072, 768], replicated, may hold values from -0.109375 to 0.109375
- plain_down_bias: bfloat16 [768], replicated, may hold values from -1.75 to 1.75
- cotangent: bfloat16 [32768, 768], P(('pb', 'ka')), may hold values from -6 to 6
Outputs:
- output: bfloat16 [32768, 768], P(('pb', 'ka'))
- input_gradient: float32 [32768, 768], P(('pb', 'ka'))
- signed_norm_gain_gradient: float32 [768], replicated
- signed_norm_bias_gradient: float32 [768], replicated
- signed_query_gradient: float32 [768, 768], P('pb', 'ka')
- signed_key_gradient: float32 [768, 768], P('pb', 'ka')
- signed_value_gradient: float32 [768, 768], P('pb', 'ka')
- signed_out_gradient: float32 [768, 768], P('pb', 'ka')
- signed_mlp_gain_gradient: float32 [768], replicated
- signed_mlp_bias_gradient: float32 [768], replicated
- signed_up_gradient: float32 [768, 3072], P('pb', 'ka')
- signed_up_bias_gradient: float32 [3072], replicated
- signed_down_gradient: float32 [3072, 768], P('pb', 'ka')
- signed_down_bias_gradient: float32 [768], replicated
- plain_norm_gain_gradient: float32 [768], replicated
- plain_norm_bias_gradient: float32 [768], replicated
- plain_query_gradient: float32 [768, 768], P('pb', 'ka')
- plain_key_gradient: float32 [768, 768], P('pb', 'ka')
- plain_value_gradient: float32 [768, 768], P('pb', 'ka')
- plain_out_gradient: float32 [768, 768], P('pb', 'ka')
- plain_mlp_gain_gradient: float32 [768], replicated
- plain_mlp_bias_gradient: float32 [768], replicated
- plain_up_gradient: float32 [768, 3072], P('pb', 'ka')
- plain_up_bias_gradient: float32 [3072], replicated
- plain_down_gradient: float32 [3072, 768], P('pb', 'ka')
- plain_down_bias_gradient: float32 [768], replicated
Inputs may be any that keep to these rules, and one draw needn't show every extreme that they name: `sequence_ids`: A sequence's tokens all lie in one group: rows b * 512 to (b + 1) * 512 - 1 of each device along ka at one index of pb, for one b below 2. A group holds one sequence of 2048 tokens or two of 1024; at half of the indices of pb every group holds two, at the other half one. Each half of a device's rows of a group belongs to one sequence, and every sequence has rows on every device along ka. `sequence_offsets`: the offsets of a sequence's tokens are 0 to its length minus 1, each once; within each half of a device's rows of a group they rise by one from row to row.
All inputs are finite; a program needn't handle non-finite values.
Results may differ from a plain program's by a relative error of at most 0.035.
Values may be sent and summed in bfloat16 or wider, within the bound.
No kernel may reach another device: no remote copies, remote signals or barrier semaphores. Data moves between devices by JAX's collectives and lax.ppermute only.
A program may use at most 704 MiB of HBM per device.

v0:
```python
import jax
import jax.numpy as jnp
from jax import lax
from jax.sharding import PartitionSpec as P

HEADS = 12
BATCH = 2


EPSILON = 1e-05
MASKED_FLOOR = -1e30


def layer_norm(values, gain, shift):
    centre = values - jnp.mean(values, axis=-1, keepdims=True)
    spread = jnp.mean(centre * centre, axis=-1, keepdims=True)
    return centre * lax.rsqrt(spread + EPSILON) * gain + shift


def norm_backward(values, gain, shift, upstream):
    _, pullback = jax.vjp(layer_norm, values, gain, shift)
    return pullback(upstream)


def exact_gelu(hidden):
    return jax.nn.gelu(hidden, approximate=False)


def split_heads(stacked):
    return stacked.reshape(stacked.shape[0], stacked.shape[1], HEADS, stacked.shape[2] // HEADS)


def merge_heads(stacked):
    return stacked.reshape(stacked.shape[0], stacked.shape[1], stacked.shape[2] * stacked.shape[3])


def score_scale(width):
    return (width // HEADS) ** (-0.5)


def contract_rows(left, right):
    return lax.dot_general(
        left, right, (((0,), (0,)), ((), ())), preferred_element_type=jnp.float32
    )


def pair_scores(queries, key_rows):
    scores = jnp.einsum(
        "bqhd,bkhd->bhqk",
        split_heads(queries),
        split_heads(key_rows),
        preferred_element_type=jnp.float32,
    )
    return scores * score_scale(queries.shape[2])


def pair_allowed(query_labels, key_labels):
    same_sequence = query_labels[0][:, :, None] == key_labels[0][:, None, :]
    causal = key_labels[1][:, None, :] <= query_labels[1][:, :, None]
    return (same_sequence & causal)[:, None]


def magnitude_of(scores, signed):
    if signed:
        return jnp.sqrt(scores * scores + 1.0)
    return scores


def finish(scores, magnitude, weights, signed):
    if signed:
        return weights * scores / magnitude
    return weights


def recompute(scores, allowed, log_total, signed):
    magnitude = magnitude_of(scores, signed)
    clipped = jnp.where(allowed, magnitude, MASKED_FLOOR)
    weights = jnp.where(allowed, jnp.exp(clipped - log_total[..., None]), 0.0)
    return (magnitude, weights, finish(scores, magnitude, weights, signed))


def score_gradient(scores, magnitude, weights, dprobs, delta, signed):
    if signed:
        ratio = scores / magnitude
        return (
            dprobs * weights / (magnitude * magnitude * magnitude)
            + weights * (dprobs * ratio - delta[..., None]) * ratio
        )
    return weights * (dprobs - delta[..., None])


def attend_by_queries(queries, key_rows, value_rows, own_labels, group_labels, signed):
    gathered = lax.all_gather(queries, "ka", axis=1, tiled=True)
    scores = pair_scores(gathered, key_rows)
    allowed = pair_allowed(group_labels, own_labels)
    magnitude = magnitude_of(scores, signed)
    clipped = jnp.where(allowed, magnitude, MASKED_FLOOR)
    highest = lax.pmax(jnp.max(clipped, axis=3).astype(jnp.bfloat16), "ka").astype(jnp.float32)
    raised = jnp.where(allowed, jnp.exp(clipped - highest[..., None]), 0.0)
    summed = lax.psum(jnp.sum(raised, axis=3).astype(jnp.bfloat16), "ka").astype(jnp.float32)
    probs = finish(scores, magnitude, raised / summed[..., None], signed).astype(jnp.bfloat16)
    term_parts = jnp.einsum(
        "bhqk,bkhd->bqhd", probs, split_heads(value_rows), preferred_element_type=jnp.float32
    )
    attended = lax.psum_scatter(
        merge_heads(term_parts).astype(jnp.bfloat16), "ka", scatter_dimension=1, tiled=True
    )
    return (attended, highest + jnp.log(summed))


def back_over_own_keys(
    gathered,
    grad_rows,
    key_rows,
    value_rows,
    log_total,
    own_labels,
    group_labels,
    signed,
    sum_delta,
    sum_queries,
):
    scores = pair_scores(gathered, key_rows)
    allowed = pair_allowed(group_labels, own_labels)
    magnitude, weights, probs = recompute(scores, allowed, log_total, signed)
    dprobs = jnp.einsum(
        "bqhd,bkhd->bhqk",
        split_heads(grad_rows),
        split_heads(value_rows),
        preferred_element_type=jnp.float32,
    )
    delta = sum_delta(jnp.sum(probs * dprobs, axis=3))
    dscores = score_gradient(scores, magnitude, weights, dprobs, delta, signed).astype(jnp.bfloat16)
    scale = score_scale(gathered.shape[2])
    grad_values = jnp.einsum(
        "bhqk,bqhd->bkhd",
        probs.astype(jnp.bfloat16),
        split_heads(grad_rows),
        preferred_element_type=jnp.float32,
    )
    grad_keys = (
        jnp.einsum(
            "bhqk,bqhd->bkhd", dscores, split_heads(gathered), preferred_element_type=jnp.float32
        )
        * scale
    )
    query_terms = (
        jnp.einsum(
            "bhqk,bkhd->bqhd", dscores, split_heads(key_rows), preferred_element_type=jnp.float32
        )
        * scale
    )
    grad_queries = sum_queries(merge_heads(query_terms))
    return (grad_queries, merge_heads(grad_keys), merge_heads(grad_values))


def layer_forward(current, params, own_labels, group_labels, signed):
    (
        norm_gain,
        norm_bias,
        w_query,
        w_key,
        w_value,
        w_out,
        mlp_gain,
        mlp_bias,
        w_up,
        up_bias,
        w_down,
        down_bias,
    ) = params
    tall, width = current.shape
    grouped = (BATCH, tall // BATCH, width)
    normed = layer_norm(
        current, norm_gain.astype(jnp.float32), norm_bias.astype(jnp.float32)
    ).astype(jnp.bfloat16)
    queries = jnp.dot(normed, w_query, preferred_element_type=jnp.float32).astype(jnp.bfloat16)
    key_rows = jnp.dot(normed, w_key, preferred_element_type=jnp.float32).astype(jnp.bfloat16)
    value_rows = jnp.dot(normed, w_value, preferred_element_type=jnp.float32).astype(jnp.bfloat16)
    attended, log_total = attend_by_queries(
        queries.reshape(grouped),
        key_rows.reshape(grouped),
        value_rows.reshape(grouped),
        own_labels,
        group_labels,
        signed,
    )
    kept = (log_total,)
    attended = attended.reshape(tall, width)
    middle = current + jnp.dot(attended, w_out, preferred_element_type=jnp.float32)
    normed_mlp = layer_norm(
        middle, mlp_gain.astype(jnp.float32), mlp_bias.astype(jnp.float32)
    ).astype(jnp.bfloat16)
    hidden = jnp.dot(normed_mlp, w_up, preferred_element_type=jnp.float32) + up_bias.astype(
        jnp.float32
    )
    active = exact_gelu(hidden).astype(jnp.bfloat16)
    result = middle + (
        jnp.dot(active, w_down, preferred_element_type=jnp.float32) + down_bias.astype(jnp.float32)
    )
    saved = (
        current,
        normed,
        queries,
        key_rows,
        value_rows,
        attended,
        kept,
        middle,
        normed_mlp,
        hidden,
        active,
    )
    return (result, saved)


def layer_backward(upstream, params, saved, own_labels, group_labels, signed):
    (
        norm_gain,
        norm_bias,
        w_query,
        w_key,
        w_value,
        w_out,
        mlp_gain,
        mlp_bias,
        w_up,
        up_bias,
        w_down,
        down_bias,
    ) = params
    (
        current,
        normed,
        queries,
        key_rows,
        value_rows,
        attended,
        kept,
        middle,
        normed_mlp,
        hidden,
        active,
    ) = saved
    tall, width = current.shape
    grouped = (BATCH, tall // BATCH, width)
    grad_rows = upstream.astype(jnp.bfloat16)
    grad_down_bias = jnp.sum(grad_rows.astype(jnp.float32), axis=0)
    grad_down = contract_rows(active, grad_rows)
    grad_active = jnp.dot(grad_rows, w_down.T, preferred_element_type=jnp.float32)
    grad_hidden = jax.vjp(exact_gelu, hidden)[1](grad_active)[0].astype(jnp.bfloat16)
    grad_up_bias = jnp.sum(grad_hidden.astype(jnp.float32), axis=0)
    grad_up = contract_rows(normed_mlp, grad_hidden)
    grad_normed_mlp = jnp.dot(grad_hidden, w_up.T, preferred_element_type=jnp.float32)
    grad_middle_norm, grad_mlp_gain, grad_mlp_bias = norm_backward(
        middle, mlp_gain.astype(jnp.float32), mlp_bias.astype(jnp.float32), grad_normed_mlp
    )
    grad_middle = upstream + grad_middle_norm
    grad_branch = grad_middle.astype(jnp.bfloat16)
    grad_out = contract_rows(attended, grad_branch)
    grad_attended = jnp.dot(grad_branch, w_out.T, preferred_element_type=jnp.float32).astype(
        jnp.bfloat16
    )
    gathered, grad_gathered = (
        lax.all_gather(queries.reshape(grouped), "ka", axis=1, tiled=True),
        lax.all_gather(grad_attended.reshape(grouped), "ka", axis=1, tiled=True),
    )

    def delta_total(partial_value):
        return lax.psum(partial_value.astype(jnp.bfloat16), "ka").astype(jnp.float32)

    def query_total(terms):
        return lax.psum_scatter(
            terms.astype(jnp.bfloat16), "ka", scatter_dimension=1, tiled=True
        ).astype(jnp.float32)

    grad_queries, grad_keys, grad_values = back_over_own_keys(
        gathered,
        grad_gathered,
        key_rows.reshape(grouped),
        value_rows.reshape(grouped),
        kept[0],
        own_labels,
        group_labels,
        signed,
        delta_total,
        query_total,
    )
    grad_queries = grad_queries.reshape(tall, width).astype(jnp.bfloat16)
    grad_keys = grad_keys.reshape(tall, width).astype(jnp.bfloat16)
    grad_values = grad_values.reshape(tall, width).astype(jnp.bfloat16)
    grad_query = contract_rows(normed, grad_queries)
    grad_key = contract_rows(normed, grad_keys)
    grad_value = contract_rows(normed, grad_values)
    grad_normed = jnp.dot(grad_queries, w_query.T, preferred_element_type=jnp.float32)
    grad_normed = grad_normed + jnp.dot(grad_keys, w_key.T, preferred_element_type=jnp.float32)
    grad_normed = grad_normed + jnp.dot(grad_values, w_value.T, preferred_element_type=jnp.float32)
    grad_current_norm, grad_norm_gain, grad_norm_bias = norm_backward(
        current, norm_gain.astype(jnp.float32), norm_bias.astype(jnp.float32), grad_normed
    )
    gradients = (
        grad_norm_gain,
        grad_norm_bias,
        grad_query,
        grad_key,
        grad_value,
        grad_out,
        grad_mlp_gain,
        grad_mlp_bias,
        grad_up,
        grad_up_bias,
        grad_down,
        grad_down_bias,
    )
    return (grad_middle + grad_current_norm, gradients)


def tile_blocks(gradient):
    height, breadth = gradient.shape
    along_pb = lax.axis_size("pb")
    along_ka = lax.axis_size("ka")
    tiled = gradient.reshape(along_pb, height // along_pb, along_ka, breadth // along_ka)
    return jnp.transpose(tiled, (0, 2, 1, 3)).reshape(
        along_pb * along_ka, height // along_pb, breadth // along_ka
    )


def per_device(
    tokens,
    sequence_ids,
    sequence_offsets,
    signed_norm_gain,
    signed_norm_bias,
    signed_query,
    signed_key,
    signed_value,
    signed_out,
    signed_mlp_gain,
    signed_mlp_bias,
    signed_up,
    signed_up_bias,
    signed_down,
    signed_down_bias,
    plain_norm_gain,
    plain_norm_bias,
    plain_query,
    plain_key,
    plain_value,
    plain_out,
    plain_mlp_gain,
    plain_mlp_bias,
    plain_up,
    plain_up_bias,
    plain_down,
    plain_down_bias,
    cotangent,
):
    own_labels = jnp.stack([sequence_ids, sequence_offsets]).reshape(
        2, BATCH, sequence_ids.shape[0] // BATCH
    )
    group_labels = lax.all_gather(own_labels, "ka", axis=2, tiled=True)
    signed_params = (
        signed_norm_gain,
        signed_norm_bias,
        signed_query,
        signed_key,
        signed_value,
        signed_out,
        signed_mlp_gain,
        signed_mlp_bias,
        signed_up,
        signed_up_bias,
        signed_down,
        signed_down_bias,
    )
    plain_params = (
        plain_norm_gain,
        plain_norm_bias,
        plain_query,
        plain_key,
        plain_value,
        plain_out,
        plain_mlp_gain,
        plain_mlp_bias,
        plain_up,
        plain_up_bias,
        plain_down,
        plain_down_bias,
    )
    between, signed_saved = layer_forward(
        tokens.astype(jnp.float32), signed_params, own_labels, group_labels, True
    )
    final_state, plain_saved = layer_forward(between, plain_params, own_labels, group_labels, False)
    upstream, plain_grads = layer_backward(
        cotangent.astype(jnp.float32), plain_params, plain_saved, own_labels, group_labels, False
    )
    input_gradient, signed_grads = layer_backward(
        upstream, signed_params, signed_saved, own_labels, group_labels, True
    )
    everything = signed_grads + plain_grads
    matrix_places = (2, 3, 4, 5, 8, 10, 14, 15, 16, 17, 20, 22)
    vector_places = (0, 1, 6, 7, 9, 11, 12, 13, 18, 19, 21, 23)
    blocks = [tile_blocks(everything[position]) for position in matrix_places]
    summed_blocks = (
        lax.psum_scatter(blocks[0], ("pb", "ka"), scatter_dimension=0, tiled=True),
        lax.psum_scatter(blocks[1], ("pb", "ka"), scatter_dimension=0, tiled=True),
        lax.psum_scatter(blocks[2], ("pb", "ka"), scatter_dimension=0, tiled=True),
        lax.psum_scatter(blocks[3], ("pb", "ka"), scatter_dimension=0, tiled=True),
        lax.psum_scatter(blocks[4], ("pb", "ka"), scatter_dimension=0, tiled=True),
        lax.psum_scatter(blocks[5], ("pb", "ka"), scatter_dimension=0, tiled=True),
        lax.psum_scatter(blocks[6], ("pb", "ka"), scatter_dimension=0, tiled=True),
        lax.psum_scatter(blocks[7], ("pb", "ka"), scatter_dimension=0, tiled=True),
        lax.psum_scatter(blocks[8], ("pb", "ka"), scatter_dimension=0, tiled=True),
        lax.psum_scatter(blocks[9], ("pb", "ka"), scatter_dimension=0, tiled=True),
        lax.psum_scatter(blocks[10], ("pb", "ka"), scatter_dimension=0, tiled=True),
        lax.psum_scatter(blocks[11], ("pb", "ka"), scatter_dimension=0, tiled=True),
    )
    summed_vectors = lax.psum(
        (
            everything[0],
            everything[1],
            everything[6],
            everything[7],
            everything[9],
            everything[11],
            everything[12],
            everything[13],
            everything[18],
            everything[19],
            everything[21],
            everything[23],
        ),
        ("pb", "ka"),
    )
    finished = [None] * 24
    for slot_index, position in enumerate(matrix_places):
        finished[position] = summed_blocks[slot_index][0]
    for slot_index, position in enumerate(vector_places):
        finished[position] = summed_vectors[slot_index]
    return tuple([final_state.astype(jnp.bfloat16), input_gradient] + finished)


def solution(mesh):
    placed = (
        P(("pb", "ka"), None),
        P(("pb", "ka")),
        P(("pb", "ka")),
        P(),
        P(),
        P(),
        P(),
        P(),
        P(),
        P(),
        P(),
        P(),
        P(),
        P(),
        P(),
        P(),
        P(),
        P(),
        P(),
        P(),
        P(),
        P(),
        P(),
        P(),
        P(),
        P(),
        P(),
        P(("pb", "ka"), None),
    )
    return jax.shard_map(
        per_device,
        mesh=mesh,
        in_specs=placed,
        out_specs=(
            P(("pb", "ka"), None),
            P(("pb", "ka"), None),
            P(),
            P(),
            P("pb", "ka"),
            P("pb", "ka"),
            P("pb", "ka"),
            P("pb", "ka"),
            P(),
            P(),
            P("pb", "ka"),
            P(),
            P("pb", "ka"),
            P(),
            P(),
            P(),
            P("pb", "ka"),
            P("pb", "ka"),
            P("pb", "ka"),
            P("pb", "ka"),
            P(),
            P(),
            P("pb", "ka"),
            P(),
            P("pb", "ka"),
            P(),
        ),
        check_vma=False,
    )
```

profile of v0, /device:TPU:0, one launch (start us, length us, event | category | flops | bytes accessed | tf_op | source)
XLA Modules:
  0.0 3511.9 jit_solution(12238320196151789890)
XLA Ops:
  43.9 89.8 %all-gather.5.cloned.1.call-done = bf16[2,2048,768]{2,1,0:T(8,128)(2,1)} async-done(((bf16[2,512,768]{2,1,0:T(8,128)(2,1)}), bf16[2,2048,768]{2,1,0:T(8,128)(2,1)}) %all-gather.5.cloned.1.call-update) | async-done | bytes 6291472 | tf_op jit(solution)/shard_map/all_gather | solution.py:93
  142.4 65.4 %fusion.6 = (bf16[2,12,2048]{2,1,0:T(8,128)(2,1)}, f32[2,12,2048,512]{2,3,1,0:T(8,128)}) fusion(pred[2,2048,512]{1,2,0:T(8,128)(4,1)S(1)} %compare_and_fusion, bf16[2,2048,12,64]{1,3,2,0:T(8,128)(2,1)} %bitcast.278, bf16[2,512,12,64]{1,0,3,2:T(2,128)(2,1)} %reshape_reshape.9), kind=kOutput, calls=%fused_computation.19 | convolution fusion | flops 3347005440 | bytes 110723072 | tf_op jit(solution)/shard_map/bqhd,bkhd->bhqk/dot_general | solution.py:48
  241.6 57.5 %fusion.4 = bf16[2,12,2048]{2,1,0:T(8,128)(2,1)} fusion(f32[2,12,2048,512]{2,3,1,0:T(8,128)} %get-tuple-element.144, f32[2,12,2048]{2,1,0:T(8,128)S(1)} %convert_element_type.261, pred[2,2048,512]{1,2,0:T(8,128)(4,1)S(1)} %compare_and_fusion), kind=kLoop, calls=%fused_computation.17 | loop fusion | flops 176111616 | bytes 103055360 | tf_op jit(solution)/shard_map/reduce_sum | solution.py:100
  334.3 82.5 %fusion.31 = bf16[2,12,64,2048]{3,2,1,0:T(8,128)(2,1)} fusion(f32[2,12,2048,512]{2,3,1,0:T(8,128)} %get-tuple-element.144, f32[2,12,2048]{2,1,0:T(8,128)S(1)} %convert_element_type.263, f32[2,12,2048]{2,1,0:T(8,128)S(1)} %convert_element_type.261, pred[2,2048,512]{1,2,0:T(8,128)(4,1)S(1)} %compare_and_fusion, bf16[2,512,12,64]{1,0,3,2:T(2,128)(2,1)} %reshape_reshape.8), kind=kOutput, calls=%fused_computation.78 | convolution fusion | flops 3476029440 | bytes 111017984 | tf_op jit(solution)/shard_map/bhqk,bkhd->bqhd/dot_general | solution.py:102
  426.3 109.8 %reduce-scatter.17.cloned.1.call-done = bf16[2,512,768]{2,1,0:T(8,128)(2,1)} async-done(((bf16[2,2048,768]{2,1,0:T(8,128)(2,1)}), bf16[2,512,768]{2,1,0:T(8,128)(2,1)}) %reduce-scatter.17.cloned.1.call-update) | async-done | bytes 1572880 | tf_op jit(solution)/shard_map/reduce_scatter | solution.py:105
  596.4 108.0 %all-gather.7.cloned.1.call-done = bf16[2,2048,768]{2,1,0:T(8,128)(2,1)} async-done(((bf16[2,512,768]{2,1,0:T(8,128)(2,1)}), bf16[2,2048,768]{2,1,0:T(8,128)(2,1)}) %all-gather.7.cloned.1.call-update) | async-done | bytes 6291472 | tf_op jit(solution)/shard_map/all_gather | solution.py:93
  905.9 107.9 %reduce-scatter.19.cloned.1.call-done = bf16[2,512,768]{2,1,0:T(8,128)(2,1)} async-done(((bf16[2,2048,768]{2,1,0:T(8,128)(2,1)}), bf16[2,512,768]{2,1,0:T(8,128)(2,1)}) %reduce-scatter.19.cloned.1.call-update) | async-done | bytes 1572880 | tf_op jit(solution)/shard_map/reduce_scatter | solution.py:105
  1089.5 115.9 %all-gather.9.cloned.1.call-done = bf16[2,2048,768]{2,1,0:T(8,128)(2,1)} async-done(((bf16[2,512,768]{2,1,0:T(8,128)(2,1)}), bf16[2,2048,768]{2,1,0:T(8,128)(2,1)}) %all-gather.9.cloned.1.call-update) | async-done | bytes 6291472 | tf_op jit(solution)/shard_map/all_gather | solution.py:266
  1214.5 71.6 %multiply_reduce_fusion.1 = (bf16[2,12,2048]{2,1,0:T(8,128)(2,1)}, f32[2,12,2048,512]{2,3,1,0:T(8,128)}) fusion(f32[2,12,2048]{2,1,0:T(8,128)S(1)} %log_add_fusion.1, f32[2,12,2048,512]{2,3,1,0:T(8,128)} %get-tuple-element.151, pred[2,2048,512]{1,2,0:T(8,128)(4,1)S(1)} %copy-done.8, bf16[2,2048,12,64]{1,3,2,0:T(8,128)(2,1)} %bitcast.288, ...), kind=kOutput, calls=%fused_computation.7 | convolution fusion | flops 3372171264 | bytes 211582976 | tf_op jit(solution)/shard_map/bqhd,bkhd->bhqk/dot_general | solution.py:126
  1320.6 79.1 %multiply_convert_fusion = bf16[2,12,2048,512]{2,3,1,0:T(8,128)(2,1)} fusion(f32[2,12,2048,512]{2,3,1,0:T(8,128)} %get-tuple-element.157, f32[2,12,2048]{2,1,0:T(8,128)} %convert_element_type.300, f32[2,12,2048]{2,1,0:T(8,128)S(1)} %log_add_fusion.1, f32[2,12,2048,512]{2,3,1,0:T(8,128)} %get-tuple-element.151, pred[2,2048,512]{1,2,0:T(8,128)(4,1)S(1)} %copy-done.8), kind=kLoop, calls=%fused_computation.6 | loop fusion | flops 176160768 | bytes 254148608 | tf_op jit(solution)/shard_map/convert_element_type | solution.py:133
  1590.4 114.9 %all-gather.11.cloned.1.call-done = bf16[2,2048,768]{2,1,0:T(8,128)(2,1)} async-done(((bf16[2,512,768]{2,1,0:T(8,128)(2,1)}), bf16[2,2048,768]{2,1,0:T(8,128)(2,1)}) %all-gather.11.cloned.1.call-update) | async-done | bytes 6291472 | tf_op jit(solution)/shard_map/all_gather | solution.py:266
  1714.3 89.6 %multiply_reduce_fusion = (bf16[2,12,2048]{2,1,0:T(8,128)(2,1)}, f32[2,12,2048,512]{2,3,1,0:T(8,128)}) fusion(f32[2,12,2048]{2,1,0:T(8,128)S(1)} %log_add_fusion, f32[2,12,2048,512]{2,3,1,0:T(8,128)} %get-tuple-element.144, pred[2,2048,512]{1,2,0:T(8,128)(4,1)S(1)} %copy-done.8, bf16[2,2048,12,64]{1,3,2,0:T(8,128)(2,1)} %bitcast.286, ...), kind=kOutput, calls=%fused_computation.3 | convolution fusion | flops 3472834560 | bytes 211582976 | tf_op jit(solution)/shard_map/bqhd,bkhd->bhqk/dot_general | solution.py:126
  1838.3 107.4 %fusion.3 = bf16[2,12,2048,512]{2,3,1,0:T(8,128)(2,1)} fusion(f32[2,12,2048,512]{2,3,1,0:T(8,128)} %get-tuple-element.161, f32[2,12,2048,512]{2,3,1,0:T(8,128)} %get-tuple-element.144, f32[2,12,2048]{2,1,0:T(8,128)} %convert_element_type.318, f32[2,12,2048]{2,1,0:T(8,128)S(1)} %log_add_fusion, pred[2,2048,512]{1,2,0:T(8,128)(4,1)S(1)} %copy-done.8), kind=kLoop, calls=%fused_computation.16 | loop fusion | flops 427819008 | bytes 254148608 | tf_op jit(solution)/shard_map/convert_element_type | solution.py:133
  2120.2 83.5 %fusion.48 = bf16[2,512,12,64]{1,3,2,0:T(8,128)(2,1)S(1)} fusion(bf16[2,2048,12,64]{1,3,2,0:T(8,128)(2,1)} %bitcast.287, f32[2,12,2048,512]{2,3,1,0:T(8,128)} %get-tuple-element.144, f32[2,12,2048]{2,1,0:T(8,128)S(1)} %log_add_fusion, pred[2,2048,512]{1,2,0:T(8,128)(4,1)S(1)} %copy-done.8), kind=kOutput, calls=%fused_computation.124 | convolution fusion | flops 3448504320 | bytes 110821376 | tf_op jit(solution)/shard_map/bhqk,bqhd->bkhd/dot_general | solution.py:135
  2334.9 141.9 %reduce-scatter.45.cloned.1.call-done = f32[1,96,768]{2,1,0:T(8,128)} async-done(((f32[32,96,768]{2,1,0:T(8,128)}), f32[1,96,768]{2,1,0:T(8,128)}) %reduce-scatter.45.cloned.1.call-update) | async-done | bytes 294928 | tf_op jit(solution)/shard_map/reduce_scatter | solution.py:415
  2476.9 106.4 %reduce-scatter.41.cloned.1.call-done = f32[1,96,192]{2,1,0:T(8,128)} async-done(((f32[32,96,192]{2,1,0:T(8,128)}), f32[1,96,192]{2,1,0:T(8,128)}) %reduce-scatter.41.cloned.1.call-update) | async-done | bytes 73744 | tf_op jit(solution)/shard_map/reduce_scatter | solution.py:413
  2583.3 106.5 %reduce-scatter.39.cloned.1.call-done = f32[1,96,192]{2,1,0:T(8,128)} async-done(((f32[32,96,192]{2,1,0:T(8,128)}), f32[1,96,192]{2,1,0:T(8,128)}) %reduce-scatter.39.cloned.1.call-update) | async-done | bytes 73744 | tf_op jit(solution)/shard_map/reduce_scatter | solution.py:412
  2689.7 106.4 %reduce-scatter.37.cloned.1.call-done = f32[1,96,192]{2,1,0:T(8,128)} async-done(((f32[32,96,192]{2,1,0:T(8,128)}), f32[1,96,192]{2,1,0:T(8,128)}) %reduce-scatter.37.cloned.1.call-update) | async-done | bytes 73744 | tf_op jit(solution)/shard_map/reduce_scatter | solution.py:411
  2796.1 106.5 %reduce-scatter.31.cloned.1.call-done = f32[1,96,192]{2,1,0:T(8,128)} async-done(((f32[32,96,192]{2,1,0:T(8,128)}), f32[1,96,192]{2,1,0:T(8,128)}) %reduce-scatter.31.cloned.1.call-update) | async-done | bytes 73744 | tf_op jit(solution)/shard_map/reduce_scatter | solution.py:408
  2902.6 141.1 %reduce-scatter.35.cloned.1.call-done = f32[1,384,192]{1,2,0:T(8,128)} async-done(((f32[32,384,192]{1,2,0:T(8,128)}), f32[1,384,192]{1,2,0:T(8,128)}) %reduce-scatter.35.cloned.1.call-update) | async-done | bytes 294928 | tf_op jit(solution)/shard_map/reduce_scatter | solution.py:410
  3043.7 142.1 %reduce-scatter.33.cloned.1.call-done = f32[1,96,768]{2,1,0:T(8,128)} async-done(((f32[32,96,768]{2,1,0:T(8,128)}), f32[1,96,768]{2,1,0:T(8,128)}) %reduce-scatter.33.cloned.1.call-update) | async-done | bytes 294928 | tf_op jit(solution)/shard_map/reduce_scatter | solution.py:409
  3185.9 106.4 %reduce-scatter.29.cloned.1.call-done = f32[1,96,192]{2,1,0:T(8,128)} async-done(((f32[32,96,192]{2,1,0:T(8,128)}), f32[1,96,192]{2,1,0:T(8,128)}) %reduce-scatter.29.cloned.1.call-update) | async-done | bytes 73744 | tf_op jit(solution)/shard_map/reduce_scatter | solution.py:407
  3292.2 106.5 %reduce-scatter.27.cloned.1.call-done = f32[1,96,192]{2,1,0:T(8,128)} async-done(((f32[32,96,192]{2,1,0:T(8,128)}), f32[1,96,192]{2,1,0:T(8,128)}) %reduce-scatter.27.cloned.1.call-update) | async-done | bytes 73744 | tf_op jit(solution)/shard_map/reduce_scatter | solution.py:406
  3398.8 106.4 %reduce-scatter.25.cloned.1.call-done = f32[1,96,192]{2,1,0:T(8,128)} async-done(((f32[32,96,192]{2,1,0:T(8,128)}), f32[1,96,192]{2,1,0:T(8,128)}) %reduce-scatter.25.cloned.1.call-update) | async-done | bytes 73744 | tf_op jit(solution)/shard_map/reduce_scatter | solution.py:405
  (431 shorter events, 1043.1 us)
Async XLA Ops:
  7.2 126.5 %all-gather.5.cloned.1.call-start = ((), (), s32[]{:S(2)}) async-start(), calls=%async_computation.16 | async-start | bytes 7864320 | tf_op jit(solution)/shard_map/all_gather | solution.py:93
  15.1 225.6 %all-reduce.8.cloned.1.call-start = ((), (), s32[]{:S(2)}) async-start(), calls=%async_computation.17 | async-start | bytes 262144 | tf_op jit(solution)/shard_map/pmax | solution.py:98
  299.1 236.9 %reduce-scatter.17.cloned.1.call-start = ((), (), s32[]{:S(2)}) async-start(), calls=%async_computation.19 | async-start | bytes 7864320 | tf_op jit(solution)/shard_map/reduce_scatter | solution.py:105
  425.5 279.0 %all-gather.7.cloned.1.call-start = ((), (), s32[]{:S(2)}) async-start(), calls=%async_computation.20 | async-start | bytes 7864320 | tf_op jit(solution)/shard_map/all_gather | solution.py:93
  588.5 195.4 %all-reduce.12.cloned.1.call-start = ((), (), s32[]{:S(2)}) async-start(), calls=%async_computation.21 | async-start | bytes 262144 | tf_op jit(solution)/shard_map/pmax | solution.py:98
  816.9 196.9 %reduce-scatter.19.cloned.1.call-start = ((), (), s32[]{:S(2)}) async-start(), calls=%async_computation.23 | async-start | bytes 7864320 | tf_op jit(solution)/shard_map/reduce_scatter | solution.py:105
  903.3 302.1 %all-gather.9.cloned.1.call-start = ((), (), s32[]{:S(2)}) async-start(), calls=%async_computation.24 | async-start | bytes 7864320 | tf_op jit(solution)/shard_map/all_gather | solution.py:266
  1089.4 229.6 %all-reduce.16.cloned.1.call-start = ((), (), s32[]{:S(2)}) async-start(), calls=%async_computation.25 | async-start | bytes 262144 | tf_op jit(solution)/shard_map/psum | solution.py:270
  1286.2 253.9 %reduce-scatter.21.cloned.1.call-start = ((), (), s32[]{:S(2)}) async-start(), calls=%async_computation.26 | async-start | bytes 7864320 | tf_op jit(solution)/shard_map/reduce_scatter | solution.py:273
  1429.5 275.9 %all-gather.11.cloned.1.call-start = ((), (), s32[]{:S(2)}) async-start(), calls=%async_computation.27 | async-start | bytes 7864320 | tf_op jit(solution)/shard_map/all_gather | solution.py:266
  1589.4 247.3 %all-reduce.18.cloned.1.call-start = ((), (), s32[]{:S(2)}) async-start(), calls=%async_computation.28 | async-start | bytes 262144 | tf_op jit(solution)/shard_map/psum | solution.py:270
  1803.9 438.6 %reduce-scatter.23.cloned.1.call-start = ((), (), s32[]{:S(2)}) async-start(), calls=%async_computation.29 | async-start | bytes 7864320 | tf_op jit(solution)/shard_map/reduce_scatter | solution.py:273
  1975.5 347.6 %reduce-scatter.43.cloned.1.call-start = ((), (), s32[]{:S(2)}) async-start(), calls=%async_computation.39 | async-start | bytes 3244032 | tf_op jit(solution)/shard_map/reduce_scatter | solution.py:414
  1983.5 351.5 %reduce-scatter.47.cloned.1.call-start = ((), (), s32[]{:S(2)}) async-start(), calls=%async_computation.41 | async-start | bytes 9732096 | tf_op jit(solution)/shard_map/reduce_scatter | solution.py:416
  2005.1 471.7 %reduce-scatter.45.cloned.1.call-start = ((), (), s32[]{:S(2)}) async-start(), calls=%async_computation.40 | async-start | bytes 9732096 | tf_op jit(solution)/shard_map/reduce_scatter | solution.py:415
  2037.8 545.4 %reduce-scatter.41.cloned.1.call-start = ((), (), s32[]{:S(2)}) async-start(), calls=%async_computation.38 | async-start | bytes 3244032 | tf_op jit(solution)/shard_map/reduce_scatter | solution.py:413
  2043.5 646.2 %reduce-scatter.39.cloned.1.call-start = ((), (), s32[]{:S(2)}) async-start(), calls=%async_computation.37 | async-start | bytes 3244032 | tf_op jit(solution)/shard_map/reduce_scatter | solution.py:412
  2048.9 747.2 %reduce-scatter.37.cloned.1.call-start = ((), (), s32[]{:S(2)}) async-start(), calls=%async_computation.36 | async-start | bytes 3244032 | tf_op jit(solution)/shard_map/reduce_scatter | solution.py:411
  2057.0 845.6 %reduce-scatter.31.cloned.1.call-start = ((), (), s32[]{:S(2)}) async-start(), calls=%async_computation.33 | async-start | bytes 3244032 | tf_op jit(solution)/shard_map/reduce_scatter | solution.py:408
  2065.2 978.5 %reduce-scatter.35.cloned.1.call-start = ((), (), s32[]{:S(2)}) async-start(), calls=%async_computation.35 | async-start | bytes 9732096 | tf_op jit(solution)/shard_map/reduce_scatter | solution.py:410
  2086.9 1099.0 %reduce-scatter.33.cloned.1.call-start = ((), (), s32[]{:S(2)}) async-start(), calls=%async_computation.34 | async-start | bytes 9732096 | tf_op jit(solution)/shard_map/reduce_scatter | solution.py:409
  2119.7 1172.5 %reduce-scatter.29.cloned.1.call-start = ((), (), s32[]{:S(2)}) async-start(), calls=%async_computation.32 | async-start | bytes 3244032 | tf_op jit(solution)/shard_map/reduce_scatter | solution.py:407
  2209.2 1189.6 %reduce-scatter.27.cloned.1.call-start = ((), (), s32[]{:S(2)}) async-start(), calls=%async_computation.31 | async-start | bytes 3244032 | tf_op jit(solution)/shard_map/reduce_scatter | solution.py:406
  2241.8 1263.4 %reduce-scatter.25.cloned.1.call-start = ((), (), s32[]{:S(2)}) async-start(), calls=%async_computation.30 | async-start | bytes 3244032 | tf_op jit(solution)/shard_map/reduce_scatter | solution.py:405
  (113 other events, 3354.6 us)
Sparse Core Ops, SparseCore 0:
  15.2 118.4 all-gather.4
  208.0 32.7 all-reduce.7
  299.2 34.1 all-reduce.9
  425.6 110.3 reduce-scatter.16
  588.6 115.8 all-gather.6
  817.0 34.1 all-reduce.13
  903.4 110.3 reduce-scatter.18
  1089.5 115.8 all-gather.8
  1286.3 32.6 all-reduce.15
  1429.6 110.3 reduce-scatter.20
  1589.5 115.8 all-gather.10
  1975.6 110.3 reduce-scatter.22
  2091.8 102.0 reduce-scatter.42
  2200.2 134.6 reduce-scatter.46
  2342.3 134.5 reduce-scatter.44
  2482.7 100.4 reduce-scatter.40
  2589.3 100.4 reduce-scatter.38
  2695.6 100.4 reduce-scatter.36
  2802.1 100.4 reduce-scatter.30
  2909.1 134.5 reduce-scatter.34
  3051.2 134.6 reduce-scatter.32
  3191.7 100.4 reduce-scatter.28
  3298.2 100.4 reduce-scatter.26
  3404.6 100.4 reduce-scatter.24
  (2 shorter events, 65.1 us)
where the time goes:
time: 3520 us; the launch traced here: 3510 us
  waiting for transfers between devices  2040 us (58%)
  matrix products  885 us (25%)
  other arithmetic  304 us (9%)
  local copies, waits for them, and re-layouts  203 us (6%)
  blocking collectives  61.4 us (2%)
    all_gather x2, waiting for transfers between devices, layer_backward(): lax.all_gather(grad_attended.reshape(grouped), 'ka', axis=1, tiled=True)  231 us
    reduce_scatter x2, waiting for transfers between devices, attend_by_queries(): lax.psum_scatter(merge_heads(term_parts).astype(jnp.bfloat16), 'ka', scat...  218 us
    all_gather x2, waiting for transfers between devices, attend_by_queries(): gathered = lax.all_gather(queries, 'ka', axis=1, tiled=True)  198 us
    convert_element_type x2, other arithmetic, back_over_own_keys(): score_gradient(scores, magnitude, weights, dprobs, delta, signed)  187 us
    dot_general x2, matrix products, back_over_own_keys(): jnp.einsum('bqhd,bkhd->bhqk', split_heads(grad_rows), split_heads(value_r...  161 us
    reduce_scatter x1, waiting for transfers between devices, per_device(): lax.psum_scatter(blocks[4], ('pb', 'ka'), scatter_dimension=0, tiled=True)  142 us
    reduce_scatter x1, waiting for transfers between devices, per_device(): lax.psum_scatter(blocks[10], ('pb', 'ka'), scatter_dimension=0, tiled=True)  142 us
    reduce_scatter x1, waiting for transfers between devices, per_device(): lax.psum_scatter(blocks[5], ('pb', 'ka'), scatter_dimension=0, tiled=True)  141 us
  transfers between devices with their start and end apart: 26, of which 24 were waited for; matrix products, arithmetic and copies ran while one was open for 12% of the time, Pallas kernels for 0%

commit v1 on v0

v1 whole, which is shorter than its diff:
```python
import functools

import jax
import jax.numpy as jnp
from jax import lax
from jax.experimental import pallas as pl
from jax.experimental.pallas import tpu as pltpu
from jax.sharding import PartitionSpec as P

HEADS = 12
BATCH = 2
HALVES = 2
OWN = BATCH * HALVES
EPSILON = 1e-05
FLOOR = -1e30
BF = jnp.bfloat16
F32 = jnp.float32
MIB = 1 << 20

NT = (((1,), (1,)), ((), ()))
NN = (((1,), (0,)), ((), ()))
TN = (((0,), (0,)), ((), ()))


def dot(left, right, dims=NN):
    return lax.dot_general(left, right, dims, preferred_element_type=F32)


def dense(left, right, left_axis, right_axis):
    return lax.dot_general(
        left, right, (((left_axis,), (right_axis,)), ((), ())), preferred_element_type=F32
    )


def attention_sizes(width):
    head = width // HEADS
    lanes = 256
    while width % lanes or lanes % head:
        lanes //= 2
    return head, lanes, width // lanes, lanes // head


def head_parts(block, head, count):
    lane = lax.broadcasted_iota(jnp.int32, block.shape, 1) // head
    return [jnp.where(lane == h, block, jnp.zeros_like(block)) for h in range(count)]


def turned(block):
    return jnp.transpose(block.astype(F32))


def causal(shape):
    key = lax.broadcasted_iota(jnp.int32, shape, 0)
    query = lax.broadcasted_iota(jnp.int32, shape, 1)
    return key <= query


def forward_kernel(head, count, signed, bounds, q_ref, k_ref, v_ref, o_ref, lse_ref, qm, vt, acc):
    step = pl.program_id(1)

    @pl.when(step == 0)
    def _():
        for j in range(k_ref.shape[0]):
            vt[j] = turned(v_ref[j]).astype(BF)

    for h, part in enumerate(head_parts(q_ref[0], head, count)):
        qm[h] = part
    acc[...] = jnp.zeros_like(acc)
    rows = q_ref.shape[1]
    start, last = bounds[0, step], bounds[1, step]

    def block(j, carry, masked):
        keys = k_ref[j]
        result = []
        for h in range(count):
            top, total = carry[2 * h], carry[2 * h + 1]
            s = dot(keys, qm[h], NT)
            if signed:
                square = s * s + 1.0
                inverse = lax.rsqrt(square)
                c = square * inverse
            else:
                c = s
            if masked:
                c = jnp.where(causal(c.shape), c, FLOOR)
            higher = jnp.maximum(top, jnp.max(c, axis=0, keepdims=True))
            raised = jnp.exp(c - higher)
            fade = jnp.exp(top - higher)
            total = total * fade + jnp.sum(raised, axis=0, keepdims=True)
            if signed:
                raised = raised * (s * inverse)
            part = dot(vt[j, h * head : (h + 1) * head, :], raised.astype(BF))
            acc[h] = acc[h] * fade + part
            result += [higher, total]
        return tuple(result)

    first = (jnp.full((1, rows), FLOOR, F32), jnp.zeros((1, rows), F32)) * count
    carry = lax.fori_loop(start, last, lambda j, c: block(j, c, False), first)
    carry = block(last, carry, True)
    for h in range(count):
        top, total = carry[2 * h], carry[2 * h + 1]
        acc[h] = acc[h] / total
        lse_ref[0, h : h + 1, :] = top + jnp.log(total)
    o_ref[0] = jnp.transpose(acc[...].reshape(count * head, rows)).astype(BF)


def attend_forward(queries, keys, values, bounds, signed):
    pieces, rows, width = queries.shape
    whole = keys.shape[0]
    head, lanes, groups, count = attention_sizes(width)
    return pl.pallas_call(
        functools.partial(forward_kernel, head, count, signed),
        out_shape=(
            jax.ShapeDtypeStruct(queries.shape, BF),
            jax.ShapeDtypeStruct((pieces * groups, count, rows), F32),
        ),
        grid_spec=pltpu.PrefetchScalarGridSpec(
            num_scalar_prefetch=1,
            grid=(groups, pieces),
            in_specs=[
                pl.BlockSpec((1, rows, lanes), lambda g, i, b: (i, 0, g)),
                pl.BlockSpec((whole, rows, lanes), lambda g, i, b: (0, 0, g)),
                pl.BlockSpec((whole, rows, lanes), lambda g, i, b: (0, 0, g)),
            ],
            out_specs=[
                pl.BlockSpec((1, rows, lanes), lambda g, i, b: (i, 0, g)),
                pl.BlockSpec((1, count, rows), lambda g, i, b: (g * pieces + i, 0, 0)),
            ],
            scratch_shapes=[
                pltpu.VMEM((count, rows, lanes), BF),
                pltpu.VMEM((whole, lanes, rows), BF),
                pltpu.VMEM((count, head, rows), F32),
            ],
        ),
        compiler_params=pltpu.CompilerParams(vmem_limit_bytes=48 * MIB),
    )(bounds, queries, keys, values)


def backward_kernel(
    head, count, signed, bounds, q_ref, do_ref, o_ref, lse_ref, k_ref, v_ref,
    dq_ref, dk_ref, dv_ref, qm, dom, kt, dq, dk, dv, delta,
):
    step = pl.program_id(1)
    whole, rows, lanes = k_ref.shape

    @pl.when(step == 0)
    def _():
        for j in range(whole):
            kt[j] = turned(k_ref[j]).astype(BF)
            dk[j] = jnp.zeros((rows, lanes), F32)
            dv[j] = jnp.zeros((rows, lanes), F32)

    for h, part in enumerate(head_parts(q_ref[0], head, count)):
        qm[h] = part
    for h, part in enumerate(head_parts(do_ref[0], head, count)):
        dom[h] = part
    product = jnp.transpose(do_ref[0].astype(F32) * o_ref[0].astype(F32))
    for h in range(count):
        delta[h : h + 1, :] = jnp.sum(product[h * head : (h + 1) * head], axis=0, keepdims=True)
    dq[...] = jnp.zeros_like(dq)
    start, last = bounds[0, step], bounds[1, step]

    def block(j, masked):
        keys, values = k_ref[j], v_ref[j]
        dk_part = dv_part = None
        for h in range(count):
            s = dot(keys, qm[h], NT)
            dp = dot(values, dom[h], NT)
            if signed:
                square = s * s + 1.0
                inverse = lax.rsqrt(square)
                c = square * inverse
            else:
                c = s
            if masked:
                c = jnp.where(causal(c.shape), c, FLOOR)
            w = jnp.exp(c - lse_ref[0, h : h + 1, :])
            if signed:
                ratio = s * inverse
                p = w * ratio
                squared = inverse * inverse
                slope = 1.0 + squared * (inverse - 1.0)
                ds = w * (dp * slope - delta[h : h + 1, :] * ratio)
            else:
                p = w
                ds = w * (dp - delta[h : h + 1, :])
            p, ds = p.astype(BF), ds.astype(BF)
            dq[h] += dot(kt[j, h * head : (h + 1) * head, :], ds)
            dv_h, dk_h = dot(p, dom[h]), dot(ds, qm[h])
            dk_part = dk_h if dk_part is None else dk_part + dk_h
            dv_part = dv_h if dv_part is None else dv_part + dv_h
        dk[j] += dk_part
        dv[j] += dv_part

    @pl.loop(start, last)
    def _(j):
        block(j, False)

    block(last, True)
    turned_back = jnp.transpose(dq[...].reshape(count * head, rows)) * (head ** -0.5)
    dq_ref[0] = turned_back.astype(BF)

    @pl.when(step == pl.num_programs(1) - 1)
    def _():
        for j in range(whole):
            dk_ref[j] = dk[j].astype(BF)
            dv_ref[j] = dv[j].astype(BF)


def attend_backward(queries, grad_rows, attended, totals, keys, values, bounds, signed):
    pieces, rows, width = queries.shape
    whole = keys.shape[0]
    head, lanes, groups, count = attention_sizes(width)
    own = pl.BlockSpec((1, rows, lanes), lambda g, i, b: (i, 0, g))
    every = pl.BlockSpec((whole, rows, lanes), lambda g, i, b: (0, 0, g))
    return pl.pallas_call(
        functools.partial(backward_kernel, head, count, signed),
        out_shape=(
            jax.ShapeDtypeStruct(queries.shape, BF),
            jax.ShapeDtypeStruct(keys.shape, BF),
            jax.ShapeDtypeStruct(keys.shape, BF),
        ),
        grid_spec=pltpu.PrefetchScalarGridSpec(
            num_scalar_prefetch=1,
            grid=(groups, pieces),
            in_specs=[
                own,
                own,
                own,
                pl.BlockSpec((1, count, rows), lambda g, i, b: (g * pieces + i, 0, 0)),
                every,
                every,
            ],
            out_specs=[own, every, every],
            scratch_shapes=[
                pltpu.VMEM((count, rows, lanes), BF),
                pltpu.VMEM((count, rows, lanes), BF),
                pltpu.VMEM((whole, lanes, rows), BF),
                pltpu.VMEM((count, head, rows), F32),
                pltpu.VMEM((whole, rows, lanes), F32),
                pltpu.VMEM((whole, rows, lanes), F32),
                pltpu.VMEM((count, rows), F32),
            ],
        ),
        compiler_params=pltpu.CompilerParams(vmem_limit_bytes=56 * MIB),
    )(bounds, queries, grad_rows, attended, totals, keys, values)


def xor_send(array, axis, bit):
    size = lax.axis_size(axis)
    return lax.ppermute(array, axis, [(i, i ^ bit) for i in range(size)])


def shift_send(array, shift):
    size = lax.axis_size("ka")
    return lax.ppermute(array, "ka", [(i, (i + shift) % size) for i in range(size)])


def pick(array, index, axis=0):
    return lax.dynamic_index_in_dim(array, index, axis, keepdims=False)


def member_send(array, offset):
    if offset & 1:
        array = xor_send(array, "pb", 1)
    if offset >> 1:
        array = xor_send(array, "ka", offset >> 1)
    return array


def share_with_group(array, members):
    return jnp.concatenate([array] + [member_send(array, e) for e in range(1, members)], axis=0)


class Layout:
    def __init__(self, sequence_ids, sequence_offsets):
        self.core = lax.axis_index("pb") % 2
        self.z = lax.axis_index("ka")
        self.depth = lax.axis_size("ka")
        self.subs = self.depth // 4
        self.members = self.depth // 2
        tall = sequence_ids.shape[0]
        self.rows = tall // OWN
        long = tall // BATCH * self.depth
        heads = slice(None, None, self.rows)
        keys = sequence_ids[heads] * long + sequence_offsets[heads]
        keys = jnp.broadcast_to(keys.reshape(BATCH, HALVES, 1), (BATCH, HALVES, self.subs))
        keys = self.gather_in(keys)[:, 0]
        count = keys.shape[0]
        rank = jnp.sum(keys[None, :] < keys[:, None], axis=1)
        places = jnp.arange(count)
        self.by_rank = jnp.sum(
            jnp.where(rank[None, :] == places[:, None], places[None, :], 0), axis=1
        )
        self.short = jnp.max(keys) // long != jnp.min(keys) // long
        self.member = (self.z % self.subs) * 2 + self.core
        ranks = self.ranks_of(self.member)
        self.ranks = ranks
        start = jnp.where(self.short, ranks // (count // 2) * (count // 2), 0)
        self.bounds = jnp.stack([start, ranks]).astype(jnp.int32)
        held = jnp.concatenate([self.ranks_of(self.member ^ e) for e in range(self.members)])
        self.held_ranks = held
        self.held_by_rank = jnp.sum(
            jnp.where(held[None, :] == places[:, None], places[None, :], 0), axis=1
        )

    def ranks_of(self, member):
        n = self.members
        m = n // 2

        def spread(e, size):
            return jnp.stack([e, 2 * size - 1 - e, 2 * size + e, 4 * size - 1 - e])

        return jnp.where(
            self.short, member // m * (2 * n) + spread(member % m, m), spread(member, n)
        )

    def gather_in(self, array):
        kept, sent = pick(array, self.core, 1), pick(array, 1 - self.core, 1)
        four = jnp.concatenate([kept, xor_send(sent, "pb", 1)], axis=0)
        four = four.reshape((4, self.subs, four.shape[1] // self.subs) + four.shape[2:])
        parts = []
        for shift in range(self.depth):
            target = (self.z + shift) % self.depth
            group, sub = target // self.subs, target % self.subs
            slot = (group // 2 ^ self.core) * 2 + group % 2
            part = pick(pick(four, slot), sub)
            parts.append(shift_send(part, shift) if shift else part)
        held = jnp.stack(parts)
        if self.subs > 1:
            held = jnp.take(held, (self.z - jnp.arange(self.depth)) % self.depth, axis=0)
        held = jnp.stack([held, xor_send(held, "pb", 1)])
        if self.subs > 1:
            groups = [
                [g * self.subs + i for i in range(self.subs)] for g in range(4)
            ]
            held = lax.all_gather(held, "ka", axis=2, axis_index_groups=groups)
            held = held.reshape(held.shape[:2] + (held.shape[2] * held.shape[3],) + held.shape[4:])
        return held.reshape((2 * self.depth,) + held.shape[2:])

    def scatter_out(self, own):
        shared = share_with_group(own, self.members)
        rows, width = own.shape[1:]
        piece = rows // self.subs
        got = []
        for shift in range(self.depth):
            index = shift if self.subs == 1 else (self.z - shift) % self.depth
            place = pick(self.held_by_rank, pick(self.rank_of_piece, index))
            part = pick(shared, place)
            if self.subs > 1:
                part = pick(part.reshape(self.subs, piece, width), self.z % self.subs)
            got.append(shift_send(part, -shift) if shift else part)
        table = jnp.stack(got)
        order = []
        for slot in range(4):
            group = ((slot // 2) ^ self.core) * 2 + slot % 2
            for sub in range(self.subs):
                order.append((group * self.subs + sub - self.z) % self.depth)
        four = jnp.take(table, jnp.stack(order), axis=0).reshape(4, rows, width)
        mine, given = four[:2], xor_send(four[2:], "pb", 1)
        first = self.core == 0
        low = jnp.where(first, mine, given)
        high = jnp.where(first, given, mine)
        return jnp.stack([low, high], axis=1).reshape(BATCH * HALVES * rows, width)

    @property
    def rank_of_piece(self):
        places = jnp.arange(self.by_rank.shape[0])
        return jnp.sum(
            jnp.where(self.by_rank[None, :] == places[:, None], places[None, :], 0), axis=1
        )


def reduce_matrix(gradient, order):
    height, breadth = gradient.shape
    along_pb, along_ka = lax.axis_size("pb"), lax.axis_size("ka")
    bits = along_pb.bit_length() - 1
    place = lax.axis_index("pb")
    view = gradient.astype(BF).reshape((2,) * bits + (height // along_pb, breadth))
    steps = [0] + [b for b in range(1, bits)][::order]
    for b in steps:
        axis = bits - 1 - b
        own = (place >> b) & 1
        kept = lax.dynamic_slice_in_dim(view, own, 1, axis)
        sent = lax.dynamic_slice_in_dim(view, 1 - own, 1, axis)
        view = kept + xor_send(sent, "pb", 1 << b)
    block = view.reshape(height // along_pb, breadth)
    wide = breadth // along_ka
    z = lax.axis_index("ka")
    total = lax.dynamic_slice_in_dim(block, z * wide, wide, 1).astype(F32)
    for shift in range(1, along_ka):
        part = lax.dynamic_slice_in_dim(block, (z + shift) % along_ka * wide, wide, 1)
        total = total + shift_send(part, shift).astype(F32)
    return total


def reduce_vectors(vectors):
    sizes = [v.shape[0] for v in vectors]
    flat = jnp.concatenate(vectors).reshape(-1, 128)
    for axis in ("pb", "ka"):
        bit = 1
        while bit < lax.axis_size(axis):
            flat = flat + xor_send(flat, axis, bit)
            bit *= 2
    flat = flat.reshape(-1)
    result, at = [], 0
    for size in sizes:
        result.append(flat[at : at + size])
        at += size
    return result


def normalized(values):
    centre = values - jnp.mean(values, axis=-1, keepdims=True)
    spread = jnp.mean(centre * centre, axis=-1, keepdims=True)
    scale = lax.rsqrt(spread + EPSILON)
    return centre * scale, scale


def layer_norm(values, gain, shift):
    return (normalized(values)[0] * gain.astype(F32) + shift.astype(F32)).astype(BF)


def norm_backward(values, gain, upstream):
    n, scale = normalized(values)
    grad_gain = jnp.sum(upstream * n, axis=0)
    grad_shift = jnp.sum(upstream, axis=0)
    dn = upstream * gain.astype(F32)
    mean = jnp.mean(dn, axis=-1, keepdims=True)
    along = jnp.mean(dn * n, axis=-1, keepdims=True)
    return scale * (dn - mean - n * along), grad_gain, grad_shift


def gelu_pair(u):
    size = jnp.abs(u) * 0.7071067811865476
    t = 1.0 / (1.0 + 0.3275911 * size)
    bell = jnp.exp(-0.5 * u * u)
    series = t * (
        0.254829592
        + t * (-0.284496736 + t * (1.421413741 + t * (-1.453152027 + t * 1.061405429)))
    )
    tail = 0.5 * series * bell
    phi = jnp.where(u < 0, tail, 1.0 - tail)
    return u * phi, phi + u * (bell * 0.3989422804014327)


def layer_forward(x_own, h_own, h_all, params, layout, signed):
    (_, _, w_query, w_key, w_value, w_out, mlp_gain, mlp_bias, w_up, up_bias, w_down, down_bias) = params
    width = x_own.shape[1]
    rows = layout.rows
    scale = (width // HEADS) ** -0.5
    queries = (dense(h_own, w_query, 1, 0) * scale).astype(BF).reshape(OWN, rows, width)
    keys = dense(h_all, w_key, 1, 0).astype(BF).reshape(-1, rows, width)
    values = dense(h_all, w_value, 1, 0).astype(BF).reshape(-1, rows, width)
    attended, totals = attend_forward(queries, keys, values, layout.bounds, signed)
    middle = x_own + dense(attended.reshape(-1, width), w_out, 1, 0)
    h2 = layer_norm(middle, mlp_gain, mlp_bias)
    hidden = dense(h2, w_up, 1, 0) + up_bias.astype(F32)
    active, slope = gelu_pair(hidden)
    active, slope = active.astype(BF), slope.astype(BF)
    result = middle + (dense(active, w_down, 1, 0) + down_bias.astype(F32))
    return result, (h_own, h_all, queries, keys, values, attended, totals, middle, h2, active, slope)


def layer_backward(upstream, x_own, params, saved, layout, signed):
    (norm_gain, _, w_query, w_key, w_value, w_out, mlp_gain, _, w_up, _, w_down, _) = params
    h_own, h_all, queries, keys, values, attended, totals, middle, h2, active, slope = saved
    tall, width = x_own.shape
    rows = layout.rows
    gb = upstream.astype(BF)
    grad_down_bias = jnp.sum(gb.astype(F32), axis=0)
    grad_down = dense(active, gb, 0, 0)
    du = (dense(gb, w_down, 1, 1) * slope.astype(F32)).astype(BF)
    grad_up_bias = jnp.sum(du.astype(F32), axis=0)
    grad_up = dense(h2, du, 0, 0)
    dh2 = dense(du, w_up, 1, 1)
    dx1, grad_mlp_gain, grad_mlp_bias = norm_backward(middle, mlp_gain, dh2)
    dx1 = upstream + dx1
    gx = dx1.astype(BF)
    grad_out = dense(attended.reshape(tall, width), gx, 0, 0)
    do = dense(gx, w_out, 1, 1).astype(BF).reshape(queries.shape)
    dq, dk, dv = attend_backward(
        queries, do, attended, totals, keys, values, layout.bounds, signed
    )
    dq, dk, dv = dq.reshape(tall, width), dk.reshape(-1, width), dv.reshape(-1, width)
    grad_query = dense(h_own, dq, 0, 0)
    grad_key = dense(h_all, dk, 0, 0)
    grad_value = dense(h_all, dv, 0, 0)
    from_keys = dense(dk, w_key, 1, 1) + dense(dv, w_value, 1, 1)
    from_keys = from_keys.astype(BF).reshape(-1, rows, width)
    by_member = jnp.take(from_keys, layout.held_ranks, axis=0).reshape(
        layout.members, tall, width
    )
    dh = dense(dq, w_query, 1, 1) + by_member[0].astype(F32)
    for e in range(1, layout.members):
        dh = dh + member_send(by_member[e], e).astype(F32)
    dx, grad_norm_gain, grad_norm_bias = norm_backward(x_own, norm_gain, dh)
    matrices = (grad_query, grad_key, grad_value, grad_out, grad_up, grad_down)
    orders = (1, -1, 1, -1, 1, -1)
    matrices = [reduce_matrix(g, o) for g, o in zip(matrices, orders)]
    vectors = (grad_norm_gain, grad_norm_bias, grad_mlp_gain, grad_mlp_bias, grad_up_bias, grad_down_bias)
    vectors = reduce_vectors(vectors)
    gradients = (
        vectors[0], vectors[1], matrices[0], matrices[1], matrices[2], matrices[3],
        vectors[2], vectors[3], matrices[4], vectors[4], matrices[5], vectors[5],
    )
    return dx1 + dx, gradients


def per_device(tokens, sequence_ids, sequence_offsets, *rest):
    signed_params, plain_params, cotangent = rest[:12], rest[12:24], rest[24]
    tall, width = tokens.shape
    layout = Layout(sequence_ids, sequence_offsets)
    shape = (BATCH, HALVES, layout.rows, width)
    x_all = layout.gather_in(tokens.reshape(shape))
    x_sorted = jnp.take(x_all, layout.by_rank, axis=0)
    h_sorted = layer_norm(x_sorted.astype(F32), signed_params[0], signed_params[1])
    x_own = jnp.take(x_sorted, layout.ranks, axis=0).reshape(tall, width).astype(F32)
    h_own = jnp.take(h_sorted, layout.ranks, axis=0).reshape(tall, width)
    between, signed_saved = layer_forward(
        x_own, h_own, h_sorted.reshape(-1, width), signed_params, layout, True
    )
    h_own = layer_norm(between, plain_params[0], plain_params[1])
    h_all = share_with_group(h_own.reshape(OWN, layout.rows, width), layout.members)
    h_all = jnp.take(h_all, layout.held_by_rank, axis=0).reshape(-1, width)
    final, plain_saved = layer_forward(between, h_own, h_all, plain_params, layout, False)
    output = layout.scatter_out(final.astype(BF).reshape(OWN, layout.rows, width))
    own_pieces = jnp.take(layout.by_rank, layout.ranks)
    upstream = jnp.take(layout.gather_in(cotangent.reshape(shape)), own_pieces, axis=0)
    upstream = upstream.reshape(tall, width).astype(F32)
    upstream, plain_grads = layer_backward(
        upstream, between, plain_params, plain_saved, layout, False
    )
    upstream, signed_grads = layer_backward(
        upstream, x_own, signed_params, signed_saved, layout, True
    )
    back = layout.scatter_out(upstream.astype(BF).reshape(OWN, layout.rows, width))
    return (output, back.astype(F32)) + signed_grads + plain_grads


def solution(mesh):
    rows, block = P(("pb", "ka"), None), P("pb", "ka")
    grads = (P(), P(), block, block, block, block, P(), P(), block, P(), block, P())
    return jax.shard_map(
        per_device,
        mesh=mesh,
        in_specs=(rows, P(("pb", "ka")), P(("pb", "ka"))) + (P(),) * 24 + (rows,),
        out_specs=(rows, rows) + grads + grads,
        check_vma=False,
    )
```

time: 3520 us -> 1100 us (0.31)
  waiting for transfers between devices: 2040 us -> 213 us
  matrix products: 885 us -> 218 us
  Pallas kernels: 0 us -> 318 us
  other arithmetic: 304 us -> 104 us
  starting transfers between devices: 2.24 us -> 125 us
  local copies, waits for them, and re-layouts: 203 us -> 93.4 us
  blocking collectives: 61.4 us -> 0 us
    reduce_scatter x16 -> x0, waiting for transfers between devices: 1430 us -> none  [the longest x2 218 us: attend_by_queries(): lax.psum_scatter(merge_heads(term_parts).astype(jnp.bfloat16), 'ka', scat...]
    dot_general x48 -> x36, matrix products: 885 us -> 218 us  [dense(): lax.dot_general(left, right, (((left_axis,), (right_axis,)), ((), ())), p...]
    all_gather x4 -> x0, waiting for transfers between devices: 429 us -> none  [the longest x2 231 us: layer_backward(): lax.all_gather(grad_attended.reshape(grouped), 'ka', axis=1, tiled=True)]
    pallas_call x0 -> x4, Pallas kernels: none -> 318 us  [the longest x2 183 us: attend_backward(): pl.pallas_call(functools.partial(backward_kernel, head, count, signed), o...]
    ppermute x0 -> x110, waiting for transfers between devices: none -> 213 us  [the longest x51 127 us: shift_send(): lax.ppermute(array, 'ka', [(i, (i + shift) % size) for i in range(size)])]
    convert_element_type x24 -> x16, other arithmetic: 198 us -> 19.8 us  [the longest x2 6 us: layer_norm(): (normalized(values)[0] * gain.astype(F32) + shift.astype(F32)).astype(BF)]
    ppermute x0 -> x110, starting transfers between devices: none -> 125 us  [the longest x51 79.9 us: shift_send(): lax.ppermute(array, 'ka', [(i, (i + shift) % size) for i in range(size)])]
    psum x4 -> x0, waiting for transfers between devices: 112 us -> none  [the longest x2 65.5 us: delta_total(): lax.psum(partial_value.astype(jnp.bfloat16), 'ka').astype(jnp.float32)]
  transfers between devices with their start and end apart: 26 -> 110, of which waited for: 24 -> 45; matrix products, arithmetic and copies ran while one was open for 12% -> 27% of each run, Pallas kernels for 0% -> 15%
where the time goes in v1:
time: 1100 us
  Pallas kernels  318 us (29%)
  matrix products  218 us (20%)
  waiting for transfers between devices  213 us (19%)
  starting transfers between devices  125 us (11%)
  other arithmetic  104 us (9%)
  local copies, waits for them, and re-layouts  93.4 us (8%)
  between operations  24.9 us (2%)
    dot_general x36, matrix products, dense(): lax.dot_general(left, right, (((left_axis,), (right_axis,)), ((), ())), p...  218 us
    pallas_call x2, Pallas kernels, attend_backward(): pl.pallas_call(functools.partial(backward_kernel, head, count, signed), o...  183 us
    pallas_call x2, Pallas kernels, attend_forward(): pl.pallas_call(functools.partial(forward_kernel, head, count, signed), ou...  135 us
    ppermute x51, waiting for transfers between devices, shift_send(): lax.ppermute(array, 'ka', [(i, (i + shift) % size) for i in range(size)])  127 us
    ppermute x59, waiting for transfers between devices, xor_send(): return lax.ppermute(array, axis, [(i, i ^ bit) for i in range(size)])  85.3 us
    ppermute x51, starting transfers between devices, shift_send(): lax.ppermute(array, 'ka', [(i, (i + shift) % size) for i in range(size)])  79.9 us
    ppermute x59, starting transfers between devices, xor_send(): return lax.ppermute(array, axis, [(i, i ^ bit) for i in range(size)])  45.4 us
    unnamed x300, local copies, waits for them, and re-layouts  26.2 us
  transfers between devices with their start and end apart: 110, of which 45 were waited for; matrix products, arithmetic and copies ran while one was open for 27% of the time, Pallas kernels for 15%

profile of v1, /device:TPU:0, one launch (start us, length us, event | category | flops | bytes accessed | tf_op | source)
XLA Modules:
  0.0 1096.0 jit_solution(1493702635798221882)
XLA Ops:
  56.9 7.7 collective-permute-done.3
  64.7 23.4 %collective-permute-done.2 = bf16[256,768]{1,0:T(8,128)(2,1)S(1)} collective-permute-done((bf16[256,768]{1,0:T(8,128)(2,1)S(1)}, bf16[256,768]{1,0:T(8,128)(2,1)S(1)}, u32[]{:S(2)}, u32[]{:S(2)}) %collective-permute-start.2) | collective-permute-done | bytes 393248 | tf_op jit(solution)/shard_map/ppermute | solution.py:256
  95.1 7.3 collective-permute-done.19
  102.5 25.7 %collective-permute-done.18 = bf16[256,768]{1,0:T(8,128)(2,1)S(1)} collective-permute-done((bf16[256,768]{1,0:T(8,128)(2,1)S(1)}, bf16[256,768]{1,0:T(8,128)(2,1)S(1)}, u32[]{:S(2)}, u32[]{:S(2)}) %collective-permute-start.18) | collective-permute-done | bytes 393248 | tf_op jit(solution)/shard_map/ppermute | solution.py:256
  166.7 69.7 %shard_map.467 = (bf16[4,256,768]{2,1,0:T(8,128)(2,1)S(1)}, f32[12,4,256]{2,1,0:T(4,128)S(1)}) custom-call(s32[2,4]{1,0:T(2,128)S(1)} %pad_add_fusion.bounds, bf16[4,256,768]{2,1,0:T(8,128)(2,1)S(1)} %bitcast.398, bf16[8,256,768]{2,1,0:T(8,128)(2,1)} %bitcast.407, bf16[8,256,768]{2,1,0:T(8,128)(2,1)} %bitcast.409), custom_call_target="tpu_custom_call" | custom-call | tf_op jit(solution)/shard_map/pallas_call | solution.py:111
  240.3 17.0 %multiply_convert_fusion.3 = (bf16[1024,3072]{1,0:T(8,128)(2,1)S(1)}, f32[1024,3072]{1,0:T(8,128)}) fusion(f32[3072]{0:T(1024)S(1)} %copy-done.75, bf16[768,3072]{1,0:T(8,128)(2,1)S(1)} %bitcast.491, f32[1024,768]{1,0:T(8,128)S(1)} %get-tuple-element.186, f32[768]{0:T(1024)S(1)} %copy-done.85, f32[768]{0:T(1024)S(1)} %copy-done.66, ...), kind=kOutput, calls=%fused_computation.27 | convolution fusion | flops 4908122112 | bytes 26765312 | tf_op jit(solution)/shard_map/dot_general | solution.py:30
  314.8 64.9 %shard_map.468 = (bf16[4,256,768]{2,1,0:T(8,128)(2,1)S(1)}, f32[12,4,256]{2,1,0:T(4,128)S(1)}) custom-call(s32[2,4]{1,0:T(2,128)S(1)} %pad_add_fusion.bounds, bf16[4,256,768]{2,1,0:T(8,128)(2,1)S(1)} %bitcast.400, bf16[8,256,768]{2,1,0:T(8,128)(2,1)} %bitcast.411, bf16[8,256,768]{2,1,0:T(8,128)(2,1)} %bitcast.413), custom_call_target="tpu_custom_call" | custom-call | tf_op jit(solution)/shard_map/pallas_call | solution.py:111
  383.7 17.4 %multiply_convert_fusion.2 = (bf16[1024,3072]{1,0:T(8,128)(2,1)}, f32[1024,3072]{1,0:T(8,128)}) fusion(f32[3072]{0:T(1024)S(1)} %copy-done.77, bf16[768,3072]{1,0:T(8,128)(2,1)S(1)} %bitcast.485, f32[1024,768]{1,0:T(8,128)S(1)} %get-tuple-element.192, f32[768]{0:T(1024)S(1)} %copy-done.88, f32[768]{0:T(1024)S(1)} %copy-done.65, ...), kind=kOutput, calls=%fused_computation.22 | convolution fusion | flops 4908122112 | bytes 26765312 | tf_op jit(solution)/shard_map/dot_general | solution.py:30
  401.1 19.5 %convert_reduce_fusion = (f32[3072]{0:T(1024)}, bf16[1024,3072]{1,0:T(8,128)(2,1)}) fusion(f32[1024,3072]{1,0:T(8,128)} %get-tuple-element.198, f32[3072]{0:T(1024)S(1)} %copy-done.77, bf16[1024,768]{1,0:T(8,128)(2,1)S(1)} %bitcast.418, bf16[3072,768]{1,0:T(8,128)(2,1)} %param.59), kind=kOutput, calls=%fused_computation.16 | convolution fusion | flops 4926206976 | bytes 25190400 | tf_op jit(solution)/shard_map/dot_general | solution.py:30
  420.6 9.8 multiply_reduce_fusion
  436.9 7.7 convolution_convert_fusion.1
  444.7 86.6 %shard_map.469 = (bf16[4,256,768]{2,1,0:T(8,128)(2,1)}, bf16[8,256,768]{2,1,0:T(8,128)(2,1)}, bf16[8,256,768]{2,1,0:T(8,128)(2,1)}) custom-call(s32[2,4]{1,0:T(2,128)} %copy-done.9, bf16[4,256,768]{2,1,0:T(8,128)(2,1)} %bitcast.401, bf16[4,256,768]{2,1,0:T(8,128)(2,1)} %bitcast.449, bf16[4,256,768]{2,1,0:T(8,128)(2,1)} %copy-done.6, ...), custom_call_target="tpu_custom_call" | custom-call | tf_op jit(solution)/shard_map/pallas_call | solution.py:216
  555.2 9.3 convolution_convert_fusion
  649.6 18.5 %convert_reduce_fusion.1 = (f32[3072]{0:T(1024)S(1)}, bf16[1024,3072]{1,0:T(8,128)(2,1)}) fusion(f32[1024,3072]{1,0:T(8,128)} %get-tuple-element.188, f32[3072]{0:T(1024)S(1)} %copy-done.76, bf16[3072,768]{1,0:T(8,128)(2,1)} %param.47, f32[1024,768]{1,0:T(8,128)S(1)} %get-tuple-element.72), kind=kOutput, calls=%fused_computation.17 | convolution fusion | flops 4926993408 | bytes 26763264 | tf_op jit(solution)/shard_map/dot_general | solution.py:30
  668.1 10.0 multiply_reduce_fusion.2
  684.4 7.2 convolution_convert_fusion.2
  691.7 96.7 %shard_map.470 = (bf16[4,256,768]{2,1,0:T(8,128)(2,1)}, bf16[8,256,768]{2,1,0:T(8,128)(2,1)}, bf16[8,256,768]{2,1,0:T(8,128)(2,1)}) custom-call(s32[2,4]{1,0:T(2,128)} %copy-done.9, bf16[4,256,768]{2,1,0:T(8,128)(2,1)} %bitcast.399, bf16[4,256,768]{2,1,0:T(8,128)(2,1)} %bitcast.450, bf16[4,256,768]{2,1,0:T(8,128)(2,1)} %copy-done.4, ...), custom_call_target="tpu_custom_call" | custom-call | tf_op jit(solution)/shard_map/pallas_call | solution.py:216
  814.5 8.9 convolution_convert_fusion.3
  937.9 20.9 %collective-permute-done.29 = f32[54,128]{1,0:T(8,128)S(1)} collective-permute-done((f32[54,128]{1,0:T(8,128)S(1)}, f32[54,128]{1,0:T(8,128)S(1)}, u32[]{:S(2)}, u32[]{:S(2)}) %collective-permute-start.29) | collective-permute-done | bytes 27680 | tf_op jit(solution)/shard_map/ppermute | solution.py:251
  978.1 13.0 %collective-permute-done.106 = bf16[1,1,1,384,768]{3,4,2,1,0:T(8,128)(2,1)S(1)} collective-permute-done((bf16[1,1,1,384,768]{3,4,2,1,0:T(8,128)(2,1)S(1)}, bf16[1,1,1,384,768]{3,4,2,1,0:T(8,128)(2,1)S(1)}, u32[]{:S(2)}, u32[]{:S(2)}) %collective-permute-start.106) | collective-permute-done | bytes 589856 | tf_op jit(solution)/shard_map/ppermute | solution.py:251
  1027.4 15.1 %collective-permute-done.64 = bf16[1,2,1,384,768]{3,4,2,1,0:T(8,128)(2,1)S(1)} collective-permute-done((bf16[1,2,1,384,768]{3,4,2,1,0:T(8,128)(2,1)S(1)}, bf16[1,2,1,384,768]{3,4,2,1,0:T(8,128)(2,1)S(1)}, u32[]{:S(2)}, u32[]{:S(2)}) %collective-permute-start.64) | collective-permute-done | bytes 1179680 | tf_op jit(solution)/shard_map/ppermute | solution.py:251
  1056.3 8.6 collective-permute-start.62
  1073.6 8.1 collective-permute-done.61
  1084.4 6.8 collective-permute-done.67
  (779 shorter events, 491.3 us)
Async XLA Ops:
  6.0 44.1 %collective-permute-start = (bf16[2,256,768]{2,1,0:T(8,128)(2,1)}, bf16[2,256,768]{2,1,0:T(8,128)(2,1)}, u32[]{:S(2)}, u32[]{:S(2)}) collective-permute-start(bf16[2,256,768]{2,1,0:T(8,128)(2,1)} %get-tuple-element.121), channel_id=1, source_target_pairs={{0,4},{4,0},{8,12},{12,8},{16,20},{20,16},{24,28},{28,24},{1,5},{5... | collective-permute-start | bytes 2359304 | tf_op jit(solution)/shard_map/ppermute | solution.py:251
  7.1 83.3 %collective-permute-start.16 = (bf16[2,256,768]{2,1,0:T(8,128)(2,1)}, bf16[2,256,768]{2,1,0:T(8,128)(2,1)S(1)}, u32[]{:S(2)}, u32[]{:S(2)}) collective-permute-start(bf16[2,256,768]{2,1,0:T(8,128)(2,1)} %get-tuple-element.113), channel_id=1, source_target_pairs={{0,4},{4,0},{8,12},{12,8},{16,20},{20,16},{24,28},{28,24},{1,5},{5... | collective-permute-start | bytes 2359304 | tf_op jit(solution)/shard_map/ppermute | solution.py:251
  52.4 35.6 %collective-permute-start.2 = (bf16[256,768]{1,0:T(8,128)(2,1)S(1)}, bf16[256,768]{1,0:T(8,128)(2,1)S(1)}, u32[]{:S(2)}, u32[]{:S(2)}) collective-permute-start(bf16[256,768]{1,0:T(8,128)(2,1)S(1)} %get-tuple-element.119), channel_id=1, source_target_pairs={{0,2},{1,3},{2,0},{3,1},{4,6},{5,7},{6,4},{7,5},{8,10},{9,11},{10,... | collective-permute-start | bytes 1179656 | tf_op jit(solution)/shard_map/ppermute | solution.py:256
  53.1 35.0 %collective-permute-start.1 = (bf16[256,768]{1,0:T(8,128)(2,1)S(1)}, bf16[256,768]{1,0:T(8,128)(2,1)S(1)}, u32[]{:S(2)}, u32[]{:S(2)}) collective-permute-start(bf16[256,768]{1,0:T(8,128)(2,1)S(1)} %get-tuple-element.118), channel_id=1, source_target_pairs={{0,1},{1,2},{2,3},{3,0},{4,5},{5,6},{6,7},{7,4},{8,9},{9,10},{10,1... | collective-permute-start | bytes 1179656 | tf_op jit(solution)/shard_map/ppermute | solution.py:256
  88.3 41.7 %collective-permute-start.4 = (bf16[4,256,768]{2,1,0:T(8,128)(2,1)S(1)}, bf16[4,256,768]{2,1,0:T(8,128)(2,1)S(1)}, u32[]{:S(2)}, u32[]{:S(2)}) collective-permute-start(bf16[4,256,768]{2,1,0:T(8,128)(2,1)S(1)} %get-tuple-element.116), channel_id=1, source_target_pairs={{0,4},{4,0},{8,12},{12,8},{16,20},{20,16},{24,28},{28,24},{1,5},{5... | collective-permute-start | bytes 4718600 | tf_op jit(solution)/shard_map/ppermute | solution.py:251
  91.0 37.1 %collective-permute-start.18 = (bf16[256,768]{1,0:T(8,128)(2,1)S(1)}, bf16[256,768]{1,0:T(8,128)(2,1)S(1)}, u32[]{:S(2)}, u32[]{:S(2)}) collective-permute-start(bf16[256,768]{1,0:T(8,128)(2,1)S(1)} %get-tuple-element.111), channel_id=1, source_target_pairs={{0,2},{1,3},{2,0},{3,1},{4,6},{5,7},{6,4},{7,5},{8,10},{9,11},{10,... | collective-permute-start | bytes 1179656 | tf_op jit(solution)/shard_map/ppermute | solution.py:256
  93.2 34.9 %collective-permute-start.17 = (bf16[256,768]{1,0:T(8,128)(2,1)S(1)}, bf16[256,768]{1,0:T(8,128)(2,1)S(1)}, u32[]{:S(2)}, u32[]{:S(2)}) collective-permute-start(bf16[256,768]{1,0:T(8,128)(2,1)S(1)} %get-tuple-element.110), channel_id=1, source_target_pairs={{0,1},{1,2},{2,3},{3,0},{4,5},{5,6},{6,7},{7,4},{8,9},{9,10},{10,1... | collective-permute-start | bytes 1179656 | tf_op jit(solution)/shard_map/ppermute | solution.py:256
  130.0 153.8 %collective-permute-start.20 = (bf16[4,256,768]{2,1,0:T(8,128)(2,1)}, bf16[4,256,768]{2,1,0:T(8,128)(2,1)}, u32[]{:S(2)}, u32[]{:S(2)}) collective-permute-start(bf16[4,256,768]{2,1,0:T(8,128)(2,1)} %get-tuple-element.108), channel_id=1, source_target_pairs={{0,4},{4,0},{8,12},{12,8},{16,20},{20,16},{24,28},{28,24},{1,5},{5... | collective-permute-start | bytes 4718600 | tf_op jit(solution)/shard_map/ppermute | solution.py:251
  265.1 30.4 %collective-permute-start.10 = (bf16[4,256,768]{2,1,0:T(8,128)(2,1)}, bf16[4,256,768]{2,1,0:T(8,128)(2,1)}, u32[]{:S(2)}, u32[]{:S(2)}) collective-permute-start(bf16[4,256,768]{2,1,0:T(8,128)(2,1)} %bitcast.48), channel_id=1, source_target_pairs={{0,4},{4,0},{8,12},{12,8},{16,20},{20,16},{24,28},{28,24},{1,5},{5... | collective-permute-start | bytes 4718600 | tf_op jit(solution)/shard_map/ppermute | solution.py:251
  555.2 88.3 %collective-permute-start.21 = (bf16[1024,768]{1,0:T(8,128)(2,1)}, bf16[1024,768]{1,0:T(8,128)(2,1)}, u32[]{:S(2)}, u32[]{:S(2)}) collective-permute-start(bf16[1024,768]{1,0:T(8,128)(2,1)} %bitcast.95), channel_id=1, source_target_pairs={{0,4},{4,0},{8,12},{12,8},{16,20},{20,16},{24,28},{28,24},{1,5},{5... | collective-permute-start | bytes 4718600 | tf_op jit(solution)/shard_map/ppermute | solution.py:251
  571.1 252.4 %collective-permute-start.11 = (bf16[4,256,768]{2,1,0:T(8,128)(2,1)}, bf16[4,256,768]{2,1,0:T(8,128)(2,1)}, u32[]{:S(2)}, u32[]{:S(2)}) collective-permute-start(bf16[4,256,768]{2,1,0:T(8,128)(2,1)} %bitcast.53), channel_id=1, source_target_pairs={{0,4},{4,0},{8,12},{12,8},{16,20},{20,16},{24,28},{28,24},{1,5},{5... | collective-permute-start | bytes 4718600 | tf_op jit(solution)/shard_map/ppermute | solution.py:251
  637.8 245.5 %collective-permute-start.98 = (bf16[2,2,1,96,3072]{4,3,2,1,0:T(8,128)(2,1)}, bf16[2,2,1,96,3072]{4,3,2,1,0:T(8,128)(2,1)}, u32[]{:S(2)}, u32[]{:S(2)}) collective-permute-start(bf16[2,2,1,96,3072]{4,3,2,1,0:T(8,128)(2,1)} %constant_dynamic-slice_fusion.6), channel_id=1, source_target_pairs={{0,4},{4,0},{8,12},{12,8},{16,20},{20,16},{24,28},{28,24},{1,5},{5... | collective-permute-start | bytes 7077896 | tf_op jit(solution)/shard_map/ppermute | solution.py:251
  640.6 237.7 %collective-permute-start.104 = (bf16[2,2,1,384,768]{3,4,2,1,0:T(8,128)(2,1)}, bf16[2,2,1,384,768]{3,4,2,1,0:T(8,128)(2,1)}, u32[]{:S(2)}, u32[]{:S(2)}) collective-permute-start(bf16[2,2,1,384,768]{3,4,2,1,0:T(8,128)(2,1)} %copy.110), channel_id=1, source_target_pairs={{0,4},{4,0},{8,12},{12,8},{16,20},{20,16},{24,28},{28,24},{1,5},{5... | collective-permute-start | bytes 7077896 | tf_op jit(solution)/shard_map/ppermute | solution.py:251
  827.6 34.0 %collective-permute-start.14 = (bf16[256,768]{1,0:T(8,128)(2,1)}, bf16[256,768]{1,0:T(8,128)(2,1)}, u32[]{:S(2)}, u32[]{:S(2)}) collective-permute-start(bf16[256,768]{1,0:T(8,128)(2,1)} %get-tuple-element.102), channel_id=1, source_target_pairs={{0,1},{1,2},{2,3},{3,0},{4,5},{5,6},{6,7},{7,4},{8,9},{9,10},{10,1... | collective-permute-start | bytes 1179656 | tf_op jit(solution)/shard_map/ppermute | solution.py:256
  827.6 34.7 %collective-permute-start.13 = (bf16[256,768]{1,0:T(8,128)(2,1)}, bf16[256,768]{1,0:T(8,128)(2,1)}, u32[]{:S(2)}, u32[]{:S(2)}) collective-permute-start(bf16[256,768]{1,0:T(8,128)(2,1)} %get-tuple-element.101), channel_id=1, source_target_pairs={{0,2},{1,3},{2,0},{3,1},{4,6},{5,7},{6,4},{7,5},{8,10},{9,11},{10,... | collective-permute-start | bytes 1179656 | tf_op jit(solution)/shard_map/ppermute | solution.py:256
  868.0 51.7 %collective-permute-start.22 = (bf16[1024,768]{1,0:T(8,128)(2,1)}, bf16[1024,768]{1,0:T(8,128)(2,1)}, u32[]{:S(2)}, u32[]{:S(2)}) collective-permute-start(bf16[1024,768]{1,0:T(8,128)(2,1)} %bitcast.446), channel_id=1, source_target_pairs={{0,4},{4,0},{8,12},{12,8},{16,20},{20,16},{24,28},{28,24},{1,5},{5... | collective-permute-start | bytes 4718600 | tf_op jit(solution)/shard_map/ppermute | solution.py:251
  877.4 98.5 %collective-permute-start.57 = (bf16[2,2,1,96,3072]{4,3,2,1,0:T(8,128)(2,1)S(1)}, bf16[2,2,1,96,3072]{4,3,2,1,0:T(8,128)(2,1)S(1)}, u32[]{:S(2)}, u32[]{:S(2)}) collective-permute-start(bf16[2,2,1,96,3072]{4,3,2,1,0:T(8,128)(2,1)S(1)} %copy-done.33), channel_id=1, source_target_pairs={{0,4},{4,0},{8,12},{12,8},{16,20},{20,16},{24,28},{28,24},{1,5},{5... | collective-permute-start | bytes 7077896 | tf_op jit(solution)/shard_map/ppermute | solution.py:251
  915.1 62.2 %collective-permute-start.63 = (bf16[2,2,1,384,768]{3,4,2,1,0:T(8,128)(2,1)S(1)}, bf16[2,2,1,384,768]{3,4,2,1,0:T(8,128)(2,1)S(1)}, u32[]{:S(2)}, u32[]{:S(2)}) collective-permute-start(bf16[2,2,1,384,768]{3,4,2,1,0:T(8,128)(2,1)S(1)} %copy-done.34), channel_id=1, source_target_pairs={{0,4},{4,0},{8,12},{12,8},{16,20},{20,16},{24,28},{28,24},{1,5},{5... | collective-permute-start | bytes 7077896 | tf_op jit(solution)/shard_map/ppermute | solution.py:251
  930.1 42.6 %collective-permute-start.99 = (bf16[2,1,1,96,3072]{4,3,2,1,0:T(8,128)(2,1)S(1)}, bf16[2,1,1,96,3072]{4,3,2,1,0:T(8,128)(2,1)S(1)}, u32[]{:S(2)}, u32[]{:S(2)}) collective-permute-start(bf16[2,1,1,96,3072]{4,3,2,1,0:T(8,128)(2,1)S(1)} %constant_dynamic-slice_fusion.5), channel_id=1, source_target_pairs={{0,8},{4,12},{8,0},{12,4},{16,24},{20,28},{24,16},{28,20},{1,9},{5... | collective-permute-start | bytes 3538952 | tf_op jit(solution)/shard_map/ppermute | solution.py:251
  932.8 41.7 %collective-permute-start.105 = (bf16[1,2,1,384,768]{3,4,2,1,0:T(8,128)(2,1)S(1)}, bf16[1,2,1,384,768]{3,4,2,1,0:T(8,128)(2,1)S(1)}, u32[]{:S(2)}, u32[]{:S(2)}) collective-permute-start(bf16[1,2,1,384,768]{3,4,2,1,0:T(8,128)(2,1)S(1)} %constant_dynamic-slice_fusion.1), channel_id=1, source_target_pairs={{0,16},{4,20},{8,24},{12,28},{16,0},{20,4},{24,8},{28,12},{1,17},{... | collective-permute-start | bytes 3538952 | tf_op jit(solution)/shard_map/ppermute | solution.py:251
  971.5 48.9 %collective-permute-start.23 = (bf16[4,256,768]{2,1,0:T(8,128)(2,1)S(1)}, bf16[4,256,768]{2,1,0:T(8,128)(2,1)S(1)}, u32[]{:S(2)}, u32[]{:S(2)}) collective-permute-start(bf16[4,256,768]{2,1,0:T(8,128)(2,1)S(1)} %bitcast.420), channel_id=1, source_target_pairs={{0,4},{4,0},{8,12},{12,8},{16,20},{20,16},{24,28},{28,24},{1,5},{5... | collective-permute-start | bytes 4718600 | tf_op jit(solution)/shard_map/ppermute | solution.py:251
  976.3 49.5 %collective-permute-start.58 = (bf16[2,1,1,96,3072]{4,3,2,1,0:T(8,128)(2,1)S(1)}, bf16[2,1,1,96,3072]{4,3,2,1,0:T(8,128)(2,1)S(1)}, u32[]{:S(2)}, u32[]{:S(2)}) collective-permute-start(bf16[2,1,1,96,3072]{4,3,2,1,0:T(8,128)(2,1)S(1)} %constant_dynamic-slice_fusion.24), channel_id=1, source_target_pairs={{0,8},{4,12},{8,0},{12,4},{16,24},{20,28},{24,16},{28,20},{1,9},{5... | collective-permute-start | bytes 3538952 | tf_op jit(solution)/shard_map/ppermute | solution.py:251
  1054.0 38.1 %collective-permute-start.15 = (bf16[2,256,768]{2,1,0:T(8,128)(2,1)S(1)}, bf16[2,256,768]{2,1,0:T(8,128)(2,1)S(1)}, u32[]{:S(2)}, u32[]{:S(2)}) collective-permute-start(bf16[2,256,768]{2,1,0:T(8,128)(2,1)S(1)} %slice.165), channel_id=1, source_target_pairs={{0,4},{4,0},{8,12},{12,8},{16,20},{20,16},{24,28},{28,24},{1,5},{5... | collective-permute-start | bytes 2359304 | tf_op jit(solution)/shard_map/ppermute | solution.py:251
  1054.1 39.5 %collective-permute-start.27 = (bf16[2,256,768]{2,1,0:T(8,128)(2,1)S(1)}, bf16[2,256,768]{2,1,0:T(8,128)(2,1)S(1)}, u32[]{:S(2)}, u32[]{:S(2)}) collective-permute-start(bf16[2,256,768]{2,1,0:T(8,128)(2,1)S(1)} %slice.171), channel_id=1, source_target_pairs={{0,4},{4,0},{8,12},{12,8},{16,20},{20,16},{24,28},{28,24},{1,5},{5... | collective-permute-start | bytes 2359304 | tf_op jit(solution)/shard_map/ppermute | solution.py:251
  (228 other events, 3681.4 us)

commit v2 on v1

v2 whole, which is shorter than its diff:
```python
import functools

import jax
import jax.numpy as jnp
from jax import lax
from jax.experimental import pallas as pl
from jax.experimental.pallas import tpu as pltpu
from jax.sharding import PartitionSpec as P

HEADS = 12
BATCH = 2
HALVES = 2
OWN = BATCH * HALVES
EPSILON = 1e-05
FLOOR = -1e30
LEAST, MOST = 1e-25, 1e30
BF = jnp.bfloat16
F32 = jnp.float32
MIB = 1 << 20

NT = (((1,), (1,)), ((), ()))
NN = (((1,), (0,)), ((), ()))
TN = (((0,), (0,)), ((), ()))


def dot(left, right, dims=NN):
    return lax.dot_general(left, right, dims, preferred_element_type=F32)


def dense(left, right, left_axis, right_axis):
    return lax.dot_general(
        left, right, (((left_axis,), (right_axis,)), ((), ())), preferred_element_type=F32
    )


def attention_sizes(width):
    head = width // HEADS
    lanes = 256
    while width % lanes or lanes % head:
        lanes //= 2
    return head, lanes, width // lanes, lanes // head


def head_parts(block, head, count):
    tile = min(128, block.shape[1])
    per = tile // head
    lane = lax.broadcasted_iota(jnp.int32, (block.shape[0], tile), 1) // head
    tiles = [block[:, t : t + tile] for t in range(0, block.shape[1], tile)]
    zero = jnp.zeros_like(tiles[0])
    return [jnp.where(lane == h % per, tiles[h // per], zero) for h in range(count)]


def tiles_of(block, head, count):
    tile = min(128, block.shape[1])
    per = tile // head
    tiles = [block[:, t : t + tile] for t in range(0, block.shape[1], tile)]
    return [tiles[h // per] for h in range(count)]


def join_tiles(parts, head):
    per = parts[0].shape[1] // head
    sums = [sum(parts[h + 1 : h + per], parts[h]) for h in range(0, len(parts), per)]
    return sums[0] if len(sums) == 1 else jnp.concatenate(sums, axis=1)


def turned(block):
    return jnp.transpose(block.astype(F32))


def causal(shape):
    key = lax.broadcasted_iota(jnp.int32, shape, 0)
    query = lax.broadcasted_iota(jnp.int32, shape, 1)
    return key <= query


def forward_kernel(head, count, signed, bounds, order, q_ref, k_ref, v_ref, o_ref, lse_ref, qm, vt, acc, sums):
    step = pl.program_id(1)

    @pl.when(step == 0)
    def _():
        for j in range(k_ref.shape[0]):
            vt[j] = turned(v_ref[j]).astype(BF)

    for h, part in enumerate(head_parts(q_ref[0], head, count)):
        qm[h] = part
    rows = q_ref.shape[1]
    start, last = bounds[step], bounds[OWN + step]

    def scores(j):
        return [dot(keys, qm[h], NT) for h, keys in enumerate(tiles_of(k_ref[j], head, count))]

    def magnitude(s, masked):
        c, ratio = s, None
        if signed:
            square = s * s + 1.0
            inverse = lax.rsqrt(square)
            c, ratio = square * inverse, s * inverse
        if masked:
            c = jnp.where(causal(c.shape), c, FLOOR)
        return c, ratio

    def weigh(j, h, raised, ratio):
        if signed:
            raised = raised * ratio
        return dot(vt[j, h * head : (h + 1) * head, :], raised.astype(BF))

    def plain_block(j, carry, masked):
        result = []
        for h, s in enumerate(scores(j)):
            c, ratio = magnitude(s, masked)
            raised = jnp.exp(c)
            result.append(carry[h] + jnp.sum(raised, axis=0, keepdims=True))
            acc[h] += weigh(j, h, raised, ratio)
        return tuple(result)

    def safe_block(j, carry, masked):
        result = []
        for h, s in enumerate(scores(j)):
            top, total = carry[2 * h], carry[2 * h + 1]
            c, ratio = magnitude(s, masked)
            higher = jnp.maximum(top, jnp.max(c, axis=0, keepdims=True))
            raised = jnp.exp(c - higher)
            fade = jnp.exp(top - higher)
            acc[h] = acc[h] * fade + weigh(j, h, raised, ratio)
            result += [higher, total * fade + jnp.sum(raised, axis=0, keepdims=True)]
        return tuple(result)

    def over_keys(block, first):
        acc[...] = jnp.zeros_like(acc)
        carry = lax.fori_loop(start, last, lambda j, c: block(order[j], c, False), first)
        return block(step, carry, True)

    zeros = jnp.zeros((1, rows), F32)
    totals = jnp.concatenate(over_keys(plain_block, (zeros,) * count), axis=0)
    fine = jnp.min(jnp.where((totals > LEAST) & (totals < MOST), 1.0, 0.0)) > 0.5
    sums[...] = totals
    lse_ref[0] = jnp.log(totals)

    @pl.when(jnp.logical_not(fine))
    def _():
        carry = over_keys(safe_block, (zeros + FLOOR, zeros) * count)
        for h in range(count):
            sums[h : h + 1, :] = carry[2 * h + 1]
            lse_ref[0, h : h + 1, :] = carry[2 * h] + jnp.log(carry[2 * h + 1])

    share = 1.0 / sums[...]
    for h in range(count):
        acc[h] = acc[h] * share[h : h + 1, :]
    o_ref[0] = jnp.transpose(acc[...].reshape(count * head, rows)).astype(BF)


def attend_forward(queries, keys, values, tables, signed):
    pieces, rows, width = queries.shape
    whole = keys.shape[0]
    head, lanes, groups, count = attention_sizes(width)
    return pl.pallas_call(
        functools.partial(forward_kernel, head, count, signed),
        out_shape=(
            jax.ShapeDtypeStruct(queries.shape, BF),
            jax.ShapeDtypeStruct((pieces * groups, count, rows), F32),
        ),
        grid_spec=pltpu.PrefetchScalarGridSpec(
            num_scalar_prefetch=2,
            grid=(groups, pieces),
            in_specs=[
                pl.BlockSpec((1, rows, lanes), lambda g, i, b, o: (i, 0, g)),
                pl.BlockSpec((whole, rows, lanes), lambda g, i, b, o: (0, 0, g)),
                pl.BlockSpec((whole, rows, lanes), lambda g, i, b, o: (0, 0, g)),
            ],
            out_specs=[
                pl.BlockSpec((1, rows, lanes), lambda g, i, b, o: (i, 0, g)),
                pl.BlockSpec((1, count, rows), lambda g, i, b, o: (g * pieces + i, 0, 0)),
            ],
            scratch_shapes=[
                pltpu.VMEM((count, rows, min(128, lanes)), BF),
                pltpu.VMEM((whole, lanes, rows), BF),
                pltpu.VMEM((count, head, rows), F32),
                pltpu.VMEM((count, rows), F32),
            ],
        ),
        compiler_params=pltpu.CompilerParams(vmem_limit_bytes=20 * MIB),
        cost_estimate=pl.CostEstimate(flops=50_000_000_000, bytes_accessed=20_000_000, transcendentals=0),
    )(*tables, queries, keys, values)


def backward_kernel(
    head, count, signed, bounds, order, q_ref, do_ref, o_ref, lse_ref, k_ref, v_ref,
    dq_ref, dk_ref, dv_ref, qm, dom, kt, dq, dk, dv, delta,
):
    step = pl.program_id(1)
    whole, rows, lanes = k_ref.shape

    @pl.when(step == 0)
    def _():
        for j in range(whole):
            kt[j] = turned(k_ref[j]).astype(BF)
            dk[j] = jnp.zeros((rows, lanes), F32)
            dv[j] = jnp.zeros((rows, lanes), F32)

    for h, part in enumerate(head_parts(q_ref[0], head, count)):
        qm[h] = part
    for h, part in enumerate(head_parts(do_ref[0], head, count)):
        dom[h] = part
    product = jnp.transpose(do_ref[0].astype(F32) * o_ref[0].astype(F32))
    for h in range(count):
        delta[h : h + 1, :] = jnp.sum(product[h * head : (h + 1) * head], axis=0, keepdims=True)
    dq[...] = jnp.zeros_like(dq)
    start, last = bounds[step], bounds[OWN + step]

    def block(j, masked):
        keys, values = tiles_of(k_ref[j], head, count), tiles_of(v_ref[j], head, count)
        heads = range(count)
        scores = [dot(keys[h], qm[h], NT) for h in heads]
        dps = [dot(values[h], dom[h], NT) for h in heads]
        ps, dss = [], []
        for h, s, dp in zip(heads, scores, dps):
            if signed:
                square = s * s + 1.0
                inverse = lax.rsqrt(square)
                c = square * inverse
            else:
                c = s
            if masked:
                c = jnp.where(causal(c.shape), c, FLOOR)
            w = jnp.exp(c - lse_ref[0, h : h + 1, :])
            if signed:
                ratio = s * inverse
                slope = 1.0 + inverse * inverse * (inverse - 1.0)
                ps.append((w * ratio).astype(BF))
                dss.append((w * (dp * slope - delta[h : h + 1, :] * ratio)).astype(BF))
            else:
                ps.append(w.astype(BF))
                dss.append((w * (dp - delta[h : h + 1, :])).astype(BF))
        dvs, dks = [], []
        for h, p, ds in zip(heads, ps, dss):
            dvs.append(dot(p, dom[h]))
            dks.append(dot(ds, qm[h]))
            dq[h] += dot(kt[j, h * head : (h + 1) * head, :], ds)
        dv[j] += join_tiles(dvs, head)
        dk[j] += join_tiles(dks, head)

    @pl.loop(start, last)
    def _(j):
        block(order[j], False)

    block(step, True)
    turned_back = jnp.transpose(dq[...].reshape(count * head, rows)) * (head ** -0.5)
    dq_ref[0] = turned_back.astype(BF)

    @pl.when(step == pl.num_programs(1) - 1)
    def _():
        for j in range(whole):
            dk_ref[j] = dk[j].astype(BF)
            dv_ref[j] = dv[j].astype(BF)


def attend_backward(queries, grad_rows, attended, totals, keys, values, tables, signed, first, end):
    pieces, rows, width = queries.shape
    whole = keys.shape[0]
    head, lanes, groups, count = attention_sizes(width)
    own = pl.BlockSpec((1, rows, lanes), lambda g, i, b, o: (i, 0, g + first))
    every = pl.BlockSpec((whole, rows, lanes), lambda g, i, b, o: (0, 0, g + first))
    own_out = pl.BlockSpec((1, rows, lanes), lambda g, i, b, o: (i, 0, g))
    every_out = pl.BlockSpec((whole, rows, lanes), lambda g, i, b, o: (0, 0, g))
    spread = (end - first) * lanes
    return pl.pallas_call(
        functools.partial(backward_kernel, head, count, signed),
        out_shape=(
            jax.ShapeDtypeStruct((pieces, rows, spread), BF),
            jax.ShapeDtypeStruct((whole, rows, spread), BF),
            jax.ShapeDtypeStruct((whole, rows, spread), BF),
        ),
        grid_spec=pltpu.PrefetchScalarGridSpec(
            num_scalar_prefetch=2,
            grid=(end - first, pieces),
            in_specs=[
                own,
                own,
                own,
                pl.BlockSpec((1, count, rows), lambda g, i, b, o: ((g + first) * pieces + i, 0, 0)),
                every,
                every,
            ],
            out_specs=[own_out, every_out, every_out],
            scratch_shapes=[
                pltpu.VMEM((count, rows, min(128, lanes)), BF),
                pltpu.VMEM((count, rows, min(128, lanes)), BF),
                pltpu.VMEM((whole, lanes, rows), BF),
                pltpu.VMEM((count, head, rows), F32),
                pltpu.VMEM((whole, rows, lanes), F32),
                pltpu.VMEM((whole, rows, lanes), F32),
                pltpu.VMEM((count, rows), F32),
            ],
        ),
        compiler_params=pltpu.CompilerParams(vmem_limit_bytes=28 * MIB),
        cost_estimate=pl.CostEstimate(flops=25_000_000_000 * (end - first), bytes_accessed=10_000_000, transcendentals=0),
    )(*tables, queries, grad_rows, attended, totals, keys, values)


def xor_send(array, axis, bit):
    size = lax.axis_size(axis)
    return lax.ppermute(array, axis, [(i, i ^ bit) for i in range(size)])


def shift_send(array, shift):
    size = lax.axis_size("ka")
    return lax.ppermute(array, "ka", [(i, (i + shift) % size) for i in range(size)])


def pick(array, index, axis=0):
    return lax.dynamic_index_in_dim(array, index, axis, keepdims=False)


def rows_at(array, index):
    return array.at[index].get(mode="promise_in_bounds")


def together(value, *others):
    return lax.optimization_barrier((value,) + others)[0]


def member_send(array, offset):
    if offset & 1:
        array = xor_send(array, "pb", 1)
    if offset >> 1:
        array = xor_send(array, "ka", offset >> 1)
    return array


def share_with_group(array, members):
    return jnp.concatenate([array] + [member_send(array, e) for e in range(1, members)], axis=0)


def plan_kernel(members, long, keys, me, held_piece, order, bounds, place, rank, by_rank, held):
    count = 4 * members

    def extremes(p, seen):
        return jnp.minimum(seen[0], keys[p]), jnp.maximum(seen[1], keys[p])

    least, most = lax.fori_loop(0, count, extremes, (keys[0], keys[0]))
    short = most - least >= long
    size = jnp.where(short, members // 2, members)

    def rank_one(p, _):
        r = lax.fori_loop(
            0, count, lambda q, r: r + jnp.where(keys[q] < keys[p], 1, 0), jnp.int32(0)
        )
        rank[p] = r
        by_rank[r] = p
        return 0

    lax.fori_loop(0, count, rank_one, 0)
    for e in range(members):
        member = me[0] ^ e
        second = jnp.where(short & (member >= members // 2), 1, 0)
        number = member - second * (members // 2)
        base = second * (2 * members)
        spread = (number, 2 * size - 1 - number, 2 * size + number, 4 * size - 1 - number)
        for i, r in enumerate(spread):
            held[4 * e + i] = base + r
            order[base + r] = 4 * e + i
            held_piece[4 * e + i] = by_rank[base + r]
            if e == 0:
                bounds[i] = base
                bounds[4 + i] = base + r

    def place_one(p, _):
        place[p] = order[rank[p]]
        return 0

    lax.fori_loop(0, count, place_one, 0)


def plan(keys, member, members, long):
    count = 4 * members
    smem = pl.BlockSpec(memory_space=pltpu.SMEM)
    table = jax.ShapeDtypeStruct((count,), jnp.int32)
    return pl.pallas_call(
        functools.partial(plan_kernel, members, long),
        out_shape=(table, table, jax.ShapeDtypeStruct((2 * OWN,), jnp.int32), table),
        in_specs=[smem, smem],
        out_specs=[smem] * 4,
        scratch_shapes=[pltpu.SMEM((count,), jnp.int32)] * 3,
    )(keys, jnp.reshape(member, (1,)).astype(jnp.int32))


class Layout:
    def __init__(self, sequence_ids, sequence_offsets):
        self.core = lax.axis_index("pb") % 2
        self.z = lax.axis_index("ka")
        self.depth = lax.axis_size("ka")
        self.subs = self.depth // 4
        self.members = self.depth // 2
        tall = sequence_ids.shape[0]
        self.rows = tall // OWN
        self.long = tall // BATCH * self.depth
        keys = (sequence_ids * self.long + sequence_offsets).reshape(OWN, self.rows)[:, :1]
        self.keys_under_way = self.send_in(
            jnp.broadcast_to(keys, (OWN, self.subs)).reshape(-1)
        )

    def settle(self):
        keys = self.arrived(self.keys_under_way).reshape(-1, self.subs)[:, 0]
        member = (self.z % self.subs) * 2 + self.core
        self.held_piece, self.order, self.bounds, self.place = plan(
            keys, member, self.members, self.long
        )
        self.tables = (self.bounds, self.order)

    def bits(self, place):
        return place // (2 * self.subs), place // self.subs % 2, place % self.subs

    def round_pairs(self, turn):
        pairs = []
        for pb in range(lax.axis_size("pb")):
            for z in range(self.depth):
                half, batch, sub = (a ^ b for a, b in zip(self.bits(z), self.bits(turn)))
                target = (2 * (pb % 2) + batch) * self.subs + sub
                pairs.append((pb * self.depth + z, (pb // 2 * 2 + half) * self.depth + target))
        return pairs

    def send_in(self, array):
        part_rows = array.shape[0] // (OWN * self.subs)
        blocks = array.reshape((BATCH, HALVES, self.subs, part_rows) + array.shape[1:])
        parts = []
        for turn in range(self.depth):
            half, batch, sub = (a ^ b for a, b in zip(self.bits(self.z), self.bits(turn)))
            part = pick(pick(pick(blocks, batch), half), sub)
            parts.append(lax.ppermute(part, ("pb", "ka"), self.round_pairs(turn)))
        return parts

    def arrived(self, parts):
        if self.subs == 1:
            return jnp.concatenate(parts + [xor_send(part, "pb", 1) for part in parts])
        held = jnp.concatenate(parts)
        part_rows, trailing = parts[0].shape[0], parts[0].shape[1:]
        held = held.reshape((4, self.subs, part_rows) + trailing)
        held = jnp.take(held, self.z % self.subs ^ jnp.arange(self.subs), axis=1)
        quarters = [[g * self.subs + i for i in range(self.subs)] for g in range(4)]
        held = lax.all_gather(held, "ka", axis=2, axis_index_groups=quarters)
        held = held.reshape((4 * self.subs * self.subs * part_rows,) + trailing)
        return jnp.concatenate([held, xor_send(held, "pb", 1)])


class Moving:
    def advance(self, value):
        self.launch(self.prepare(value))


class ScatterOut(Moving):
    def __init__(self, own, layout):
        self.layout = layout
        self.steps = ["first", "second", "assemble"]
        self.result = share_with_group(own, layout.members)

    def prepare(self, value):
        self.now = self.steps.pop(0) if self.steps else None
        turns = self.layout.depth // 2
        if self.now == "first":
            parts = self.parts(value)
            return parts[:turns], parts[turns:]
        return self.assemble(sum(value, [])) if self.now == "assemble" else value

    def launch(self, value):
        turns = self.layout.depth // 2
        if self.now == "first":
            value = (self.send(value[0], 0), value[1])
        elif self.now == "second":
            value = (value[0], self.send(value[1], turns))
        self.result = value

    def send(self, parts, first):
        return [
            lax.ppermute(part, ("pb", "ka"), [(b, a) for a, b in self.layout.round_pairs(turn)])
            for turn, part in enumerate(parts, first)
        ]

    def parts(self, shared):
        layout = self.layout
        subs = layout.subs
        rows, width = shared.shape[1:]
        shared = shared.reshape(-1, subs, rows // subs, width)
        sub = layout.z % subs
        parts = []
        for turn in range(layout.depth):
            piece = turn if subs == 1 else turn // subs * subs + (sub ^ turn % subs)
            parts.append(pick(pick(shared, pick(layout.place, piece)), sub))
        return parts

    def assemble(self, got):
        layout = self.layout
        subs = layout.subs
        order = []
        for block in range(OWN * subs):
            batch, half, part = block // (2 * subs), block // subs % 2, block % subs
            z_half, z_batch, z_sub = layout.bits(layout.z)
            order.append(((z_half ^ half) * 2 + (z_batch ^ batch)) * subs + (z_sub ^ part))
        return rows_at(jnp.stack(got), jnp.stack(order)).reshape(-1, got[0].shape[-1])


class VectorSum(Moving):
    def __init__(self, vectors):
        self.sizes = [v.shape[0] for v in vectors]
        self.steps = []
        for axis in ("ka", "pb"):
            bits = lax.axis_size(axis).bit_length() - 1
            self.steps += [(axis, 1 << b) for b in range(bits)]
        self.advance(jnp.concatenate(vectors).reshape(-1, 128))

    def prepare(self, flat):
        self.now = self.steps.pop(0) if self.steps else None
        return flat

    def launch(self, flat):
        self.result = flat + xor_send(flat, *self.now) if self.now else flat

    def parts(self):
        flat, at, result = self.result.reshape(-1), 0, []
        for size in self.sizes:
            result.append(flat[at : at + size])
            at += size
        return result


class BundleSum(Moving):
    def __init__(self, arrays, segments):
        self.along_pb, self.along_ka = lax.axis_size("pb"), lax.axis_size("ka")
        self.bits = self.along_pb.bit_length() - 1
        rest = list(range(1, self.bits))
        self.steps = list(zip(rest, rest[::-1])) + ["ka"]
        self.narrow = arrays[0][0].shape[-1]
        self.segments = segments
        self.result = []
        for kept, sent in arrays:
            total = kept + xor_send(sent, "pb", 1)
            self.result.append(total.reshape((2,) * (self.bits - 1) + (1,) + kept.shape[1:]))

    def split(self, view, bit):
        axis = self.bits - 1 - bit
        own = (lax.axis_index("pb") >> bit) & 1
        kept = lax.dynamic_slice_in_dim(view, own, 1, axis)
        return kept, lax.dynamic_slice_in_dim(view, 1 - own, 1, axis)

    def prepare(self, views):
        self.now = self.steps.pop(0) if self.steps else None
        if not self.now:
            return views
        if self.now != "ka":
            if len(views) == 1:
                half = views[0].shape[-2] // 2
                views = [views[0][..., :half, :], views[0][..., half:, :]]
            return [self.split(view, bit) for view, bit in zip(views, self.now)]
        return split_columns(
            [v.reshape(-1, self.narrow) for v in views], self.segments, self.along_ka
        )

    def launch(self, made):
        if not self.now:
            self.result = made
        elif self.now != "ka":
            self.result = [
                kept + xor_send(sent, "pb", 1 << bit)
                for (kept, sent), bit in zip(made, self.now)
            ]
        else:
            got = [shift_send(sent, shift) for shift, sent in enumerate(made[1:], 1)]
            self.result = [made[0]] + got

    def matrices(self):
        return join_columns(self.result, self.segments, self.narrow, self.along_ka)


def split_kernel(segments, ways, z, *refs):
    views, outs, whole = refs[:-ways - 1], refs[-ways - 1 : -1], refs[-1]
    at = 0
    for view in views:
        whole[at : at + view.shape[0], :] = view[...]
        at += view.shape[0]
    narrow = whole.shape[1]
    thin = narrow // ways
    for target in range(ways):
        pieces, at = [], 0
        for height, folds in segments:
            share = ways // folds
            first = at + target // share * height
            wide = narrow // share
            for i in range(wide // thin):
                left = target % share * wide + i * thin
                pieces.append(whole[first : first + height, left : left + thin])
            at += height * folds
        rows = jnp.concatenate(pieces, axis=0)
        half = rows.shape[0] // 2
        block = jnp.concatenate([rows[:half], rows[half:]], axis=1)
        for shift in range(ways):

            @pl.when((z[0] + shift) % ways == target)
            def _():
                outs[shift][...] = block


def split_columns(views, segments, ways):
    narrow = views[0].shape[1]
    height = sum(v.shape[0] for v in views)
    shape = jax.ShapeDtypeStruct((height // 2, 2 * narrow // ways), BF)
    vmem = pl.BlockSpec(memory_space=pltpu.VMEM)
    return pl.pallas_call(
        functools.partial(split_kernel, segments, ways),
        out_shape=[shape] * ways,
        in_specs=[pl.BlockSpec(memory_space=pltpu.SMEM)] + [vmem] * len(views),
        out_specs=[vmem] * ways,
        scratch_shapes=[pltpu.VMEM((height, narrow), BF)],
        compiler_params=pltpu.CompilerParams(vmem_limit_bytes=16 * MIB),
    )(lax.axis_index("ka").reshape(1).astype(jnp.int32), *views)


def join_kernel(segments, narrow, ways, *refs):
    parts, outs = refs[:ways], refs[ways:]
    total = parts[0][...].astype(F32)
    for part in parts[1:]:
        total = total + part[...].astype(F32)
    thin = narrow // ways
    rows = jnp.concatenate([total[:, :thin], total[:, thin:]], axis=0)
    at = 0
    for (height, folds), out in zip(segments, outs):
        pieces = [rows[at + i * height : at + (i + 1) * height] for i in range(folds)]
        out[...] = pieces[0] if folds == 1 else jnp.concatenate(pieces, axis=1)
        at += height * folds


def join_columns(parts, segments, narrow, ways):
    vmem = pl.BlockSpec(memory_space=pltpu.VMEM)
    thin = narrow // ways
    return pl.pallas_call(
        functools.partial(join_kernel, segments, narrow, ways),
        out_shape=[jax.ShapeDtypeStruct((height, thin * folds), F32) for height, folds in segments],
        in_specs=[vmem] * ways,
        out_specs=[vmem] * len(segments),
        compiler_params=pltpu.CompilerParams(vmem_limit_bytes=16 * MIB),
    )(*parts)


class Background:
    def __init__(self):
        self.moving = []

    def tick(self, value):
        live = [m for m in self.moving if not getattr(m, "ended", False)]
        value, results = lax.optimization_barrier((value, [m.result for m in live]))
        for m in live:
            m.ended = not m.steps
        made = [m.prepare(r) for m, r in zip(live, results)]
        value, made = lax.optimization_barrier((value, made))
        for m, parts in zip(live, made):
            m.launch(parts)
        return value

    def drain(self):
        for m in self.moving:
            while m.steps:
                m.advance(m.result)


def normalized(values):
    centre = values - jnp.mean(values, axis=-1, keepdims=True)
    spread = jnp.mean(centre * centre, axis=-1, keepdims=True)
    scale = lax.rsqrt(spread + EPSILON)
    return centre * scale, scale


def layer_norm(values, gain, shift):
    return (normalized(values)[0] * gain.astype(F32) + shift.astype(F32)).astype(BF)


def norm_backward(values, gain, upstream):
    n, scale = normalized(values)
    grad_gain = jnp.sum(upstream * n, axis=0)
    grad_shift = jnp.sum(upstream, axis=0)
    dn = upstream * gain.astype(F32)
    mean = jnp.mean(dn, axis=-1, keepdims=True)
    along = jnp.mean(dn * n, axis=-1, keepdims=True)
    return scale * (dn - mean - n * along), grad_gain, grad_shift


def gelu_pair(u):
    size = jnp.abs(u) * 0.7071067811865476
    t = 1.0 / (1.0 + 0.3275911 * size)
    bell = jnp.exp(-0.5 * u * u)
    series = t * (
        0.254829592
        + t * (-0.284496736 + t * (1.421413741 + t * (-1.453152027 + t * 1.061405429)))
    )
    tail = 0.5 * series * bell
    phi = jnp.where(u < 0, tail, 1.0 - tail)
    return u * phi, phi + u * (bell * 0.3989422804014327)


def row_tiles(tall):
    tile = min(256, tall)
    return [slice(r, r + tile) for r in range(0, tall, tile)]


def norm_rows(values, gain, shift):
    centre = values - jnp.mean(values, axis=-1, keepdims=True)
    spread = jnp.mean(centre * centre, axis=-1, keepdims=True)
    return (centre * lax.rsqrt(spread + EPSILON) * gain + shift).astype(BF)


def mlp_kernel(
    following, o_ref, x_ref, wo_ref, gain_ref, bias_ref, wu_ref, ub_ref, wd_ref, db_ref, ng_ref, nb_ref,
    x1_ref, h2_ref, a_ref, s_ref, y_ref, *rest,
):
    acc = rest[-1]
    step = pl.program_id(0)
    tiles = row_tiles(o_ref.shape[0])

    @pl.when(step == 0)
    def _():
        gain, shift = gain_ref[...].astype(F32), bias_ref[...].astype(F32)
        for t in tiles:
            x1 = x_ref[t].astype(F32) + dot(o_ref[t], wo_ref[...])
            x1_ref[t] = x1
            h2_ref[t] = norm_rows(x1, gain, shift)
            acc[t] = jnp.zeros_like(x1)

    up_bias = ub_ref[...].astype(F32)
    for t in tiles:
        u = dot(h2_ref[t], wu_ref[...]) + up_bias
        active, slope = gelu_pair(u)
        active = active.astype(BF)
        a_ref[t] = active
        s_ref[t] = slope.astype(BF)
        acc[t] += dot(active, wd_ref[...])

    @pl.when(step == pl.num_programs(0) - 1)
    def _():
        down_bias = db_ref[...].astype(F32)
        gain, shift = ng_ref[...].astype(F32), nb_ref[...].astype(F32)
        for t in tiles:
            y = x1_ref[t] + (acc[t] + down_bias)
            y_ref[t] = y.astype(y_ref.dtype)
            if following:
                rest[0][t] = norm_rows(y, gain, shift)


ONCE = pl.Buffered(1)


def whole_block(array):
    return pl.BlockSpec(array.shape, lambda i: (0,) * len(array.shape), pipeline_mode=ONCE)


def cost(flops, *arrays):
    moved = sum(a.size * a.dtype.itemsize for a in arrays)
    return pl.CostEstimate(flops=flops, bytes_accessed=moved, transcendentals=0)


def mlp_forward(attended, x_own, params, following):
    (_, _, _, _, _, w_out, mlp_gain, mlp_bias, w_up, up_bias, w_down, down_bias) = params
    tall, width = attended.shape
    hidden = w_up.shape[1]
    row = lambda v: v.reshape(1, -1)
    gain, shift = following or (mlp_gain, mlp_bias)
    inputs = (
        attended, x_own, w_out, row(mlp_gain), row(mlp_bias), w_up, row(up_bias), w_down,
        row(down_bias), row(gain), row(shift),
    )
    specs = [whole_block(a) for a in inputs]
    specs[5] = pl.BlockSpec((width, width), lambda i: (0, i))
    specs[6] = pl.BlockSpec((1, width), lambda i: (0, i))
    specs[7] = pl.BlockSpec((width, width), lambda i: (i, 0))
    wide, narrow = (tall, hidden), (tall, width)
    shapes = [(narrow, F32), (narrow, BF), (wide, BF), (wide, BF), (narrow, F32 if following else BF)]
    shapes += [(narrow, BF)] if following else []
    out_shape = [jax.ShapeDtypeStruct(shape, kind) for shape, kind in shapes]
    chunk = pl.BlockSpec((tall, width), lambda i: (0, i))
    full = pl.BlockSpec((tall, width), lambda i: (0, 0), pipeline_mode=ONCE)
    return pl.pallas_call(
        functools.partial(mlp_kernel, following is not None),
        out_shape=out_shape,
        grid=(hidden // width,),
        in_specs=specs,
        out_specs=[full, full, chunk, chunk, full] + ([full] if following else []),
        scratch_shapes=[pltpu.VMEM((tall, width), F32)],
        compiler_params=pltpu.CompilerParams(vmem_limit_bytes=36 * MIB),
        cost_estimate=cost(2 * tall * width * (2 * hidden + width), *inputs, *out_shape),
    )(*inputs)


def mlp_back_kernel(
    g_ref, slope_ref, wd_ref, wu_ref, x1_ref, gain_ref, wo_ref,
    du_ref, dx_ref, gx_ref, do_ref, gb_ref, sums_ref, vectors_ref, acc,
):
    step = pl.program_id(0)
    tiles = row_tiles(g_ref.shape[0])

    @pl.when(step == 0)
    def _():
        for t in tiles:
            gb_ref[t] = g_ref[t].astype(BF)
            acc[t] = jnp.zeros(acc[t].shape, F32)

    total = 0.0
    for t in tiles:
        da = dot(gb_ref[t], wd_ref[...], NT)
        du = (da * slope_ref[t].astype(F32)).astype(BF)
        du_ref[t] = du
        total = total + jnp.sum(du.astype(F32), axis=0, keepdims=True)
        acc[t] += dot(du, wu_ref[...], NT)
    sums_ref[...] = total

    @pl.when(step == pl.num_programs(0) - 1)
    def _():
        gain = gain_ref[...].astype(F32)
        of_gain = of_shift = of_down = 0.0
        for t in tiles:
            dh2, x1 = acc[t], x1_ref[t]
            centre = x1 - jnp.mean(x1, axis=-1, keepdims=True)
            scale = lax.rsqrt(jnp.mean(centre * centre, axis=-1, keepdims=True) + EPSILON)
            n = centre * scale
            of_gain = of_gain + jnp.sum(dh2 * n, axis=0, keepdims=True)
            of_shift = of_shift + jnp.sum(dh2, axis=0, keepdims=True)
            of_down = of_down + jnp.sum(gb_ref[t].astype(F32), axis=0, keepdims=True)
            dn = dh2 * gain
            mean = jnp.mean(dn, axis=-1, keepdims=True)
            along = jnp.mean(dn * n, axis=-1, keepdims=True)
            dx = g_ref[t].astype(F32) + scale * (dn - mean - n * along)
            dx_ref[t] = dx
            gx = dx.astype(BF)
            gx_ref[t] = gx
            do_ref[t] = dot(gx, wo_ref[...], NT).astype(BF)
        vectors_ref[0:1, :] = of_gain
        vectors_ref[1:2, :] = of_shift
        vectors_ref[2:3, :] = of_down


def mlp_backward(upstream, slope, middle, params):
    (_, _, _, _, _, w_out, mlp_gain, _, w_up, _, w_down, _) = params
    tall, width = upstream.shape
    hidden = slope.shape[1]
    inputs = (upstream, slope, w_down, w_up, middle, mlp_gain.reshape(1, -1), w_out)
    specs = [whole_block(a) for a in inputs]
    specs[1] = pl.BlockSpec((tall, width), lambda i: (0, i))
    specs[2] = pl.BlockSpec((width, width), lambda i: (i, 0))
    specs[3] = pl.BlockSpec((width, width), lambda i: (0, i))
    shapes = [((tall, hidden), BF), ((tall, width), F32)] + [((tall, width), BF)] * 3
    shapes += [((1, hidden), F32), ((3, width), F32)]
    out_shape = [jax.ShapeDtypeStruct(shape, kind) for shape, kind in shapes]
    full = pl.BlockSpec((tall, width), lambda i: (0, 0), pipeline_mode=ONCE)
    return pl.pallas_call(
        mlp_back_kernel,
        out_shape=out_shape,
        grid=(hidden // width,),
        in_specs=specs,
        out_specs=[
            pl.BlockSpec((tall, width), lambda i: (0, i)), full, full, full, full,
            pl.BlockSpec((1, width), lambda i: (0, i)), pl.BlockSpec((3, width), lambda i: (0, 0)),
        ],
        scratch_shapes=[pltpu.VMEM((tall, width), F32)],
        compiler_params=pltpu.CompilerParams(vmem_limit_bytes=40 * MIB),
        cost_estimate=cost(2 * tall * width * (2 * hidden + width), *inputs, *out_shape),
    )(*inputs)


def put_halves(core, kept_ref, sent_ref, low, high):
    @pl.when(core == 0)
    def _():
        kept_ref[...] = low
        sent_ref[...] = high

    @pl.when(core != 0)
    def _():
        kept_ref[...] = high
        sent_ref[...] = low


def by_blocks(product, blocks):
    height, breadth = product.shape
    parts = product.astype(BF).reshape(blocks // 2, 2, height // blocks, breadth)
    return parts[:, 0], parts[:, 1]


def mlp_weights_kernel(
    blocks, folds, core, h2_ref, du_ref, o_ref, gx_ref, a_ref, gb_ref,
    kept_a, sent_a, kept_b, sent_b,
):
    step = pl.program_id(0)

    @pl.when(step < folds)
    def _():
        put_halves(core[0], kept_a, sent_a, *by_blocks(dot(h2_ref[...], du_ref[...], TN), blocks))

    @pl.when(step == folds)
    def _():
        put_halves(core[0], kept_a, sent_a, *by_blocks(dot(o_ref[...], gx_ref[...], TN), blocks))

    @pl.when(step > folds)
    def _():
        product = dot(a_ref[...], gb_ref[...], TN)
        pairs, _, height, _ = kept_b.shape
        parts = product.astype(BF).reshape(pairs, 1, 2, height, product.shape[1])
        put_halves(core[0], kept_b, sent_b, parts[:, :, 0], parts[:, :, 1])


def mlp_weights(h2, du, attended, gx, active, gb):
    blocks = lax.axis_size("pb")
    tall, width = h2.shape
    hidden = du.shape[1]
    folds = hidden // width
    thin, tall_block = width // blocks, hidden // blocks
    pairs = blocks // 2 // folds
    full = pl.BlockSpec((tall, width), lambda i, c: (0, 0), pipeline_mode=ONCE)
    a_block = pl.BlockSpec(
        (blocks // 2, thin, width), lambda i, c: (0, jnp.minimum(i, folds), 0)
    )
    b_block = pl.BlockSpec(
        (pairs, 1, tall_block, width), lambda i, c: (jnp.maximum(i - folds - 1, 0), 0, 0, 0)
    )
    a_shape = jax.ShapeDtypeStruct((blocks // 2, thin * (folds + 1), width), BF)
    b_shape = jax.ShapeDtypeStruct((blocks // 2, 1, tall_block, width), BF)
    core = (lax.axis_index("pb") % 2).reshape(1).astype(jnp.int32)
    inputs = (h2, du, attended, gx, active, gb)
    kept_a, sent_a, kept_b, sent_b = pl.pallas_call(
        functools.partial(mlp_weights_kernel, blocks, folds),
        out_shape=(a_shape, a_shape, b_shape, b_shape),
        grid_spec=pltpu.PrefetchScalarGridSpec(
            num_scalar_prefetch=1,
            grid=(2 * folds + 1,),
            in_specs=[
                full,
                pl.BlockSpec((tall, width), lambda i, c: (0, jnp.minimum(i, folds - 1))),
                full,
                full,
                pl.BlockSpec((tall, width), lambda i, c: (0, jnp.clip(i - folds - 1, 0, folds - 1))),
                full,
            ],
            out_specs=[a_block, a_block, b_block, b_block],
        ),
        compiler_params=pltpu.CompilerParams(vmem_limit_bytes=32 * MIB),
        cost_estimate=cost(2 * tall * width * (2 * hidden + width), *inputs, a_shape, b_shape),
    )(core, *inputs)
    flat = lambda v: v.reshape(blocks // 2, tall_block, width)
    arrays = [(kept_a, sent_a), (flat(kept_b), flat(sent_b))]
    return BundleSum(arrays, [(thin, folds), (thin, 1), (tall_block, 1)])


def attention_weights_kernel(blocks, core, *refs):
    h_ref, kept_ref, sent_ref = refs[0], refs[-2], refs[-1]
    parts = refs[1:-2]
    count = len(parts) // 3
    for which in range(3):

        @pl.when(pl.program_id(0) == which)
        def _():
            products = [
                dot(h_ref[: part.shape[0], :], part[...], TN)
                for part in parts[which * count : (which + 1) * count]
            ]
            product = products[0] if count == 1 else jnp.concatenate(products, axis=1)
            put_halves(core[0], kept_ref, sent_ref, *by_blocks(product, blocks))


def attention_weights(h_all, dqs, dks, dvs):
    blocks = lax.axis_size("pb")
    width = h_all.shape[1]
    thin = width // blocks
    inputs = (h_all, *dqs, *dks, *dvs)
    block = pl.BlockSpec((blocks // 2, thin, width), lambda i, c: (0, i, 0))
    shape = jax.ShapeDtypeStruct((blocks // 2, 3 * thin, width), BF)
    core = (lax.axis_index("pb") % 2).reshape(1).astype(jnp.int32)
    kept, sent = pl.pallas_call(
        functools.partial(attention_weights_kernel, blocks),
        out_shape=(shape, shape),
        grid_spec=pltpu.PrefetchScalarGridSpec(
            num_scalar_prefetch=1,
            grid=(3,),
            in_specs=[
                pl.BlockSpec(a.shape, lambda i, c: (0, 0), pipeline_mode=ONCE) for a in inputs
            ],
            out_specs=[block, block],
        ),
        compiler_params=pltpu.CompilerParams(vmem_limit_bytes=28 * MIB),
        cost_estimate=cost(5 * h_all.shape[0] * width * width, *inputs, shape),
    )(core, *inputs)
    return BundleSum([(kept, sent)], [(thin, 1)] * 3)


def layer_forward(x_own, h_all, params, layout, signed, passing, following):
    (_, _, w_query, w_key, w_value, *_) = params
    tall, width = x_own.shape
    rows = layout.rows
    scale = (width // HEADS) ** -0.5
    queries = (dense(h_all[:tall], w_query, 1, 0) * scale).astype(BF).reshape(OWN, rows, width)
    keys = dense(h_all, w_key, 1, 0).astype(BF).reshape(-1, rows, width)
    values = dense(h_all, w_value, 1, 0).astype(BF).reshape(-1, rows, width)
    attended, totals = attend_forward(queries, keys, values, layout.tables, signed)
    (attended, totals), passing = lax.optimization_barrier(((attended, totals), passing))
    middle, h2, active, slope, *result = mlp_forward(
        attended.reshape(tall, width), x_own, params, following
    )
    saved = (h_all, queries, keys, values, attended, totals, middle, h2, active, slope)
    return result, saved, passing


def layer_backward(upstream, x_own, params, saved, layout, signed, background, cuts, earlier):
    (norm_gain, _, w_query, w_key, w_value, *_) = params
    h_all, queries, keys, values, attended, totals, middle, h2, active, slope = saved
    tall, width = x_own.shape
    du, dx1, gx, do, gb, sum_du, vectors = mlp_backward(upstream, slope, middle, params)
    mlp_vectors = (vectors[0], vectors[1], sum_du[0], vectors[2])
    sum_mlp = mlp_weights(h2, du, attended.reshape(tall, width), gx, active, gb)
    background.moving.append(sum_mlp)
    sum_vectors = VectorSum(earlier + mlp_vectors) if earlier else None
    if earlier:
        background.moving.append(sum_vectors)
    do = do.reshape(queries.shape)
    outcome = []
    for first, end in zip(cuts, cuts[1:]):
        do = background.tick(do)
        if end > first:
            outcome.append(
                attend_backward(
                    queries, do, attended, totals, keys, values, layout.tables, signed, first, end
                )
            )
            do = together(do, outcome[-1])
    outcome = background.tick(outcome)
    dqs, dks, dvs = ([p.reshape(-1, p.shape[-1]) for p in parts] for parts in zip(*outcome))
    dq, dk, dv = (jnp.concatenate(parts, axis=-1) for parts in (dqs, dks, dvs))
    from_keys = (dense(dk, w_key, 1, 1) + dense(dv, w_value, 1, 1)).astype(BF)
    (dqs, dks, dvs), from_keys = lax.optimization_barrier(((dqs, dks, dvs), from_keys))
    from_keys = from_keys.reshape(layout.members, tall, width)
    given = [member_send(from_keys[e], e) for e in range(1, layout.members)]
    dh = dense(dq, w_query, 1, 1) + from_keys[0].astype(F32)
    sum_att = attention_weights(h_all, dqs, dks, dvs)
    background.moving.append(sum_att)
    for part in given:
        dh = dh + part.astype(F32)
    dx, grad_norm_gain, grad_norm_bias = norm_backward(x_own.astype(F32), norm_gain, dh)
    norm_vectors = (grad_norm_gain, grad_norm_bias)

    def finish(mlp, norm):
        up, out, down = sum_mlp.matrices()
        query, key, value = sum_att.matrices()
        return (
            norm[0], norm[1], query, key, value, out,
            mlp[0], mlp[1], up, mlp[2], down, mlp[3],
        )

    return dx1 + dx, mlp_vectors, norm_vectors, sum_vectors, finish


def per_device(tokens, sequence_ids, sequence_offsets, *rest):
    signed_params, plain_params, cotangent = rest[:12], rest[12:24], rest[24]
    tall, width = tokens.shape
    layout = Layout(sequence_ids, sequence_offsets)
    tokens, layout.keys_under_way = lax.optimization_barrier((tokens, layout.keys_under_way))
    rows = layout.rows
    background = Background()
    x_all = layout.arrived(layout.send_in(tokens)).reshape(-1, rows, width)
    layout.settle()
    x_held = rows_at(x_all, layout.held_piece).reshape(-1, width)
    cotangent = layout.send_in(together(cotangent, x_held))
    h_all = layer_norm(x_held.astype(F32), signed_params[0], signed_params[1])
    x_own = x_held[:tall]
    (between, h_own), signed_saved, cotangent = layer_forward(
        x_own, h_all, signed_params, layout, True, cotangent, plain_params[:2]
    )
    h_all = share_with_group(h_own, layout.members)
    upstream = layout.arrived(cotangent).reshape(-1, rows, width)
    (final,), plain_saved, upstream = layer_forward(
        between, h_all, plain_params, layout, False, upstream, None
    )
    output = ScatterOut(final.reshape(OWN, rows, width), layout)
    background.moving.append(output)
    upstream = rows_at(upstream, layout.held_piece[:OWN]).reshape(tall, width)
    groups = attention_sizes(width)[2]
    upstream, mlp_plain, norm_plain, _, finish_plain = layer_backward(
        upstream, between, plain_params, plain_saved, layout, False, background,
        (0, max(1, groups * 2 // 3), groups), (),
    )
    upstream = background.tick(upstream)
    upstream, _, norm_signed, early, finish_signed = layer_backward(
        upstream, x_own, signed_params, signed_saved, layout, True, background,
        tuple(range(groups + 1)), mlp_plain + norm_plain,
    )
    upstream = background.tick(upstream)
    back = ScatterOut(upstream.astype(BF).reshape(OWN, rows, width), layout)
    late = VectorSum(norm_signed)
    background.moving += [back, late]
    background.tick(())
    background.drain()
    early, late = early.parts(), late.parts()
    return (
        (output.result, back.result.astype(F32))
        + finish_signed(early[6:], late)
        + finish_plain(early[:4], early[4:6])
    )


def solution(mesh):
    rows, block = P(("pb", "ka"), None), P("pb", "ka")
    grads = (P(), P(), block, block, block, block, P(), P(), block, P(), block, P())
    return jax.shard_map(
        per_device,
        mesh=mesh,
        in_specs=(rows, P(("pb", "ka")), P(("pb", "ka"))) + (P(),) * 24 + (rows,),
        out_specs=(rows, rows) + grads + grads,
        check_vma=False,
    )
```

time: 1100 us -> 734 us (0.67)
  matrix products: 218 us -> 34.5 us
  waiting for transfers between devices: 213 us -> 114 us
  other arithmetic: 104 us -> 41.2 us
  Pallas kernels: 318 us -> 270 us
  starting transfers between devices: 125 us -> 166 us
  between operations: 24.9 us -> 11.1 us
    dot_general x36 -> x12, matrix products: 218 us -> 34.5 us  [dense(): lax.dot_general(left, right, (((left_axis,), (right_axis,)), ((), ())), p...]
    pallas_call x0 -> x17, Pallas kernels: none -> 150 us  [the longest x2 51.4 us: mlp_forward(): pl.pallas_call(functools.partial(mlp_kernel, following is not None), out_...]
    pallas_call x2 -> x5, Pallas kernels: 183 us -> 75.5 us  [attend_backward(): pl.pallas_call(functools.partial(backward_kernel, head, count, signed), o...]
    pallas_call x2, Pallas kernels: 135 us -> 43.8 us  [attend_forward(): pl.pallas_call(functools.partial(forward_kernel, head, count, signed), ou...]
    ppermute x51 -> x12, waiting for transfers between devices: 127 us -> 60.2 us  [shift_send(): lax.ppermute(array, 'ka', [(i, (i + shift) % size) for i in range(size)])]
    ppermute x59 -> x49, starting transfers between devices: 45.4 us -> 112 us  [xor_send(): return lax.ppermute(array, axis, [(i, i ^ bit) for i in range(size)])]
    ppermute x51 -> x12, starting transfers between devices: 79.9 us -> 19.9 us  [shift_send(): lax.ppermute(array, 'ka', [(i, (i + shift) % size) for i in range(size)])]
    ppermute x0 -> x20, starting transfers between devices: none -> 34.3 us  [the longest x12 22.5 us: send_in(): parts.append(lax.ppermute(part, ('pb', 'ka'), self.round_pairs(turn)))]
  transfers between devices with their start and end apart: 110 -> 81, of which waited for: 45 -> 18; matrix products, arithmetic and copies ran while one was open for 27% -> 12% of each run, Pallas kernels for 15% -> 17%
where the time goes in v2:
time: 734 us; the launch traced here: 729 us
  Pallas kernels  270 us (37%)
  starting transfers between devices  166 us (23%)
  waiting for transfers between devices  114 us (16%)
  local copies, waits for them, and re-layouts  92.4 us (13%)
  other arithmetic  41.2 us (6%)
  matrix products  34.5 us (5%)
  between operations  11.1 us (2%)
    ppermute x49, starting transfers between devices, xor_send(): return lax.ppermute(array, axis, [(i, i ^ bit) for i in range(size)])  112 us
    pallas_call x5, Pallas kernels, attend_backward(): pl.pallas_call(functools.partial(backward_kernel, head, count, signed), o...  75.5 us
    ppermute x12, waiting for transfers between devices, shift_send(): lax.ppermute(array, 'ka', [(i, (i + shift) % size) for i in range(size)])  60.2 us
    ppermute x49, waiting for transfers between devices, xor_send(): return lax.ppermute(array, axis, [(i, i ^ bit) for i in range(size)])  53.8 us
    unnamed x264, local copies, waits for them, and re-layouts  53.6 us
    pallas_call x2, Pallas kernels, mlp_forward(): pl.pallas_call(functools.partial(mlp_kernel, following is not None), out_...  51.4 us
    pallas_call x2, Pallas kernels, attend_forward(): pl.pallas_call(functools.partial(forward_kernel, head, count, signed), ou...  43.8 us
    pallas_call x2, Pallas kernels, mlp_backward(): pl.pallas_call(mlp_back_kernel, out_shape=out_shape, grid=(hidden // widt...  38.7 us
  transfers between devices with their start and end apart: 81, of which 18 were waited for; matrix products, arithmetic and copies ran while one was open for 12% of the time, Pallas kernels for 17%

profile of v2, /device:TPU:0, one launch (start us, length us, event | category | flops | bytes accessed | tf_op | source)
XLA Modules:
  0.0 729.3 jit_solution(18303197517757199936)
XLA Ops:
  35.1 23.6 %collective-permute-start.12 = (bf16[256,768]{1,0:T(8,128)(2,1)}, bf16[256,768]{1,0:T(8,128)(2,1)S(1)}, u32[]{:S(2)}, u32[]{:S(2)}) collective-permute-start(bf16[256,768]{1,0:T(8,128)(2,1)} %collective-permute-done.8), channel_id=1, source_target_pairs={{0,4},{4,0},{8,12},{12,8},{16,20},{20,16},{24,28},{28,24},{1,5},{5... | collective-permute-start | bytes 1179656 | tf_op jit(solution)/shard_map/ppermute | solution.py:302
  89.5 25.1 %shard_map.468 = (bf16[4,256,768]{2,1,0:T(8,128)(2,1)S(1)}, f32[12,4,256]{2,1,0:T(4,128)S(1)}) custom-call(s32[8]{0:T(128)S(1)} %copy-done.74, s32[8]{0:T(128)S(1)} %copy-done.73, bf16[4,256,768]{2,1,0:T(8,128)(2,1)S(1)} %bitcast.209, bf16[8,256,768]{2,1,0:T(8,128)(2,1)S(1)} %bitcast.195, bf16[8,256,768]{2,1,0:T(8,128)(2,1)S(1)} %bitcast.191), custom_call_target="tpu_custom_call" | custom-call | flops 49999998976 | bytes 20000000 | tf_op jit(solution)/shard_map/pallas_call | solution.py:156
  116.8 26.2 %shard_map.469 = (f32[1024,768]{1,0:T(8,128)S(1)}, bf16[1024,768]{1,0:T(8,128)(2,1)S(1)}, bf16[1024,3072]{1,0:T(8,128)(2,1)}, bf16[1024,3072]{1,0:T(8,128)(2,1)}...) custom-call(bf16[1024,768]{1,0:T(8,128)(2,1)S(1)} %bitcast.213, bf16[1024,768]{1,0:T(8,128)(2,1)S(1)} %bitcast.179, ...), custom_call_target="tpu_custom_call" | custom-call | flops 10871635968 | bytes 35796480 | tf_op jit(solution)/shard_map/pallas_call | solution.py:777
  159.3 18.8 %shard_map.470 = (bf16[4,256,768]{2,1,0:T(8,128)(2,1)S(1)}, f32[12,4,256]{2,1,0:T(4,128)S(1)}) custom-call(s32[8]{0:T(128)S(1)} %copy-done.74, s32[8]{0:T(128)S(1)} %copy-done.73, bf16[4,256,768]{2,1,0:T(8,128)(2,1)S(1)} %bitcast.218, bf16[8,256,768]{2,1,0:T(8,128)(2,1)S(1)} %bitcast.202, bf16[8,256,768]{2,1,0:T(8,128)(2,1)S(1)} %bitcast.199), custom_call_target="tpu_custom_call" | custom-call | flops 49999998976 | bytes 20000000 | tf_op jit(solution)/shard_map/pallas_call | solution.py:156
  188.7 25.2 %shard_map.471 = (f32[1024,768]{1,0:T(8,128)S(1)}, bf16[1024,768]{1,0:T(8,128)(2,1)S(1)}, bf16[1024,3072]{1,0:T(8,128)(2,1)}, bf16[1024,3072]{1,0:T(8,128)(2,1)}, bf16[1024,768]{1,0:T(8,128)(2,1)}) custom-call(bf16[1024,768]{1,0:T(8,128)(2,1)S(1)} %bitcast.221, f32[1024,768]{1,0:T(8,128)S(1)} %copy-done.2, bf16[768,768]{1,0:T(8,128)(2,1)S(1)} %copy-done.32, ...), custom_call_target="tpu_custom_call" | custom-call | flops 10871635968 | bytes 34223616 | tf_op jit(solution)/shard_map/pallas_call | solution.py:777
  213.9 18.7 %shard_map.472 = (bf16[1024,3072]{1,0:T(8,128)(2,1)}, f32[1024,768]{1,0:T(8,128)S(1)}, bf16[1024,768]{1,0:T(8,128)(2,1)S(1)}, bf16[1024,768]{1,0:T(8,128)(2,1)S(...) custom-call(bf16[1024,768]{1,0:T(8,128)(2,1)S(1)} %bitcast.184, ...), custom_call_target="tpu_custom_call" | custom-call | flops 10871635968 | bytes 35805696 | tf_op jit(solution)/shard_map/pallas_call | solution.py:849
  234.4 18.7 %shard_map.473 = (bf16[4,480,768]{2,1,0:T(8,128)(2,1)S(1)}, bf16[4,480,768]{2,1,0:T(8,128)(2,1)}, bf16[4,1,384,768]{3,2,1,0:T(8,128)(2,1)S(1)}, bf16[4,1,384,768]{3,2,1,0:T(8,128)(2,1)}) custom-call(s32[1]{0:T(128)} %bitcast.4.me.core, bf16[1024,768]{1,0:T(8,128)(2,1)S(1)} %get-tuple-element.331.h2_ref, bf16[1024,3072]{1,0:T(8,128)(2,1)} %get-tuple-element.332.du_ref, ...), custom_call_target="tpu_custom_call" | custom-call | flops 10871635968 | bytes 24182784 | tf_op jit(solution)/shard_map/pallas_call | solution.py:922
  277.2 29.0 %collective-permute-start.30 = (bf16[2,1,1,480,768]{4,3,2,1,0:T(8,128)(2,1)S(1)}, bf16[2,1,1,480,768]{4,3,2,1,0:T(8,128)(2,1)S(1)}, u32[]{:S(2)}, u32[]{:S(2)}) collective-permute-start(bf16[2,1,1,480,768]{4,3,2,1,0:T(8,128)(2,1)S(1)} %get-tuple-element.356), channel_id=1, source_target_pairs={{0,8},{4,12},{8,0},{12,4},{16,24},{20,28},{24,16},{28,20},{1,9},{5... | collective-permute-start | bytes 4423688 | tf_op jit(solution)/shard_map/ppermute | solution.py:302
  306.2 21.1 %shard_map.474 = (bf16[4,256,512]{2,1,0:T(8,128)(2,1)S(1)}, bf16[8,256,512]{2,1,0:T(8,128)(2,1)S(1)}, bf16[8,256,512]{2,1,0:T(8,128)(2,1)S(1)}) custom-call(s32[8]{0:T(128)S(1)} %copy-done.75, s32[8]{0:T(128)S(1)} %copy-done.73, bf16[4,256,768]{2,1,0:T(8,128)(2,1)S(1)} %bitcast.219, bf16[4,256,768]{2,1,0:T(8,128)(2,1)S(1)} %bitcast.223, ...), custom_call_target="tpu_custom_call" | custom-call | flops 49999998976 | bytes 10000000 | tf_op jit(solution)/shard_map/pallas_call | solution.py:266
  327.7 8.7 %collective-permute-done.30 = bf16[2,1,1,480,768]{4,3,2,1,0:T(8,128)(2,1)S(1)} collective-permute-done((bf16[2,1,1,480,768]{4,3,2,1,0:T(8,128)(2,1)S(1)}, bf16[2,1,1,480,768]{4,3,2,1,0:T(8,128)(2,1)S(1)}, u32[]{:S(2)}, u32[]{:S(2)}) %collective-permute-start.30) | collective-permute-done | bytes 1474592 | tf_op jit(solution)/shard_map/ppermute | solution.py:302
  349.5 10.6 %shard_map.475 = (bf16[4,256,256]{2,1,0:T(8,128)(2,1)S(1)}, bf16[8,256,256]{2,1,0:T(8,128)(2,1)S(1)}, bf16[8,256,256]{2,1,0:T(8,128)(2,1)S(1)}) custom-call(s32[8]{0:T(128)S(1)} %copy-done.75, s32[8]{0:T(128)S(1)} %copy-done.73, bf16[4,256,768]{2,1,0:T(8,128)(2,1)S(1)} %bitcast.220, bf16[4,256,768]{2,1,0:T(8,128)(2,1)S(1)} %bitcast.224, ...), custom_call_target="tpu_custom_call" | custom-call | flops 24999999488 | bytes 10000000 | tf_op jit(solution)/shard_map/pallas_call | solution.py:266
  394.5 7.4 %shard_map.477 = (bf16[4,288,768]{2,1,0:T(8,128)(2,1)S(1)}, bf16[4,288,768]{2,1,0:T(8,128)(2,1)S(1)}) custom-call(s32[1]{0:T(128)} %bitcast.4.me.core, bf16[2048,768]{1,0:T(8,128)(2,1)S(1)} %copy-done.17, bf16[1024,512]{1,0:T(8,128)(2,1)S(1)} %bitcast.229, bf16[1024,256]{1,0:T(8,128)(2,1)S(1)} %bitcast.247, bf16[2048,512]{1,0:T(8,128)(2,1)S(1)} %bitcast.206, ...), custom_call_target="tpu_custom_call" | custom-call | flops 6039797760 | bytes 12779520 | tf_op jit(solution)/shard_map/pallas_call | solution.py:970
  414.6 13.3 %collective-permute-done.38.refs_2_ = bf16[432,384]{1,0:T(8,128)(2,1)S(1)} collective-permute-done((bf16[432,384]{1,0:T(8,128)(2,1)S(1)}, bf16[432,384]{1,0:T(8,128)(2,1)S(1)}, u32[]{:S(2)}, u32[]{:S(2)}) %collective-permute-start.38) | collective-permute-done | bytes 331808 | tf_op jit(solution)/shard_map/ppermute | solution.py:307
  430.2 20.0 %shard_map.478 = (bf16[1024,3072]{1,0:T(8,128)(2,1)}, f32[1024,768]{1,0:T(8,128)S(1)}, bf16[1024,768]{1,0:T(8,128)(2,1)S(1)}, bf16[1024,768]{1,0:T(8,128)(2,1)S(...) custom-call(f32[1024,768]{1,0:T(8,128)S(1)} %multiply_add_fusion.1.g_ref, ...), custom_call_target="tpu_custom_call" | custom-call | flops 10871635968 | bytes 37378560 | tf_op jit(solution)/shard_map/pallas_call | solution.py:849
  451.8 18.2 %shard_map.479 = (bf16[4,480,768]{2,1,0:T(8,128)(2,1)S(1)}, bf16[4,480,768]{2,1,0:T(8,128)(2,1)}, bf16[4,1,384,768]{3,2,1,0:T(8,128)(2,1)S(1)}, bf16[4,1,384,768]{3,2,1,0:T(8,128)(2,1)}) custom-call(s32[1]{0:T(128)} %bitcast.4.me.core, bf16[1024,768]{1,0:T(8,128)(2,1)S(1)} %copy-done.79, bf16[1024,3072]{1,0:T(8,128)(2,1)} %get-tuple-element.432.du_ref, ...), custom_call_target="tpu_custom_call" | custom-call | flops 10871635968 | bytes 24182784 | tf_op jit(solution)/shard_map/pallas_call | solution.py:922
  490.2 7.2 collective-permute-start.45
  513.6 14.6 %shard_map.480 = (bf16[4,256,256]{2,1,0:T(8,128)(2,1)S(1)}, bf16[8,256,256]{2,1,0:T(8,128)(2,1)S(1)}, bf16[8,256,256]{2,1,0:T(8,128)(2,1)S(1)}) custom-call(s32[8]{0:T(128)S(1)} %copy-done.76, s32[8]{0:T(128)S(1)} %copy-done.73, bf16[4,256,768]{2,1,0:T(8,128)(2,1)S(1)} %bitcast.210, bf16[4,256,768]{2,1,0:T(8,128)(2,1)S(1)} %bitcast.215, ...), custom_call_target="tpu_custom_call" | custom-call | flops 24999999488 | bytes 10000000 | tf_op jit(solution)/shard_map/pallas_call | solution.py:266
  528.4 12.0 %collective-permute-done.49 = bf16[1,2,1,384,768]{4,3,2,1,0:T(8,128)(2,1)S(1)} collective-permute-done((bf16[1,2,1,384,768]{4,3,2,1,0:T(8,128)(2,1)S(1)}, bf16[1,2,1,384,768]{4,3,2,1,0:T(8,128)(2,1)S(1)}, u32[]{:S(2)}, u32[]{:S(2)}) %collective-permute-start.49) | collective-permute-done | bytes 1179680 | tf_op jit(solution)/shard_map/ppermute | solution.py:302
  540.8 6.7 collective-permute-done.48
  555.5 14.6 %shard_map.482 = (bf16[4,256,256]{2,1,0:T(8,128)(2,1)S(1)}, bf16[8,256,256]{2,1,0:T(8,128)(2,1)S(1)}, bf16[8,256,256]{2,1,0:T(8,128)(2,1)S(1)}) custom-call(s32[8]{0:T(128)S(1)} %copy-done.76, s32[8]{0:T(128)S(1)} %copy-done.73, bf16[4,256,768]{2,1,0:T(8,128)(2,1)S(1)} %bitcast.211, bf16[4,256,768]{2,1,0:T(8,128)(2,1)S(1)} %bitcast.216, ...), custom_call_target="tpu_custom_call" | custom-call | flops 24999999488 | bytes 10000000 | tf_op jit(solution)/shard_map/pallas_call | solution.py:266
  573.2 9.7 %collective-permute-start.60 = (f32[96,128]{1,0:T(8,128)S(1)}, f32[96,128]{1,0:T(8,128)S(1)}, u32[]{:S(2)}, u32[]{:S(2)}) collective-permute-start(f32[96,128]{1,0:T(8,128)S(1)} %add.490), channel_id=1, source_target_pairs={{0,8},{4,12},{8,0},{12,4},{16,24},{20,28},{24,16},{28,20},{1,9},{5... | collective-permute-start | bytes 147464 | tf_op jit(solution)/shard_map/ppermute | solution.py:302
  586.9 14.6 %shard_map.484 = (bf16[4,256,256]{2,1,0:T(8,128)(2,1)S(1)}, bf16[8,256,256]{2,1,0:T(8,128)(2,1)S(1)}, bf16[8,256,256]{2,1,0:T(8,128)(2,1)S(1)}) custom-call(s32[8]{0:T(128)S(1)} %copy-done.76, s32[8]{0:T(128)S(1)} %copy-done.73, bf16[4,256,768]{2,1,0:T(8,128)(2,1)S(1)} %bitcast.212, bf16[4,256,768]{2,1,0:T(8,128)(2,1)S(1)} %bitcast.217, ...), custom_call_target="tpu_custom_call" | custom-call | flops 24999999488 | bytes 10000000 | tf_op jit(solution)/shard_map/pallas_call | solution.py:266
  617.0 7.6 %shard_map.485 = (bf16[4,288,768]{2,1,0:T(8,128)(2,1)S(1)}, bf16[4,288,768]{2,1,0:T(8,128)(2,1)S(1)}) custom-call(s32[1]{0:T(128)} %bitcast.4.me.core, bf16[2048,768]{1,0:T(8,128)(2,1)S(1)} %copy-done.7, bf16[1024,256]{1,0:T(8,128)(2,1)S(1)} %bitcast.243, bf16[1024,256]{1,0:T(8,128)(2,1)S(1)} %bitcast.245, bf16[1024,256]{1,0:T(8,128)(2,1)S(1)} %bitcast.249, ...), custom_call_target="tpu_custom_call" | custom-call | flops 6039797760 | bytes 12779520 | tf_op jit(solution)/shard_map/pallas_call | solution.py:970
  681.5 35.5 %collective-permute-done.79.refs_2_ = bf16[144,384]{1,0:T(8,128)(2,1)S(1)} collective-permute-done((bf16[144,384]{1,0:T(8,128)(2,1)S(1)}, bf16[144,384]{1,0:T(8,128)(2,1)S(1)}, u32[]{:S(2)}, u32[]{:S(2)}) %collective-permute-start.79) | collective-permute-done | bytes 110624 | tf_op jit(solution)/shard_map/ppermute | solution.py:307
  (560 shorter events, 311.1 us)
Async XLA Ops:
  11.4 103.4 %collective-permute-start.19 = (bf16[256,768]{1,0:T(8,128)(2,1)}, bf16[256,768]{1,0:T(8,128)(2,1)S(1)}, u32[]{:S(2)}, u32[]{:S(2)}) collective-permute-start(bf16[256,768]{1,0:T(8,128)(2,1)} %get-tuple-element.694), channel_id=1, source_target_pairs={{0,5},{1,4},{2,1},{3,0},{4,7},{5,6},{6,3},{7,2},{8,13},{9,12},{10,... | collective-permute-start | bytes 1179656 | tf_op jit(solution)/shard_map/ppermute | solution.py:429
  20.1 40.4 %collective-permute-start.11 = (bf16[256,768]{1,0:T(8,128)(2,1)}, bf16[256,768]{1,0:T(8,128)(2,1)S(1)}, u32[]{:S(2)}, u32[]{:S(2)}) collective-permute-start(bf16[256,768]{1,0:T(8,128)(2,1)} %get-tuple-element.698), channel_id=1, source_target_pairs={{0,5},{1,4},{2,1},{3,0},{4,7},{5,6},{6,3},{7,2},{8,13},{9,12},{10,... | collective-permute-start | bytes 1179656 | tf_op jit(solution)/shard_map/ppermute | solution.py:429
  20.1 40.4 %collective-permute-start.10 = (bf16[256,768]{1,0:T(8,128)(2,1)}, bf16[256,768]{1,0:T(8,128)(2,1)S(1)}, u32[]{:S(2)}, u32[]{:S(2)}) collective-permute-start(bf16[256,768]{1,0:T(8,128)(2,1)} %get-tuple-element.699), channel_id=1, source_target_pairs={{0,4},{1,5},{2,0},{3,1},{4,6},{5,7},{6,2},{7,3},{8,12},{9,13},{10,... | collective-permute-start | bytes 1179656 | tf_op jit(solution)/shard_map/ppermute | solution.py:429
  20.6 40.5 %collective-permute-start.9 = (bf16[256,768]{1,0:T(8,128)(2,1)}, bf16[256,768]{1,0:T(8,128)(2,1)S(1)}, u32[]{:S(2)}, u32[]{:S(2)}) collective-permute-start(bf16[256,768]{1,0:T(8,128)(2,1)} %get-tuple-element.700), channel_id=1, source_target_pairs={{0,1},{1,0},{2,5},{3,4},{4,3},{5,2},{6,7},{7,6},{8,9},{9,8},{10,13... | collective-permute-start | bytes 1179656 | tf_op jit(solution)/shard_map/ppermute | solution.py:429
  35.1 28.3 %collective-permute-start.12 = (bf16[256,768]{1,0:T(8,128)(2,1)}, bf16[256,768]{1,0:T(8,128)(2,1)S(1)}, u32[]{:S(2)}, u32[]{:S(2)}) collective-permute-start(bf16[256,768]{1,0:T(8,128)(2,1)} %collective-permute-done.8), channel_id=1, source_target_pairs={{0,4},{4,0},{8,12},{12,8},{16,20},{20,16},{24,28},{28,24},{1,5},{5... | collective-permute-start | bytes 1179656 | tf_op jit(solution)/shard_map/ppermute | solution.py:302
  63.4 51.4 %collective-permute-start.18 = (bf16[256,768]{1,0:T(8,128)(2,1)}, bf16[256,768]{1,0:T(8,128)(2,1)}, u32[]{:S(2)}, u32[]{:S(2)}) collective-permute-start(bf16[256,768]{1,0:T(8,128)(2,1)} %get-tuple-element.695), channel_id=1, source_target_pairs={{0,4},{1,5},{2,0},{3,1},{4,6},{5,7},{6,2},{7,3},{8,12},{9,13},{10,... | collective-permute-start | bytes 1179656 | tf_op jit(solution)/shard_map/ppermute | solution.py:429
  64.6 50.2 %collective-permute-start.17 = (bf16[256,768]{1,0:T(8,128)(2,1)}, bf16[256,768]{1,0:T(8,128)(2,1)}, u32[]{:S(2)}, u32[]{:S(2)}) collective-permute-start(bf16[256,768]{1,0:T(8,128)(2,1)} %get-tuple-element.696), channel_id=1, source_target_pairs={{0,1},{1,0},{2,5},{3,4},{4,3},{5,2},{6,7},{7,6},{8,9},{9,8},{10,13... | collective-permute-start | bytes 1179656 | tf_op jit(solution)/shard_map/ppermute | solution.py:429
  65.4 49.4 %collective-permute-start.16 = (bf16[256,768]{1,0:T(8,128)(2,1)}, bf16[256,768]{1,0:T(8,128)(2,1)}, u32[]{:S(2)}, u32[]{:S(2)}) collective-permute-start(bf16[256,768]{1,0:T(8,128)(2,1)} %get-tuple-element.697), channel_id=1, source_target_pairs={{0,0},{1,1},{2,4},{3,5},{4,2},{5,3},{6,6},{7,7},{8,8},{9,9},{10,12... | collective-permute-start | bytes 1179656 | tf_op jit(solution)/shard_map/ppermute | solution.py:429
  274.0 62.9 %collective-permute-start.28 = (bf16[256,768]{1,0:T(8,128)(2,1)S(1)}, bf16[256,768]{1,0:T(8,128)(2,1)S(1)}, u32[]{:S(2)}, u32[]{:S(2)}) collective-permute-start(bf16[256,768]{1,0:T(8,128)(2,1)S(1)} %get-tuple-element.351), channel_id=1, source_target_pairs={{0,0},{1,1},{4,2},{5,3},{2,4},{3,5},{6,6},{7,7},{8,8},{9,9},{12,10... | collective-permute-start | bytes 1179656 | tf_op jit(solution)/shard_map/ppermute | solution.py:474
  274.8 62.0 %collective-permute-start.29 = (bf16[256,768]{1,0:T(8,128)(2,1)S(1)}, bf16[256,768]{1,0:T(8,128)(2,1)S(1)}, u32[]{:S(2)}, u32[]{:S(2)}) collective-permute-start(bf16[256,768]{1,0:T(8,128)(2,1)S(1)} %get-tuple-element.352), channel_id=1, source_target_pairs={{1,0},{0,1},{5,2},{4,3},{3,4},{2,5},{7,6},{6,7},{9,8},{8,9},{13,10... | collective-permute-start | bytes 1179656 | tf_op jit(solution)/shard_map/ppermute | solution.py:474
  275.6 51.7 %collective-permute-start.31 = (bf16[1,2,1,384,768]{4,3,2,1,0:T(8,128)(2,1)S(1)}, bf16[1,2,1,384,768]{4,3,2,1,0:T(8,128)(2,1)S(1)}, u32[]{:S(2)}, u32[]{:S(2)}) collective-permute-start(bf16[1,2,1,384,768]{4,3,2,1,0:T(8,128)(2,1)S(1)} %get-tuple-element.358), channel_id=1, source_target_pairs={{0,16},{4,20},{8,24},{12,28},{16,0},{20,4},{24,8},{28,12},{1,17},{... | collective-permute-start | bytes 3538952 | tf_op jit(solution)/shard_map/ppermute | solution.py:302
  277.2 59.2 %collective-permute-start.30 = (bf16[2,1,1,480,768]{4,3,2,1,0:T(8,128)(2,1)S(1)}, bf16[2,1,1,480,768]{4,3,2,1,0:T(8,128)(2,1)S(1)}, u32[]{:S(2)}, u32[]{:S(2)}) collective-permute-start(bf16[2,1,1,480,768]{4,3,2,1,0:T(8,128)(2,1)S(1)} %get-tuple-element.356), channel_id=1, source_target_pairs={{0,8},{4,12},{8,0},{12,4},{16,24},{20,28},{24,16},{28,20},{1,9},{5... | collective-permute-start | bytes 4423688 | tf_op jit(solution)/shard_map/ppermute | solution.py:302
  337.0 29.6 %collective-permute-start.32 = (bf16[256,768]{1,0:T(8,128)(2,1)S(1)}, bf16[256,768]{1,0:T(8,128)(2,1)S(1)}, u32[]{:S(2)}, u32[]{:S(2)}) collective-permute-start(bf16[256,768]{1,0:T(8,128)(2,1)S(1)} %get-tuple-element.372), channel_id=1, source_target_pairs={{4,0},{5,1},{0,2},{1,3},{6,4},{7,5},{2,6},{3,7},{12,8},{13,9},{8,1... | collective-permute-start | bytes 1179656 | tf_op jit(solution)/shard_map/ppermute | solution.py:474
  340.5 26.2 %collective-permute-start.33 = (bf16[256,768]{1,0:T(8,128)(2,1)S(1)}, bf16[256,768]{1,0:T(8,128)(2,1)S(1)}, u32[]{:S(2)}, u32[]{:S(2)}) collective-permute-start(bf16[256,768]{1,0:T(8,128)(2,1)S(1)} %get-tuple-element.373), channel_id=1, source_target_pairs={{5,0},{4,1},{1,2},{0,3},{7,4},{6,5},{3,6},{2,7},{13,8},{12,9},{9,1... | collective-permute-start | bytes 1179656 | tf_op jit(solution)/shard_map/ppermute | solution.py:474
  471.7 33.2 %collective-permute-start.43 = (bf16[4,480,768]{2,1,0:T(8,128)(2,1)}, bf16[4,480,768]{2,1,0:T(8,128)(2,1)}, u32[]{:S(2)}, u32[]{:S(2)}) collective-permute-start(bf16[4,480,768]{2,1,0:T(8,128)(2,1)} %get-tuple-element.437), channel_id=1, source_target_pairs={{0,4},{4,0},{8,12},{12,8},{16,20},{20,16},{24,28},{28,24},{1,5},{5... | collective-permute-start | bytes 8847368 | tf_op jit(solution)/shard_map/ppermute | solution.py:302
  471.7 31.0 %collective-permute-start.44 = (bf16[4,384,768]{2,1,0:T(8,128)(2,1)}, bf16[4,384,768]{2,1,0:T(8,128)(2,1)}, u32[]{:S(2)}, u32[]{:S(2)}) collective-permute-start(bf16[4,384,768]{2,1,0:T(8,128)(2,1)} %bitcast.65), channel_id=1, source_target_pairs={{0,4},{4,0},{8,12},{12,8},{16,20},{20,16},{24,28},{28,24},{1,5},{5... | collective-permute-start | bytes 7077896 | tf_op jit(solution)/shard_map/ppermute | solution.py:302
  510.7 29.8 %collective-permute-start.49 = (bf16[1,2,1,384,768]{4,3,2,1,0:T(8,128)(2,1)S(1)}, bf16[1,2,1,384,768]{4,3,2,1,0:T(8,128)(2,1)S(1)}, u32[]{:S(2)}, u32[]{:S(2)}) collective-permute-start(bf16[1,2,1,384,768]{4,3,2,1,0:T(8,128)(2,1)S(1)} %get-tuple-element.463), channel_id=1, source_target_pairs={{0,16},{4,20},{8,24},{12,28},{16,0},{20,4},{24,8},{28,12},{1,17},{... | collective-permute-start | bytes 3538952 | tf_op jit(solution)/shard_map/ppermute | solution.py:302
  512.1 35.4 %collective-permute-start.48 = (bf16[2,1,1,480,768]{4,3,2,1,0:T(8,128)(2,1)S(1)}, bf16[2,1,1,480,768]{4,3,2,1,0:T(8,128)(2,1)S(1)}, u32[]{:S(2)}, u32[]{:S(2)}) collective-permute-start(bf16[2,1,1,480,768]{4,3,2,1,0:T(8,128)(2,1)S(1)} %get-tuple-element.461), channel_id=1, source_target_pairs={{0,8},{4,12},{8,0},{12,4},{16,24},{20,28},{24,16},{28,20},{1,9},{5... | collective-permute-start | bytes 4423688 | tf_op jit(solution)/shard_map/ppermute | solution.py:302
  573.2 28.3 %collective-permute-start.60 = (f32[96,128]{1,0:T(8,128)S(1)}, f32[96,128]{1,0:T(8,128)S(1)}, u32[]{:S(2)}, u32[]{:S(2)}) collective-permute-start(f32[96,128]{1,0:T(8,128)S(1)} %add.490), channel_id=1, source_target_pairs={{0,8},{4,12},{8,0},{12,4},{16,24},{20,28},{24,16},{28,20},{1,9},{5... | collective-permute-start | bytes 147464 | tf_op jit(solution)/shard_map/ppermute | solution.py:302
  674.7 48.8 %collective-permute-start.68 = (bf16[256,768]{1,0:T(8,128)(2,1)}, bf16[256,768]{1,0:T(8,128)(2,1)S(1)}, u32[]{:S(2)}, u32[]{:S(2)}) collective-permute-start(bf16[256,768]{1,0:T(8,128)(2,1)} %get-tuple-element.544), channel_id=1, source_target_pairs={{0,0},{1,1},{4,2},{5,3},{2,4},{3,5},{6,6},{7,7},{8,8},{9,9},{12,10... | collective-permute-start | bytes 1179656 | tf_op jit(solution)/shard_map/ppermute | solution.py:474
  676.4 47.2 %collective-permute-start.69 = (bf16[256,768]{1,0:T(8,128)(2,1)}, bf16[256,768]{1,0:T(8,128)(2,1)S(1)}, u32[]{:S(2)}, u32[]{:S(2)}) collective-permute-start(bf16[256,768]{1,0:T(8,128)(2,1)} %get-tuple-element.545), channel_id=1, source_target_pairs={{1,0},{0,1},{5,2},{4,3},{3,4},{2,5},{7,6},{6,7},{9,8},{8,9},{13,10... | collective-permute-start | bytes 1179656 | tf_op jit(solution)/shard_map/ppermute | solution.py:474
  676.4 47.2 %collective-permute-start.70 = (bf16[256,768]{1,0:T(8,128)(2,1)}, bf16[256,768]{1,0:T(8,128)(2,1)S(1)}, u32[]{:S(2)}, u32[]{:S(2)}) collective-permute-start(bf16[256,768]{1,0:T(8,128)(2,1)} %get-tuple-element.546), channel_id=1, source_target_pairs={{4,0},{5,1},{0,2},{1,3},{6,4},{7,5},{2,6},{3,7},{12,8},{13,9},{8,1... | collective-permute-start | bytes 1179656 | tf_op jit(solution)/shard_map/ppermute | solution.py:474
  678.3 45.3 %collective-permute-start.71 = (bf16[256,768]{1,0:T(8,128)(2,1)}, bf16[256,768]{1,0:T(8,128)(2,1)S(1)}, u32[]{:S(2)}, u32[]{:S(2)}) collective-permute-start(bf16[256,768]{1,0:T(8,128)(2,1)} %get-tuple-element.547), channel_id=1, source_target_pairs={{5,0},{4,1},{1,2},{0,3},{7,4},{6,5},{3,6},{2,7},{13,8},{12,9},{9,1... | collective-permute-start | bytes 1179656 | tf_op jit(solution)/shard_map/ppermute | solution.py:474
  680.3 36.8 %collective-permute-start.79 = (bf16[144,384]{1,0:T(8,128)(2,1)S(1)}, bf16[144,384]{1,0:T(8,128)(2,1)S(1)}, u32[]{:S(2)}, u32[]{:S(2)}) collective-permute-start(bf16[144,384]{1,0:T(8,128)(2,1)S(1)} %get-tuple-element.555), channel_id=1, source_target_pairs={{0,2},{1,3},{2,0},{3,1},{4,6},{5,7},{6,4},{7,5},{8,10},{9,11},{10,... | collective-permute-start | bytes 331784 | tf_op jit(solution)/shard_map/ppermute | solution.py:307
  (174 other events, 2228.4 us)

commit v3 on v2

--- a/solution.py
+++ b/solution.py
@@ -302,11 +302,6 @@
     return lax.ppermute(array, axis, [(i, i ^ bit) for i in range(size)])
 
 
-def shift_send(array, shift):
-    size = lax.axis_size("ka")
-    return lax.ppermute(array, "ka", [(i, (i + shift) % size) for i in range(size)])
-
-
 def pick(array, index, axis=0):
     return lax.dynamic_index_in_dim(array, index, axis, keepdims=False)
 
@@ -498,14 +493,36 @@
         return rows_at(jnp.stack(got), jnp.stack(order)).reshape(-1, got[0].shape[-1])
 
 
+def stack_kernel(*refs):
+    out, at = refs[-1], 0
+    width = out.shape[1]
+    for ref in refs[:-1]:
+        for row in range(ref.shape[0]):
+            for left in range(0, ref.shape[1], width):
+                out[at : at + 1, :] = ref[row : row + 1, left : left + width]
+                at += 1
+
+
+def stack_rows(arrays):
+    width = min(a.shape[1] for a in arrays)
+    height = sum(a.size for a in arrays) // width
+    vmem = pl.BlockSpec(memory_space=pltpu.VMEM)
+    return pl.pallas_call(
+        stack_kernel,
+        out_shape=jax.ShapeDtypeStruct((height, width), F32),
+        in_specs=[vmem] * len(arrays),
+        out_specs=vmem,
+        compiler_params=pltpu.CompilerParams(vmem_limit_bytes=4 * MIB),
+    )(*arrays)
+
+
 class VectorSum(Moving):
-    def __init__(self, vectors):
-        self.sizes = [v.shape[0] for v in vectors]
+    def __init__(self, arrays):
         self.steps = []
         for axis in ("ka", "pb"):
             bits = lax.axis_size(axis).bit_length() - 1
             self.steps += [(axis, 1 << b) for b in range(bits)]
-        self.advance(jnp.concatenate(vectors).reshape(-1, 128))
+        self.result = stack_rows(arrays)
 
     def prepare(self, flat):
         self.now = self.steps.pop(0) if self.steps else None
@@ -514,26 +531,19 @@
     def launch(self, flat):
         self.result = flat + xor_send(flat, *self.now) if self.now else flat
 
-    def parts(self):
-        flat, at, result = self.result.reshape(-1), 0, []
-        for size in self.sizes:
-            result.append(flat[at : at + size])
-            at += size
-        return result
-
 
 class BundleSum(Moving):
-    def __init__(self, arrays, segments):
+    def __init__(self, arrays, segments, at_once=False):
         self.along_pb, self.along_ka = lax.axis_size("pb"), lax.axis_size("ka")
         self.bits = self.along_pb.bit_length() - 1
         rest = list(range(1, self.bits))
-        self.steps = list(zip(rest, rest[::-1])) + ["ka"]
+        self.steps = ["core"] + list(zip(rest, rest[::-1]))
+        self.steps += ["columns"] + list(range(1, self.along_ka.bit_length() - 1))
         self.narrow = arrays[0][0].shape[-1]
         self.segments = segments
-        self.result = []
-        for kept, sent in arrays:
-            total = kept + xor_send(sent, "pb", 1)
-            self.result.append(total.reshape((2,) * (self.bits - 1) + (1,) + kept.shape[1:]))
+        self.result = arrays
+        if at_once:
+            self.advance(arrays)
 
     def split(self, view, bit):
         axis = self.bits - 1 - bit
@@ -542,36 +552,47 @@
         return kept, lax.dynamic_slice_in_dim(view, 1 - own, 1, axis)
 
     def prepare(self, views):
-        self.now = self.steps.pop(0) if self.steps else None
-        if not self.now:
+        self.now = step = self.steps.pop(0) if self.steps else None
+        if step is None or step == "core":
             return views
-        if self.now != "ka":
+        if isinstance(step, tuple):
             if len(views) == 1:
                 half = views[0].shape[-2] // 2
                 views = [views[0][..., :half, :], views[0][..., half:, :]]
-            return [self.split(view, bit) for view, bit in zip(views, self.now)]
-        return split_columns(
-            [v.reshape(-1, self.narrow) for v in views], self.segments, self.along_ka
-        )
+            return [self.split(view, bit) for view, bit in zip(views, step)]
+        if step == "columns":
+            return split_columns(
+                [v.reshape(-1, self.narrow) for v in views], self.segments, self.along_ka
+            )
+        own = (lax.axis_index("ka") >> step) & 1
+        pairs = views.reshape((-1, 2) + views.shape[1:])
+        return pick(pairs, own, 1), pick(pairs, 1 - own, 1)
 
     def launch(self, made):
-        if not self.now:
+        step = self.now
+        if step is None:
             self.result = made
-        elif self.now != "ka":
+        elif step == "core":
+            shape = (2,) * (self.bits - 1) + (1,)
             self.result = [
-                kept + xor_send(sent, "pb", 1 << bit)
-                for (kept, sent), bit in zip(made, self.now)
+                (kept + xor_send(sent, "pb", 1)).reshape(shape + kept.shape[1:])
+                for kept, sent in made
+            ]
+        elif isinstance(step, tuple):
+            self.result = [
+                kept + xor_send(sent, "pb", 1 << bit) for (kept, sent), bit in zip(made, step)
             ]
         else:
-            got = [shift_send(sent, shift) for shift, sent in enumerate(made[1:], 1)]
-            self.result = [made[0]] + got
+            kept, sent = made
+            got = xor_send(sent, "ka", 1 if step == "columns" else 1 << step)
+            self.result = kept + got if self.steps else [kept[0], got[0]]
 
     def matrices(self):
         return join_columns(self.result, self.segments, self.narrow, self.along_ka)
 
 
 def split_kernel(segments, ways, z, *refs):
-    views, outs, whole = refs[:-ways - 1], refs[-ways - 1 : -1], refs[-1]
+    views, (kept, sent, whole) = refs[:-3], refs[-3:]
     at = 0
     for view in views:
         whole[at : at + view.shape[0], :] = view[...]
@@ -591,33 +612,35 @@
         rows = jnp.concatenate(pieces, axis=0)
         half = rows.shape[0] // 2
         block = jnp.concatenate([rows[:half], rows[half:]], axis=1)
-        for shift in range(ways):
-
-            @pl.when((z[0] + shift) % ways == target)
-            def _():
-                outs[shift][...] = block
+        mine = z[0] % 2 == target % 2
+
+        @pl.when(mine)
+        def _():
+            kept[target // 2] = block
+
+        @pl.when(jnp.logical_not(mine))
+        def _():
+            sent[target // 2] = block
 
 
 def split_columns(views, segments, ways):
     narrow = views[0].shape[1]
     height = sum(v.shape[0] for v in views)
-    shape = jax.ShapeDtypeStruct((height // 2, 2 * narrow // ways), BF)
+    shape = jax.ShapeDtypeStruct((ways // 2, height // 2, 2 * narrow // ways), BF)
     vmem = pl.BlockSpec(memory_space=pltpu.VMEM)
     return pl.pallas_call(
         functools.partial(split_kernel, segments, ways),
-        out_shape=[shape] * ways,
+        out_shape=[shape] * 2,
         in_specs=[pl.BlockSpec(memory_space=pltpu.SMEM)] + [vmem] * len(views),
-        out_specs=[vmem] * ways,
+        out_specs=[vmem] * 2,
         scratch_shapes=[pltpu.VMEM((height, narrow), BF)],
         compiler_params=pltpu.CompilerParams(vmem_limit_bytes=16 * MIB),
     )(lax.axis_index("ka").reshape(1).astype(jnp.int32), *views)
 
 
 def join_kernel(segments, narrow, ways, *refs):
-    parts, outs = refs[:ways], refs[ways:]
-    total = parts[0][...].astype(F32)
-    for part in parts[1:]:
-        total = total + part[...].astype(F32)
+    outs = refs[2:]
+    total = refs[0][...].astype(F32) + refs[1][...].astype(F32)
     thin = narrow // ways
     rows = jnp.concatenate([total[:, :thin], total[:, thin:]], axis=0)
     at = 0
@@ -633,7 +656,7 @@
     return pl.pallas_call(
         functools.partial(join_kernel, segments, narrow, ways),
         out_shape=[jax.ShapeDtypeStruct((height, thin * folds), F32) for height, folds in segments],
-        in_specs=[vmem] * ways,
+        in_specs=[vmem] * 2,
         out_specs=[vmem] * len(segments),
         compiler_params=pltpu.CompilerParams(vmem_limit_bytes=16 * MIB),
     )(*parts)
@@ -673,12 +696,11 @@
 
 def norm_backward(values, gain, upstream):
     n, scale = normalized(values)
-    grad_gain = jnp.sum(upstream * n, axis=0)
-    grad_shift = jnp.sum(upstream, axis=0)
+    vectors = jnp.sum(jnp.stack([upstream * n, upstream]), axis=1)
     dn = upstream * gain.astype(F32)
     mean = jnp.mean(dn, axis=-1, keepdims=True)
     along = jnp.mean(dn * n, axis=-1, keepdims=True)
-    return scale * (dn - mean - n * along), grad_gain, grad_shift
+    return scale * (dn - mean - n * along), vectors
 
 
 def gelu_pair(u):
@@ -723,12 +745,14 @@
             acc[t] = jnp.zeros_like(x1)
 
     up_bias = ub_ref[...].astype(F32)
-    for t in tiles:
-        u = dot(h2_ref[t], wu_ref[...]) + up_bias
-        active, slope = gelu_pair(u)
-        active = active.astype(BF)
-        a_ref[t] = active
+    hidden = [dot(h2_ref[t], wu_ref[...]) for t in tiles]
+    actives = []
+    for t, u in zip(tiles, hidden):
+        active, slope = gelu_pair(u + up_bias)
+        actives.append(active.astype(BF))
+        a_ref[t] = actives[-1]
         s_ref[t] = slope.astype(BF)
+    for t, active in zip(tiles, actives):
         acc[t] += dot(active, wd_ref[...])
 
     @pl.when(step == pl.num_programs(0) - 1)
@@ -800,8 +824,8 @@
             acc[t] = jnp.zeros(acc[t].shape, F32)
 
     total = 0.0
-    for t in tiles:
-        da = dot(gb_ref[t], wd_ref[...], NT)
+    products = [dot(gb_ref[t], wd_ref[...], NT) for t in tiles]
+    for t, da in zip(tiles, products):
         du = (da * slope_ref[t].astype(F32)).astype(BF)
         du_ref[t] = du
         total = total + jnp.sum(du.astype(F32), axis=0, keepdims=True)
@@ -981,7 +1005,7 @@
         compiler_params=pltpu.CompilerParams(vmem_limit_bytes=28 * MIB),
         cost_estimate=cost(5 * h_all.shape[0] * width * width, *inputs, shape),
     )(core, *inputs)
-    return BundleSum([(kept, sent)], [(thin, 1)] * 3)
+    return BundleSum([(kept, sent)], [(thin, 1)] * 3, at_once=True)
 
 
 def layer_forward(x_own, h_all, params, layout, signed, passing, following):
@@ -1006,7 +1030,9 @@
     h_all, queries, keys, values, attended, totals, middle, h2, active, slope = saved
     tall, width = x_own.shape
     du, dx1, gx, do, gb, sum_du, vectors = mlp_backward(upstream, slope, middle, params)
-    mlp_vectors = (vectors[0], vectors[1], sum_du[0], vectors[2])
+    mlp_vectors = [vectors, sum_du]
+    if earlier:
+        du, gx, do, gb = background.tick((du, gx, do, gb))
     sum_mlp = mlp_weights(h2, du, attended.reshape(tall, width), gx, active, gb)
     background.moving.append(sum_mlp)
     sum_vectors = VectorSum(earlier + mlp_vectors) if earlier else None
@@ -1035,15 +1061,14 @@
     background.moving.append(sum_att)
     for part in given:
         dh = dh + part.astype(F32)
-    dx, grad_norm_gain, grad_norm_bias = norm_backward(x_own.astype(F32), norm_gain, dh)
-    norm_vectors = (grad_norm_gain, grad_norm_bias)
+    dx, norm_vectors = norm_backward(x_own.astype(F32), norm_gain, dh)
 
     def finish(mlp, norm):
         up, out, down = sum_mlp.matrices()
         query, key, value = sum_att.matrices()
         return (
             norm[0], norm[1], query, key, value, out,
-            mlp[0], mlp[1], up, mlp[2], down, mlp[3],
+            mlp[0], mlp[1], up, mlp[3:].reshape(-1), down, mlp[2],
         )
 
     return dx1 + dx, mlp_vectors, norm_vectors, sum_vectors, finish
@@ -1076,24 +1101,28 @@
     groups = attention_sizes(width)[2]
     upstream, mlp_plain, norm_plain, _, finish_plain = layer_backward(
         upstream, between, plain_params, plain_saved, layout, False, background,
-        (0, max(1, groups * 2 // 3), groups), (),
+        (0, groups // 3, groups), [],
     )
     upstream = background.tick(upstream)
     upstream, _, norm_signed, early, finish_signed = layer_backward(
         upstream, x_own, signed_params, signed_saved, layout, True, background,
-        tuple(range(groups + 1)), mlp_plain + norm_plain,
+        tuple(range(groups + 1)), mlp_plain + [norm_plain],
     )
     upstream = background.tick(upstream)
     back = ScatterOut(upstream.astype(BF).reshape(OWN, rows, width), layout)
-    late = VectorSum(norm_signed)
+    late = VectorSum([norm_signed])
+    for _ in range(2):
+        late.advance(late.result)
     background.moving += [back, late]
     background.tick(())
+    background.tick(())
     background.drain()
-    early, late = early.parts(), late.parts()
+    count = signed_params[8].shape[1] // width + 3
+    early, late = early.result, late.result
     return (
         (output.result, back.result.astype(F32))
-        + finish_signed(early[6:], late)
-        + finish_plain(early[:4], early[4:6])
+        + finish_signed(early[count + 2 :], late)
+        + finish_plain(early[:count], early[count : count + 2])
     )
 
 

time: 734 us -> 669 us (0.911)
  waiting for transfers between devices: 114 us -> 40.7 us
  Pallas kernels: 270 us -> 340 us
  starting transfers between devices: 166 us -> 102 us
    ppermute x12 -> x0, waiting for transfers between devices: 60.2 us -> none  [shift_send(): lax.ppermute(array, 'ka', [(i, (i + shift) % size) for i in range(size)])]
    ppermute x49 -> x57, starting transfers between devices: 112 us -> 61.6 us  [xor_send(): return lax.ppermute(array, axis, [(i, i ^ bit) for i in range(size)])]
    pallas_call x5, Pallas kernels: 75.5 us -> 125 us  [attend_backward(): pl.pallas_call(functools.partial(backward_kernel, head, count, signed), o...]
    pallas_call x2, Pallas kernels: 43.8 us -> 71.6 us  [attend_forward(): pl.pallas_call(functools.partial(forward_kernel, head, count, signed), ou...]
    ppermute x12 -> x0, starting transfers between devices: 19.9 us -> none  [shift_send(): lax.ppermute(array, 'ka', [(i, (i + shift) % size) for i in range(size)])]
    ppermute x49 -> x57, waiting for transfers between devices: 53.8 us -> 40.7 us  [xor_send(): return lax.ppermute(array, axis, [(i, i ^ bit) for i in range(size)])]
    ppermute x8, starting transfers between devices: 11.8 us -> 20.4 us  [send(): lax.ppermute(part, ('pb', 'ka'), [(b, a) for a, b in self.layout.round_pa...]
    unnamed x264 -> x277, local copies, waits for them, and re-layouts: 53.6 us -> 51.7 us
  transfers between devices with their start and end apart: 81 -> 77, of which waited for: 18 -> 8; matrix products, arithmetic and copies ran while one was open for 12% -> 11% of each run, Pallas kernels for 17% -> 39%
where the time goes in v3:
time: 669 us; the launch traced here: 661 us
  Pallas kernels  340 us (51%)
  starting transfers between devices  102 us (15%)
  local copies, waits for them, and re-layouts  90.6 us (14%)
  waiting for transfers between devices  40.7 us (6%)
  other arithmetic  40.6 us (6%)
  matrix products  36 us (5%)
  between operations  11.3 us (2%)
    pallas_call x5, Pallas kernels, attend_backward(): pl.pallas_call(functools.partial(backward_kernel, head, count, signed), o...  125 us
    pallas_call x2, Pallas kernels, attend_forward(): pl.pallas_call(functools.partial(forward_kernel, head, count, signed), ou...  71.6 us
    ppermute x57, starting transfers between devices, xor_send(): return lax.ppermute(array, axis, [(i, i ^ bit) for i in range(size)])  61.6 us
    unnamed x277, local copies, waits for them, and re-layouts  51.7 us
    pallas_call x2, Pallas kernels, mlp_forward(): pl.pallas_call(functools.partial(mlp_kernel, following is not None), out_...  47.8 us
    ppermute x57, waiting for transfers between devices, xor_send(): return lax.ppermute(array, axis, [(i, i ^ bit) for i in range(size)])  40.7 us
    pallas_call x2, Pallas kernels, mlp_backward(): pl.pallas_call(mlp_back_kernel, out_shape=out_shape, grid=(hidden // widt...  37.5 us
    dot_general x12, matrix products, dense(): lax.dot_general(left, right, (((left_axis,), (right_axis,)), ((), ())), p...  36 us
  transfers between devices with their start and end apart: 77, of which 8 were waited for; matrix products, arithmetic and copies ran while one was open for 11% of the time, Pallas kernels for 39%

profile of v3, /device:TPU:0, one launch (start us, length us, event | category | flops | bytes accessed | tf_op | source)
XLA Modules:
  0.0 661.2 jit_solution(17723573459190290535)
XLA Ops:
  23.5 5.5 concatenate.55.keys
  41.4 17.3 %collective-permute-start.12 = (bf16[256,768]{1,0:T(8,128)(2,1)S(1)}, bf16[256,768]{1,0:T(8,128)(2,1)S(1)}, u32[]{:S(2)}, u32[]{:S(2)}) collective-permute-start(bf16[256,768]{1,0:T(8,128)(2,1)S(1)} %collective-permute-done.8), channel_id=1, source_target_pairs={{0,4},{4,0},{8,12},{12,8},{16,20},{20,16},{24,28},{28,24},{1,5},{5... | collective-permute-start | bytes 1179656 | tf_op jit(solution)/shard_map/ppermute | solution.py:302
  88.4 41.5 %shard_map.468 = (bf16[4,256,768]{2,1,0:T(8,128)(2,1)S(1)}, f32[12,4,256]{2,1,0:T(4,128)S(1)}) custom-call(s32[8]{0:T(128)S(1)} %copy-done.70, s32[8]{0:T(128)S(1)} %copy-done.69, bf16[4,256,768]{2,1,0:T(8,128)(2,1)S(1)} %bitcast.202, bf16[8,256,768]{2,1,0:T(8,128)(2,1)S(1)} %bitcast.188, bf16[8,256,768]{2,1,0:T(8,128)(2,1)S(1)} %bitcast.184), custom_call_target="tpu_custom_call" | custom-call | flops 49999998976 | bytes 20000000 | tf_op jit(solution)/shard_map/pallas_call | solution.py:156
  132.1 24.0 %shard_map.469 = (f32[1024,768]{1,0:T(8,128)S(1)}, bf16[1024,768]{1,0:T(8,128)(2,1)S(1)}, bf16[1024,3072]{1,0:T(8,128)(2,1)}, bf16[1024,3072]{1,0:T(8,128)(2,1)}...) custom-call(bf16[1024,768]{1,0:T(8,128)(2,1)S(1)} %bitcast.206, bf16[1024,768]{1,0:T(8,128)(2,1)S(1)} %bitcast.160, ...), custom_call_target="tpu_custom_call" | custom-call | flops 10871635968 | bytes 35796480 | tf_op jit(solution)/shard_map/pallas_call | solution.py:801
  172.4 30.2 %shard_map.470 = (bf16[4,256,768]{2,1,0:T(8,128)(2,1)S(1)}, f32[12,4,256]{2,1,0:T(4,128)S(1)}) custom-call(s32[8]{0:T(128)S(1)} %copy-done.70, s32[8]{0:T(128)S(1)} %copy-done.69, bf16[4,256,768]{2,1,0:T(8,128)(2,1)S(1)} %bitcast.211, bf16[8,256,768]{2,1,0:T(8,128)(2,1)S(1)} %bitcast.195, bf16[8,256,768]{2,1,0:T(8,128)(2,1)S(1)} %bitcast.192), custom_call_target="tpu_custom_call" | custom-call | flops 49999998976 | bytes 20000000 | tf_op jit(solution)/shard_map/pallas_call | solution.py:156
  202.7 23.8 %shard_map.471 = (f32[1024,768]{1,0:T(8,128)S(1)}, bf16[1024,768]{1,0:T(8,128)(2,1)S(1)}, bf16[1024,3072]{1,0:T(8,128)(2,1)}, bf16[1024,3072]{1,0:T(8,128)(2,1)}, bf16[1024,768]{1,0:T(8,128)(2,1)}) custom-call(bf16[1024,768]{1,0:T(8,128)(2,1)S(1)} %bitcast.214, f32[1024,768]{1,0:T(8,128)S(1)} %get-tuple-element.362.x_ref, bf16[768,768]{1,0:T(8,128)(2,1)S(1)} %copy-done.18, ...), custom_call_target="tpu_custom_call" | custom-call | flops 10871635968 | bytes 34223616 | tf_op jit(solution)/shard_map/pallas_call | solution.py:801
  235.0 18.0 %shard_map.472 = (bf16[1024,3072]{1,0:T(8,128)(2,1)}, f32[1024,768]{1,0:T(8,128)S(1)}, bf16[1024,768]{1,0:T(8,128)(2,1)S(1)}, bf16[1024,768]{1,0:T(8,128)(2,1)S(...) custom-call(bf16[1024,768]{1,0:T(8,128)(2,1)S(1)} %bitcast.167, ...), custom_call_target="tpu_custom_call" | custom-call | flops 10871635968 | bytes 35805696 | tf_op jit(solution)/shard_map/pallas_call | solution.py:873
  255.4 18.3 %shard_map.473 = (bf16[4,480,768]{2,1,0:T(8,128)(2,1)S(1)}, bf16[4,480,768]{2,1,0:T(8,128)(2,1)}, bf16[4,1,384,768]{3,2,1,0:T(8,128)(2,1)S(1)}, bf16[4,1,384,768]{3,2,1,0:T(8,128)(2,1)}) custom-call(s32[1]{0:T(128)} %bitcast.4.me.core, bf16[1024,768]{1,0:T(8,128)(2,1)S(1)} %copy-done.83, bf16[1024,3072]{1,0:T(8,128)(2,1)} %get-tuple-element.369.du_ref, ...), custom_call_target="tpu_custom_call" | custom-call | flops 10871635968 | bytes 24182784 | tf_op jit(solution)/shard_map/pallas_call | solution.py:946
  290.9 17.3 %shard_map.474 = (bf16[4,256,256]{2,1,0:T(8,128)(2,1)S(1)}, bf16[8,256,256]{2,1,0:T(8,128)(2,1)S(1)}, bf16[8,256,256]{2,1,0:T(8,128)(2,1)S(1)}) custom-call(s32[8]{0:T(128)S(1)} %copy-done.71, s32[8]{0:T(128)S(1)} %copy-done.69, bf16[4,256,768]{2,1,0:T(8,128)(2,1)S(1)} %bitcast.212, bf16[4,256,768]{2,1,0:T(8,128)(2,1)S(1)} %bitcast.216, ...), custom_call_target="tpu_custom_call" | custom-call | flops 24999999488 | bytes 10000000 | tf_op jit(solution)/shard_map/pallas_call | solution.py:266
  321.8 34.3 %shard_map.475 = (bf16[4,256,512]{2,1,0:T(8,128)(2,1)S(1)}, bf16[8,256,512]{2,1,0:T(8,128)(2,1)S(1)}, bf16[8,256,512]{2,1,0:T(8,128)(2,1)S(1)}) custom-call(s32[8]{0:T(128)S(1)} %copy-done.72, s32[8]{0:T(128)S(1)} %copy-done.69, bf16[4,256,768]{2,1,0:T(8,128)(2,1)S(1)} %bitcast.213, bf16[4,256,768]{2,1,0:T(8,128)(2,1)S(1)} %bitcast.217, ...), custom_call_target="tpu_custom_call" | custom-call | flops 49999998976 | bytes 10000000 | tf_op jit(solution)/shard_map/pallas_call | solution.py:266
  385.7 7.8 %shard_map.476 = (bf16[4,288,768]{2,1,0:T(8,128)(2,1)S(1)}, bf16[4,288,768]{2,1,0:T(8,128)(2,1)S(1)}) custom-call(s32[1]{0:T(128)} %bitcast.4.me.core, bf16[2048,768]{1,0:T(8,128)(2,1)S(1)} %copy-done.13, bf16[1024,256]{1,0:T(8,128)(2,1)S(1)} %bitcast.238, bf16[1024,512]{1,0:T(8,128)(2,1)S(1)} %bitcast.226, bf16[2048,256]{1,0:T(8,128)(2,1)S(1)} %bitcast.223, ...), custom_call_target="tpu_custom_call" | custom-call | flops 6039797760 | bytes 12779520 | tf_op jit(solution)/shard_map/pallas_call | solution.py:994
  405.6 19.4 %shard_map.478 = (bf16[1024,3072]{1,0:T(8,128)(2,1)}, f32[1024,768]{1,0:T(8,128)S(1)}, bf16[1024,768]{1,0:T(8,128)(2,1)S(1)}, bf16[1024,768]{1,0:T(8,128)(2,1)S(...) custom-call(f32[1024,768]{1,0:T(8,128)S(1)} %get-tuple-element.457.g_ref, ...), custom_call_target="tpu_custom_call" | custom-call | flops 10871635968 | bytes 37378560 | tf_op jit(solution)/shard_map/pallas_call | solution.py:873
  432.6 17.0 %shard_map.479 = (bf16[4,480,768]{2,1,0:T(8,128)(2,1)S(1)}, bf16[4,480,768]{2,1,0:T(8,128)(2,1)S(1)}, bf16[4,1,384,768]{3,2,1,0:T(8,128)(2,1)S(1)}, bf16[4,1,384,768]{3,2,1,0:T(8,128)(2,1)S(1)}) custom-call(s32[1]{0:T(128)} %bitcast.4.me.core, bf16[1024,768]{1,0:T(8,128)(2,1)S(1)} %copy-done.81, bf16[1024,3072]{1,0:T(8,128)(2,1)} %get-tuple-element.486.du_ref, ...), custom_call_target="tpu_custom_call" | custom-call | flops 10871635968 | bytes 24182784 | tf_op jit(solution)/shard_map/pallas_call | solution.py:946
  454.2 24.8 %shard_map.482 = (bf16[4,256,256]{2,1,0:T(8,128)(2,1)S(1)}, bf16[8,256,256]{2,1,0:T(8,128)(2,1)S(1)}, bf16[8,256,256]{2,1,0:T(8,128)(2,1)S(1)}) custom-call(s32[8]{0:T(128)S(1)} %copy-done.72, s32[8]{0:T(128)S(1)} %copy-done.69, bf16[4,256,768]{2,1,0:T(8,128)(2,1)S(1)} %bitcast.203, bf16[4,256,768]{2,1,0:T(8,128)(2,1)S(1)} %bitcast.208, ...), custom_call_target="tpu_custom_call" | custom-call | flops 24999999488 | bytes 10000000 | tf_op jit(solution)/shard_map/pallas_call | solution.py:266
  486.2 24.4 %shard_map.483 = (bf16[4,256,256]{2,1,0:T(8,128)(2,1)S(1)}, bf16[8,256,256]{2,1,0:T(8,128)(2,1)S(1)}, bf16[8,256,256]{2,1,0:T(8,128)(2,1)S(1)}) custom-call(s32[8]{0:T(128)S(1)} %copy-done.72, s32[8]{0:T(128)S(1)} %copy-done.69, bf16[4,256,768]{2,1,0:T(8,128)(2,1)S(1)} %bitcast.204, bf16[4,256,768]{2,1,0:T(8,128)(2,1)S(1)} %bitcast.209, ...), custom_call_target="tpu_custom_call" | custom-call | flops 24999999488 | bytes 10000000 | tf_op jit(solution)/shard_map/pallas_call | solution.py:266
  513.3 6.0 collective-permute-done.49
  522.4 24.4 %shard_map.484 = (bf16[4,256,256]{2,1,0:T(8,128)(2,1)S(1)}, bf16[8,256,256]{2,1,0:T(8,128)(2,1)S(1)}, bf16[8,256,256]{2,1,0:T(8,128)(2,1)S(1)}) custom-call(s32[8]{0:T(128)S(1)} %copy-done.72, s32[8]{0:T(128)S(1)} %copy-done.69, bf16[4,256,768]{2,1,0:T(8,128)(2,1)S(1)} %bitcast.205, bf16[4,256,768]{2,1,0:T(8,128)(2,1)S(1)} %bitcast.210, ...), custom_call_target="tpu_custom_call" | custom-call | flops 24999999488 | bytes 10000000 | tf_op jit(solution)/shard_map/pallas_call | solution.py:266
  552.8 5.0 add_convert_fusion
  560.9 7.5 %shard_map.486 = (bf16[4,288,768]{2,1,0:T(8,128)(2,1)S(1)}, bf16[4,288,768]{2,1,0:T(8,128)(2,1)S(1)}) custom-call(s32[1]{0:T(128)} %bitcast.4.me.core, bf16[2048,768]{1,0:T(8,128)(2,1)S(1)} %copy-done.9, bf16[1024,256]{1,0:T(8,128)(2,1)S(1)} %bitcast.236, bf16[1024,256]{1,0:T(8,128)(2,1)S(1)} %bitcast.240, bf16[1024,256]{1,0:T(8,128)(2,1)S(1)} %bitcast.242, ...), custom_call_target="tpu_custom_call" | custom-call | flops 6039797760 | bytes 12779520 | tf_op jit(solution)/shard_map/pallas_call | solution.py:994
  568.6 7.7 %collective-permute-done.56 = bf16[2,432,384]{2,1,0:T(8,128)(2,1)S(1)} collective-permute-done((bf16[2,432,384]{2,1,0:T(8,128)(2,1)S(1)}, bf16[2,432,384]{2,1,0:T(8,128)(2,1)S(1)}, u32[]{:S(2)}, u32[]{:S(2)}) %collective-permute-start.56) | collective-permute-done | bytes 663584 | tf_op jit(solution)/shard_map/ppermute | solution.py:302
  587.3 5.3 collective-permute-done.64
  595.1 5.5 collective-permute-done.65
  623.1 10.1 %collective-permute-start.71 = (bf16[256,768]{1,0:T(8,128)(2,1)}, bf16[256,768]{1,0:T(8,128)(2,1)S(1)}, u32[]{:S(2)}, u32[]{:S(2)}) collective-permute-start(bf16[256,768]{1,0:T(8,128)(2,1)} %get-tuple-element.632), channel_id=1, source_target_pairs={{4,0},{5,1},{0,2},{1,3},{6,4},{7,5},{2,6},{3,7},{12,8},{13,9},{8,1... | collective-permute-start | bytes 1179656 | tf_op jit(solution)/shard_map/ppermute | solution.py:469
  642.7 9.9 %collective-permute-done.76 = bf16[1,144,384]{2,1,0:T(8,128)(2,1)S(1)} collective-permute-done((bf16[1,144,384]{2,1,0:T(8,128)(2,1)S(1)}, bf16[1,144,384]{2,1,0:T(8,128)(2,1)S(1)}, u32[]{:S(2)}, u32[]{:S(2)}) %collective-permute-start.76) | collective-permute-done | bytes 110624 | tf_op jit(solution)/shard_map/ppermute | solution.py:302
  (576 shorter events, 245.0 us)
Async XLA Ops:
  11.4 118.6 %collective-permute-start.19 = (bf16[256,768]{1,0:T(8,128)(2,1)}, bf16[256,768]{1,0:T(8,128)(2,1)S(1)}, u32[]{:S(2)}, u32[]{:S(2)}) collective-permute-start(bf16[256,768]{1,0:T(8,128)(2,1)} %get-tuple-element.771), channel_id=1, source_target_pairs={{0,5},{1,4},{2,1},{3,0},{4,7},{5,6},{6,3},{7,2},{8,13},{9,12},{10,... | collective-permute-start | bytes 1179656 | tf_op jit(solution)/shard_map/ppermute | solution.py:424
  20.1 39.3 %collective-permute-start.11 = (bf16[256,768]{1,0:T(8,128)(2,1)}, bf16[256,768]{1,0:T(8,128)(2,1)S(1)}, u32[]{:S(2)}, u32[]{:S(2)}) collective-permute-start(bf16[256,768]{1,0:T(8,128)(2,1)} %get-tuple-element.775), channel_id=1, source_target_pairs={{0,5},{1,4},{2,1},{3,0},{4,7},{5,6},{6,3},{7,2},{8,13},{9,12},{10,... | collective-permute-start | bytes 1179656 | tf_op jit(solution)/shard_map/ppermute | solution.py:424
  20.1 39.3 %collective-permute-start.10 = (bf16[256,768]{1,0:T(8,128)(2,1)}, bf16[256,768]{1,0:T(8,128)(2,1)S(1)}, u32[]{:S(2)}, u32[]{:S(2)}) collective-permute-start(bf16[256,768]{1,0:T(8,128)(2,1)} %get-tuple-element.776), channel_id=1, source_target_pairs={{0,4},{1,5},{2,0},{3,1},{4,6},{5,7},{6,2},{7,3},{8,12},{9,13},{10,... | collective-permute-start | bytes 1179656 | tf_op jit(solution)/shard_map/ppermute | solution.py:424
  20.6 39.4 %collective-permute-start.9 = (bf16[256,768]{1,0:T(8,128)(2,1)}, bf16[256,768]{1,0:T(8,128)(2,1)S(1)}, u32[]{:S(2)}, u32[]{:S(2)}) collective-permute-start(bf16[256,768]{1,0:T(8,128)(2,1)} %get-tuple-element.777), channel_id=1, source_target_pairs={{0,1},{1,0},{2,5},{3,4},{4,3},{5,2},{6,7},{7,6},{8,9},{9,8},{10,13... | collective-permute-start | bytes 1179656 | tf_op jit(solution)/shard_map/ppermute | solution.py:424
  62.3 67.7 %collective-permute-start.18 = (bf16[256,768]{1,0:T(8,128)(2,1)}, bf16[256,768]{1,0:T(8,128)(2,1)}, u32[]{:S(2)}, u32[]{:S(2)}) collective-permute-start(bf16[256,768]{1,0:T(8,128)(2,1)} %get-tuple-element.772), channel_id=1, source_target_pairs={{0,4},{1,5},{2,0},{3,1},{4,6},{5,7},{6,2},{7,3},{8,12},{9,13},{10,... | collective-permute-start | bytes 1179656 | tf_op jit(solution)/shard_map/ppermute | solution.py:424
  63.5 66.5 %collective-permute-start.17 = (bf16[256,768]{1,0:T(8,128)(2,1)}, bf16[256,768]{1,0:T(8,128)(2,1)}, u32[]{:S(2)}, u32[]{:S(2)}) collective-permute-start(bf16[256,768]{1,0:T(8,128)(2,1)} %get-tuple-element.773), channel_id=1, source_target_pairs={{0,1},{1,0},{2,5},{3,4},{4,3},{5,2},{6,7},{7,6},{8,9},{9,8},{10,13... | collective-permute-start | bytes 1179656 | tf_op jit(solution)/shard_map/ppermute | solution.py:424
  64.3 65.7 %collective-permute-start.16 = (bf16[256,768]{1,0:T(8,128)(2,1)}, bf16[256,768]{1,0:T(8,128)(2,1)}, u32[]{:S(2)}, u32[]{:S(2)}) collective-permute-start(bf16[256,768]{1,0:T(8,128)(2,1)} %get-tuple-element.774), channel_id=1, source_target_pairs={{0,0},{1,1},{2,4},{3,5},{4,2},{5,3},{6,6},{7,7},{8,8},{9,9},{10,12... | collective-permute-start | bytes 1179656 | tf_op jit(solution)/shard_map/ppermute | solution.py:424
  229.3 44.3 %collective-permute-start.25 = (bf16[4,256,768]{2,1,0:T(8,128)(2,1)}, bf16[4,256,768]{2,1,0:T(8,128)(2,1)}, u32[]{:S(2)}, u32[]{:S(2)}) collective-permute-start(bf16[4,256,768]{2,1,0:T(8,128)(2,1)} %bitcast.29), channel_id=1, source_target_pairs={{0,4},{4,0},{8,12},{12,8},{16,20},{20,16},{24,28},{28,24},{1,5},{5... | collective-permute-start | bytes 4718600 | tf_op jit(solution)/shard_map/ppermute | solution.py:302
  278.1 33.3 %collective-permute-start.28 = (bf16[4,480,768]{2,1,0:T(8,128)(2,1)}, bf16[4,480,768]{2,1,0:T(8,128)(2,1)}, u32[]{:S(2)}, u32[]{:S(2)}) collective-permute-start(bf16[4,480,768]{2,1,0:T(8,128)(2,1)} %get-tuple-element.395), channel_id=1, source_target_pairs={{0,4},{4,0},{8,12},{12,8},{16,20},{20,16},{24,28},{28,24},{1,5},{5... | collective-permute-start | bytes 8847368 | tf_op jit(solution)/shard_map/ppermute | solution.py:302
  278.6 29.6 %collective-permute-start.29 = (bf16[4,384,768]{2,1,0:T(8,128)(2,1)}, bf16[4,384,768]{2,1,0:T(8,128)(2,1)}, u32[]{:S(2)}, u32[]{:S(2)}) collective-permute-start(bf16[4,384,768]{2,1,0:T(8,128)(2,1)} %bitcast.31), channel_id=1, source_target_pairs={{0,4},{4,0},{8,12},{12,8},{16,20},{20,16},{24,28},{28,24},{1,5},{5... | collective-permute-start | bytes 7077896 | tf_op jit(solution)/shard_map/ppermute | solution.py:302
  278.6 35.7 %collective-permute-start.26 = (bf16[256,768]{1,0:T(8,128)(2,1)}, bf16[256,768]{1,0:T(8,128)(2,1)S(1)}, u32[]{:S(2)}, u32[]{:S(2)}) collective-permute-start(bf16[256,768]{1,0:T(8,128)(2,1)} %get-tuple-element.390), channel_id=1, source_target_pairs={{0,0},{1,1},{4,2},{5,3},{2,4},{3,5},{6,6},{7,7},{8,8},{9,9},{12,10... | collective-permute-start | bytes 1179656 | tf_op jit(solution)/shard_map/ppermute | solution.py:469
  280.2 34.1 %collective-permute-start.27 = (bf16[256,768]{1,0:T(8,128)(2,1)}, bf16[256,768]{1,0:T(8,128)(2,1)S(1)}, u32[]{:S(2)}, u32[]{:S(2)}) collective-permute-start(bf16[256,768]{1,0:T(8,128)(2,1)} %get-tuple-element.391), channel_id=1, source_target_pairs={{1,0},{0,1},{5,2},{4,3},{3,4},{2,5},{7,6},{6,7},{9,8},{8,9},{13,10... | collective-permute-start | bytes 1179656 | tf_op jit(solution)/shard_map/ppermute | solution.py:469
  315.7 42.1 %collective-permute-start.30 = (bf16[256,768]{1,0:T(8,128)(2,1)S(1)}, bf16[256,768]{1,0:T(8,128)(2,1)S(1)}, u32[]{:S(2)}, u32[]{:S(2)}) collective-permute-start(bf16[256,768]{1,0:T(8,128)(2,1)S(1)} %copy-done.98), channel_id=1, source_target_pairs={{4,0},{5,1},{0,2},{1,3},{6,4},{7,5},{2,6},{3,7},{12,8},{13,9},{8,1... | collective-permute-start | bytes 1179656 | tf_op jit(solution)/shard_map/ppermute | solution.py:469
  318.0 39.8 %collective-permute-start.31 = (bf16[256,768]{1,0:T(8,128)(2,1)S(1)}, bf16[256,768]{1,0:T(8,128)(2,1)S(1)}, u32[]{:S(2)}, u32[]{:S(2)}) collective-permute-start(bf16[256,768]{1,0:T(8,128)(2,1)S(1)} %copy-done.97), channel_id=1, source_target_pairs={{5,0},{4,1},{1,2},{0,3},{7,4},{6,5},{3,6},{2,7},{13,8},{12,9},{9,1... | collective-permute-start | bytes 1179656 | tf_op jit(solution)/shard_map/ppermute | solution.py:469
  320.3 35.9 %collective-permute-start.33 = (bf16[1,2,1,384,768]{4,3,2,1,0:T(8,128)(2,1)S(1)}, bf16[1,2,1,384,768]{4,3,2,1,0:T(8,128)(2,1)S(1)}, u32[]{:S(2)}, u32[]{:S(2)}) collective-permute-start(bf16[1,2,1,384,768]{4,3,2,1,0:T(8,128)(2,1)S(1)} %get-tuple-element.416), channel_id=1, source_target_pairs={{0,16},{4,20},{8,24},{12,28},{16,0},{20,4},{24,8},{28,12},{1,17},{... | collective-permute-start | bytes 3538952 | tf_op jit(solution)/shard_map/ppermute | solution.py:302
  321.8 34.7 %collective-permute-start.32 = (bf16[2,1,1,480,768]{4,3,2,1,0:T(8,128)(2,1)S(1)}, bf16[2,1,1,480,768]{4,3,2,1,0:T(8,128)(2,1)S(1)}, u32[]{:S(2)}, u32[]{:S(2)}) collective-permute-start(bf16[2,1,1,480,768]{4,3,2,1,0:T(8,128)(2,1)S(1)} %get-tuple-element.414), channel_id=1, source_target_pairs={{0,8},{4,12},{8,0},{12,4},{16,24},{20,28},{24,16},{28,20},{1,9},{5... | collective-permute-start | bytes 4423688 | tf_op jit(solution)/shard_map/ppermute | solution.py:302
  450.2 29.9 %collective-permute-start.45 = (bf16[4,480,768]{2,1,0:T(8,128)(2,1)S(1)}, bf16[4,480,768]{2,1,0:T(8,128)(2,1)}, u32[]{:S(2)}, u32[]{:S(2)}) collective-permute-start(bf16[4,480,768]{2,1,0:T(8,128)(2,1)S(1)} %get-tuple-element.519), channel_id=1, source_target_pairs={{0,4},{4,0},{8,12},{12,8},{16,20},{20,16},{24,28},{28,24},{1,5},{5... | collective-permute-start | bytes 8847368 | tf_op jit(solution)/shard_map/ppermute | solution.py:302
  450.3 28.9 %collective-permute-start.46 = (bf16[4,384,768]{2,1,0:T(8,128)(2,1)S(1)}, bf16[4,384,768]{2,1,0:T(8,128)(2,1)S(1)}, u32[]{:S(2)}, u32[]{:S(2)}) collective-permute-start(bf16[4,384,768]{2,1,0:T(8,128)(2,1)S(1)} %bitcast.183), channel_id=1, source_target_pairs={{0,4},{4,0},{8,12},{12,8},{16,20},{20,16},{24,28},{28,24},{1,5},{5... | collective-permute-start | bytes 7077896 | tf_op jit(solution)/shard_map/ppermute | solution.py:302
  450.8 28.3 %collective-permute-start.47 = (f32[16,768]{1,0:T(8,128)S(1)}, f32[16,768]{1,0:T(8,128)S(1)}, u32[]{:S(2)}, u32[]{:S(2)}) collective-permute-start(f32[16,768]{1,0:T(8,128)S(1)} %shard_map.480), channel_id=1, source_target_pairs={{0,1},{1,0},{2,3},{3,2},{4,5},{5,4},{6,7},{7,6},{8,9},{9,8},{10,11... | collective-permute-start | bytes 147464 | tf_op jit(solution)/shard_map/ppermute | solution.py:302
  451.2 27.9 %collective-permute-start.44 = (bf16[2,144,384]{2,1,0:T(8,128)(2,1)S(1)}, bf16[2,144,384]{2,1,0:T(8,128)(2,1)S(1)}, u32[]{:S(2)}, u32[]{:S(2)}) collective-permute-start(bf16[2,144,384]{2,1,0:T(8,128)(2,1)S(1)} %get-tuple-element.517), channel_id=1, source_target_pairs={{0,1},{1,0},{2,3},{3,2},{4,5},{5,4},{6,7},{7,6},{8,9},{9,8},{10,11... | collective-permute-start | bytes 663560 | tf_op jit(solution)/shard_map/ppermute | solution.py:302
  483.2 27.4 %collective-permute-start.51 = (f32[16,768]{1,0:T(8,128)S(1)}, f32[16,768]{1,0:T(8,128)S(1)}, u32[]{:S(2)}, u32[]{:S(2)}) collective-permute-start(f32[16,768]{1,0:T(8,128)S(1)} %add.515), channel_id=1, source_target_pairs={{0,2},{1,3},{2,0},{3,1},{4,6},{5,7},{6,4},{7,5},{8,10},{9,11},{10,... | collective-permute-start | bytes 147464 | tf_op jit(solution)/shard_map/ppermute | solution.py:302
  484.4 35.3 %collective-permute-start.48 = (bf16[1,144,384]{2,1,0:T(8,128)(2,1)S(1)}, bf16[1,144,384]{2,1,0:T(8,128)(2,1)S(1)}, u32[]{:S(2)}, u32[]{:S(2)}) collective-permute-start(bf16[1,144,384]{2,1,0:T(8,128)(2,1)S(1)} %get-tuple-element.534), channel_id=1, source_target_pairs={{0,2},{1,3},{2,0},{3,1},{4,6},{5,7},{6,4},{7,5},{8,10},{9,11},{10,... | collective-permute-start | bytes 331784 | tf_op jit(solution)/shard_map/ppermute | solution.py:302
  486.2 33.1 %collective-permute-start.49 = (bf16[2,1,1,480,768]{4,3,2,1,0:T(8,128)(2,1)S(1)}, bf16[2,1,1,480,768]{4,3,2,1,0:T(8,128)(2,1)S(1)}, u32[]{:S(2)}, u32[]{:S(2)}) collective-permute-start(bf16[2,1,1,480,768]{4,3,2,1,0:T(8,128)(2,1)S(1)} %get-tuple-element.536), channel_id=1, source_target_pairs={{0,8},{4,12},{8,0},{12,4},{16,24},{20,28},{24,16},{28,20},{1,9},{5... | collective-permute-start | bytes 4423688 | tf_op jit(solution)/shard_map/ppermute | solution.py:302
  623.1 30.3 %collective-permute-start.71 = (bf16[256,768]{1,0:T(8,128)(2,1)}, bf16[256,768]{1,0:T(8,128)(2,1)S(1)}, u32[]{:S(2)}, u32[]{:S(2)}) collective-permute-start(bf16[256,768]{1,0:T(8,128)(2,1)} %get-tuple-element.632), channel_id=1, source_target_pairs={{4,0},{5,1},{0,2},{1,3},{6,4},{7,5},{2,6},{3,7},{12,8},{13,9},{8,1... | collective-permute-start | bytes 1179656 | tf_op jit(solution)/shard_map/ppermute | solution.py:469
  (181 other events, 2223.3 us)

commit v4 on v3

--- a/solution.py
+++ b/solution.py
@@ -310,10 +310,6 @@
     return array.at[index].get(mode="promise_in_bounds")
 
 
-def together(value, *others):
-    return lax.optimization_barrier((value,) + others)[0]
-
-
 def member_send(array, offset):
     if offset & 1:
         array = xor_send(array, "pb", 1)
@@ -1048,7 +1044,7 @@
                     queries, do, attended, totals, keys, values, layout.tables, signed, first, end
                 )
             )
-            do = together(do, outcome[-1])
+            do, outcome[-1] = lax.optimization_barrier((do, outcome[-1]))
     outcome = background.tick(outcome)
     dqs, dks, dvs = ([p.reshape(-1, p.shape[-1]) for p in parts] for parts in zip(*outcome))
     dq, dk, dv = (jnp.concatenate(parts, axis=-1) for parts in (dqs, dks, dvs))
@@ -1084,7 +1080,8 @@
     x_all = layout.arrived(layout.send_in(tokens)).reshape(-1, rows, width)
     layout.settle()
     x_held = rows_at(x_all, layout.held_piece).reshape(-1, width)
-    cotangent = layout.send_in(together(cotangent, x_held))
+    cotangent, x_held = lax.optimization_barrier((cotangent, x_held))
+    cotangent = layout.send_in(cotangent)
     h_all = layer_norm(x_held.astype(F32), signed_params[0], signed_params[1])
     x_own = x_held[:tall]
     (between, h_own), signed_saved, cotangent = layer_forward(

time: 669 us -> 671 us (level)
  starting transfers between devices: 102 us -> 82 us
  waiting for transfers between devices: 40.7 us -> 59 us
    ppermute x57, starting transfers between devices: 61.6 us -> 39.3 us  [xor_send(): return lax.ppermute(array, axis, [(i, i ^ bit) for i in range(size)])]
    ppermute x57, waiting for transfers between devices: 40.7 us -> 54.3 us  [xor_send(): return lax.ppermute(array, axis, [(i, i ^ bit) for i in range(size)])]
    reshape x10, local copies, waits for them, and re-layouts: 0.06 us -> 6.88 us  [mlp_forward(): row = lambda v: v.reshape(1, -1)]
    unnamed x277 -> x247, local copies, waits for them, and re-layouts: 51.7 us -> 48.5 us
  transfers between devices with their start and end apart: 77 -> 77, of which waited for: 8 -> 17; matrix products, arithmetic and copies ran while one was open for 11% -> 9% of each run, Pallas kernels for 39% -> 39%
where the time goes in v4:
time: 671 us; the launch traced here: 661 us
  Pallas kernels  340 us (51%)
  local copies, waits for them, and re-layouts  91.5 us (14%)
  starting transfers between devices  82 us (12%)
  waiting for transfers between devices  59 us (9%)
  other arithmetic  41.2 us (6%)
  matrix products  36.1 us (5%)
  between operations  11 us (2%)
    pallas_call x5, Pallas kernels, attend_backward(): pl.pallas_call(functools.partial(backward_kernel, head, count, signed), o...  125 us
    pallas_call x2, Pallas kernels, attend_forward(): pl.pallas_call(functools.partial(forward_kernel, head, count, signed), ou...  71.2 us
    ppermute x57, waiting for transfers between devices, xor_send(): return lax.ppermute(array, axis, [(i, i ^ bit) for i in range(size)])  54.3 us
    unnamed x247, local copies, waits for them, and re-layouts  48.5 us
    pallas_call x2, Pallas kernels, mlp_forward(): pl.pallas_call(functools.partial(mlp_kernel, following is not None), out_...  48 us
    ppermute x57, starting transfers between devices, xor_send(): return lax.ppermute(array, axis, [(i, i ^ bit) for i in range(size)])  39.3 us
    pallas_call x2, Pallas kernels, mlp_backward(): pl.pallas_call(mlp_back_kernel, out_shape=out_shape, grid=(hidden // widt...  37.5 us
    dot_general x12, matrix products, dense(): lax.dot_general(left, right, (((left_axis,), (right_axis,)), ((), ())), p...  36.1 us
  transfers between devices with their start and end apart: 77, of which 17 were waited for; matrix products, arithmetic and copies ran while one was open for 9% of the time, Pallas kernels for 39%

profile of v4, /device:TPU:0, one launch (start us, length us, event | category | flops | bytes accessed | tf_op | source)
XLA Modules:
  0.0 660.9 jit_solution(6254838410732025445)
XLA Ops:
  33.6 5.4 concatenate.55.keys
  90.0 41.5 %shard_map.468 = (bf16[4,256,768]{2,1,0:T(8,128)(2,1)S(1)}, f32[12,4,256]{2,1,0:T(4,128)S(1)}) custom-call(s32[8]{0:T(128)S(1)} %copy-done.68, s32[8]{0:T(128)S(1)} %copy-done.67, bf16[4,256,768]{2,1,0:T(8,128)(2,1)S(1)} %bitcast.184, bf16[8,256,768]{2,1,0:T(8,128)(2,1)S(1)} %bitcast.166, bf16[8,256,768]{2,1,0:T(8,128)(2,1)S(1)} %bitcast.170), custom_call_target="tpu_custom_call" | custom-call | flops 49999998976 | bytes 20000000 | tf_op jit(solution)/shard_map/pallas_call | solution.py:156
  133.4 24.2 %shard_map.469 = (f32[1024,768]{1,0:T(8,128)S(1)}, bf16[1024,768]{1,0:T(8,128)(2,1)S(1)}, bf16[1024,3072]{1,0:T(8,128)(2,1)}, bf16[1024,3072]{1,0:T(8,128)(2,1)}...) custom-call(bf16[1024,768]{1,0:T(8,128)(2,1)S(1)} %bitcast.188, bf16[1024,768]{1,0:T(8,128)(2,1)S(1)} %slice.95.x_ref, ...), custom_call_target="tpu_custom_call" | custom-call | flops 10871635968 | bytes 35796480 | tf_op jit(solution)/shard_map/pallas_call | solution.py:797
  170.4 29.7 %shard_map.470 = (bf16[4,256,768]{2,1,0:T(8,128)(2,1)S(1)}, f32[12,4,256]{2,1,0:T(4,128)S(1)}) custom-call(s32[8]{0:T(128)S(1)} %copy-done.68, s32[8]{0:T(128)S(1)} %copy-done.67, bf16[4,256,768]{2,1,0:T(8,128)(2,1)S(1)} %bitcast.193, bf16[8,256,768]{2,1,0:T(8,128)(2,1)S(1)} %bitcast.174, bf16[8,256,768]{2,1,0:T(8,128)(2,1)S(1)} %bitcast.177), custom_call_target="tpu_custom_call" | custom-call | flops 49999998976 | bytes 20000000 | tf_op jit(solution)/shard_map/pallas_call | solution.py:156
  200.2 23.8 %shard_map.471 = (f32[1024,768]{1,0:T(8,128)S(1)}, bf16[1024,768]{1,0:T(8,128)(2,1)S(1)}, bf16[1024,3072]{1,0:T(8,128)(2,1)}, bf16[1024,3072]{1,0:T(8,128)(2,1)}, bf16[1024,768]{1,0:T(8,128)(2,1)}) custom-call(bf16[1024,768]{1,0:T(8,128)(2,1)S(1)} %bitcast.196, f32[1024,768]{1,0:T(8,128)S(1)} %get-tuple-element.379.x_ref, bf16[768,768]{1,0:T(8,128)(2,1)S(1)} %copy-done.16, ...), custom_call_target="tpu_custom_call" | custom-call | flops 10871635968 | bytes 34223616 | tf_op jit(solution)/shard_map/pallas_call | solution.py:797
  232.9 18.0 %shard_map.472 = (bf16[1024,3072]{1,0:T(8,128)(2,1)}, f32[1024,768]{1,0:T(8,128)S(1)}, bf16[1024,768]{1,0:T(8,128)(2,1)S(1)}, bf16[1024,768]{1,0:T(8,128)(2,1)S(...) custom-call(bf16[1024,768]{1,0:T(8,128)(2,1)S(1)} %bitcast.149, ...), custom_call_target="tpu_custom_call" | custom-call | flops 10871635968 | bytes 35805696 | tf_op jit(solution)/shard_map/pallas_call | solution.py:869
  253.2 18.3 %shard_map.473 = (bf16[4,480,768]{2,1,0:T(8,128)(2,1)S(1)}, bf16[4,480,768]{2,1,0:T(8,128)(2,1)}, bf16[4,1,384,768]{3,2,1,0:T(8,128)(2,1)S(1)}, bf16[4,1,384,768]{3,2,1,0:T(8,128)(2,1)}) custom-call(s32[1]{0:T(128)} %bitcast.4.me.core, bf16[1024,768]{1,0:T(8,128)(2,1)S(1)} %copy-done.81, bf16[1024,3072]{1,0:T(8,128)(2,1)} %get-tuple-element.386.du_ref, ...), custom_call_target="tpu_custom_call" | custom-call | flops 10871635968 | bytes 24182784 | tf_op jit(solution)/shard_map/pallas_call | solution.py:942
  288.6 17.3 %shard_map.474 = (bf16[4,256,256]{2,1,0:T(8,128)(2,1)S(1)}, bf16[8,256,256]{2,1,0:T(8,128)(2,1)S(1)}, bf16[8,256,256]{2,1,0:T(8,128)(2,1)S(1)}) custom-call(s32[8]{0:T(128)S(1)} %copy-done.69, s32[8]{0:T(128)S(1)} %copy-done.67, bf16[4,256,768]{2,1,0:T(8,128)(2,1)S(1)} %bitcast.194, bf16[4,256,768]{2,1,0:T(8,128)(2,1)S(1)} %bitcast.198, ...), custom_call_target="tpu_custom_call" | custom-call | flops 24999999488 | bytes 10000000 | tf_op jit(solution)/shard_map/pallas_call | solution.py:266
  314.1 5.7 collective-permute-start.30
  319.9 34.3 %shard_map.475 = (bf16[4,256,512]{2,1,0:T(8,128)(2,1)S(1)}, bf16[8,256,512]{2,1,0:T(8,128)(2,1)S(1)}, bf16[8,256,512]{2,1,0:T(8,128)(2,1)S(1)}) custom-call(s32[8]{0:T(128)S(1)} %copy-done.70, s32[8]{0:T(128)S(1)} %copy-done.67, bf16[4,256,768]{2,1,0:T(8,128)(2,1)S(1)} %bitcast.195, bf16[4,256,768]{2,1,0:T(8,128)(2,1)S(1)} %bitcast.199, ...), custom_call_target="tpu_custom_call" | custom-call | flops 49999998976 | bytes 10000000 | tf_op jit(solution)/shard_map/pallas_call | solution.py:266
  383.8 7.8 %shard_map.476 = (bf16[4,288,768]{2,1,0:T(8,128)(2,1)S(1)}, bf16[4,288,768]{2,1,0:T(8,128)(2,1)S(1)}) custom-call(s32[1]{0:T(128)} %bitcast.4.me.core, bf16[2048,768]{1,0:T(8,128)(2,1)S(1)} %copy-done.11, bf16[1024,256]{1,0:T(8,128)(2,1)S(1)} %bitcast.220, bf16[1024,512]{1,0:T(8,128)(2,1)S(1)} %bitcast.208, bf16[2048,256]{1,0:T(8,128)(2,1)S(1)} %bitcast.205, ...), custom_call_target="tpu_custom_call" | custom-call | flops 6039797760 | bytes 12779520 | tf_op jit(solution)/shard_map/pallas_call | solution.py:990
  404.7 19.4 %shard_map.478 = (bf16[1024,3072]{1,0:T(8,128)(2,1)}, f32[1024,768]{1,0:T(8,128)S(1)}, bf16[1024,768]{1,0:T(8,128)(2,1)S(1)}, bf16[1024,768]{1,0:T(8,128)(2,1)S(...) custom-call(f32[1024,768]{1,0:T(8,128)S(1)} %get-tuple-element.480.g_ref, ...), custom_call_target="tpu_custom_call" | custom-call | flops 10871635968 | bytes 37378560 | tf_op jit(solution)/shard_map/pallas_call | solution.py:869
  430.6 17.0 %shard_map.479 = (bf16[4,480,768]{2,1,0:T(8,128)(2,1)S(1)}, bf16[4,480,768]{2,1,0:T(8,128)(2,1)S(1)}, bf16[4,1,384,768]{3,2,1,0:T(8,128)(2,1)S(1)}, bf16[4,1,384,768]{3,2,1,0:T(8,128)(2,1)S(1)}) custom-call(s32[1]{0:T(128)} %bitcast.4.me.core, bf16[1024,768]{1,0:T(8,128)(2,1)S(1)} %copy-done.79, bf16[1024,3072]{1,0:T(8,128)(2,1)} %get-tuple-element.509.du_ref, ...), custom_call_target="tpu_custom_call" | custom-call | flops 10871635968 | bytes 24182784 | tf_op jit(solution)/shard_map/pallas_call | solution.py:942
  452.2 24.8 %shard_map.482 = (bf16[4,256,256]{2,1,0:T(8,128)(2,1)S(1)}, bf16[8,256,256]{2,1,0:T(8,128)(2,1)S(1)}, bf16[8,256,256]{2,1,0:T(8,128)(2,1)S(1)}) custom-call(s32[8]{0:T(128)S(1)} %copy-done.70, s32[8]{0:T(128)S(1)} %copy-done.67, bf16[4,256,768]{2,1,0:T(8,128)(2,1)S(1)} %bitcast.185, bf16[4,256,768]{2,1,0:T(8,128)(2,1)S(1)} %bitcast.190, ...), custom_call_target="tpu_custom_call" | custom-call | flops 24999999488 | bytes 10000000 | tf_op jit(solution)/shard_map/pallas_call | solution.py:266
  486.3 24.4 %shard_map.483 = (bf16[4,256,256]{2,1,0:T(8,128)(2,1)S(1)}, bf16[8,256,256]{2,1,0:T(8,128)(2,1)S(1)}, bf16[8,256,256]{2,1,0:T(8,128)(2,1)S(1)}) custom-call(s32[8]{0:T(128)S(1)} %copy-done.70, s32[8]{0:T(128)S(1)} %copy-done.67, bf16[4,256,768]{2,1,0:T(8,128)(2,1)S(1)} %bitcast.186, bf16[4,256,768]{2,1,0:T(8,128)(2,1)S(1)} %bitcast.191, ...), custom_call_target="tpu_custom_call" | custom-call | flops 24999999488 | bytes 10000000 | tf_op jit(solution)/shard_map/pallas_call | solution.py:266
  511.0 6.7 %collective-permute-done.49 = bf16[2,1,1,480,768]{4,3,2,1,0:T(8,128)(2,1)S(1)} collective-permute-done((bf16[2,1,1,480,768]{4,3,2,1,0:T(8,128)(2,1)S(1)}, bf16[2,1,1,480,768]{4,3,2,1,0:T(8,128)(2,1)S(1)}, u32[]{:S(2)}, u32[]{:S(2)}) %collective-permute-start.49) | collective-permute-done | bytes 1474592 | tf_op jit(solution)/shard_map/ppermute | solution.py:302
  520.4 24.4 %shard_map.484 = (bf16[4,256,256]{2,1,0:T(8,128)(2,1)S(1)}, bf16[8,256,256]{2,1,0:T(8,128)(2,1)S(1)}, bf16[8,256,256]{2,1,0:T(8,128)(2,1)S(1)}) custom-call(s32[8]{0:T(128)S(1)} %copy-done.70, s32[8]{0:T(128)S(1)} %copy-done.67, bf16[4,256,768]{2,1,0:T(8,128)(2,1)S(1)} %bitcast.187, bf16[4,256,768]{2,1,0:T(8,128)(2,1)S(1)} %bitcast.192, ...), custom_call_target="tpu_custom_call" | custom-call | flops 24999999488 | bytes 10000000 | tf_op jit(solution)/shard_map/pallas_call | solution.py:266
  550.8 5.0 add_convert_fusion
  558.1 7.4 %shard_map.486 = (bf16[4,288,768]{2,1,0:T(8,128)(2,1)S(1)}, bf16[4,288,768]{2,1,0:T(8,128)(2,1)S(1)}) custom-call(s32[1]{0:T(128)} %bitcast.4.me.core, bf16[2048,768]{1,0:T(8,128)(2,1)S(1)} %copy-done.7, bf16[1024,256]{1,0:T(8,128)(2,1)S(1)} %bitcast.218, bf16[1024,256]{1,0:T(8,128)(2,1)S(1)} %bitcast.222, bf16[1024,256]{1,0:T(8,128)(2,1)S(1)} %bitcast.224, ...), custom_call_target="tpu_custom_call" | custom-call | flops 6039797760 | bytes 12779520 | tf_op jit(solution)/shard_map/pallas_call | solution.py:990
  565.7 8.7 %collective-permute-done.56 = bf16[2,432,384]{2,1,0:T(8,128)(2,1)S(1)} collective-permute-done((bf16[2,432,384]{2,1,0:T(8,128)(2,1)S(1)}, bf16[2,432,384]{2,1,0:T(8,128)(2,1)S(1)}, u32[]{:S(2)}, u32[]{:S(2)}) %collective-permute-start.56) | collective-permute-done | bytes 663584 | tf_op jit(solution)/shard_map/ppermute | solution.py:302
  585.0 5.6 collective-permute-done.64
  593.4 6.6 %collective-permute-done.65 = f32[2,768]{1,0:T(2,128)S(1)} collective-permute-done((f32[2,768]{1,0:T(2,128)S(1)}, f32[2,768]{1,0:T(2,128)S(1)}, u32[]{:S(2)}, u32[]{:S(2)}) %collective-permute-start.65) | collective-permute-done | bytes 6176 | tf_op jit(solution)/shard_map/ppermute | solution.py:302
  622.4 10.5 %collective-permute-start.72 = (bf16[256,768]{1,0:T(8,128)(2,1)}, bf16[256,768]{1,0:T(8,128)(2,1)S(1)}, u32[]{:S(2)}, u32[]{:S(2)}) collective-permute-start(bf16[256,768]{1,0:T(8,128)(2,1)} %get-tuple-element.665), channel_id=1, source_target_pairs={{5,0},{4,1},{1,2},{0,3},{7,4},{6,5},{3,6},{2,7},{13,8},{12,9},{9,1... | collective-permute-start | bytes 1179656 | tf_op jit(solution)/shard_map/ppermute | solution.py:465
  639.8 12.6 %collective-permute-done.76 = bf16[1,144,384]{2,1,0:T(8,128)(2,1)S(1)} collective-permute-done((bf16[1,144,384]{2,1,0:T(8,128)(2,1)S(1)}, bf16[1,144,384]{2,1,0:T(8,128)(2,1)S(1)}, u32[]{:S(2)}, u32[]{:S(2)}) %collective-permute-start.76) | collective-permute-done | bytes 110624 | tf_op jit(solution)/shard_map/ppermute | solution.py:302
  (546 shorter events, 250.9 us)
Async XLA Ops:
  20.6 30.8 %collective-permute-start.8 = (bf16[256,768]{1,0:T(8,128)(2,1)}, bf16[256,768]{1,0:T(8,128)(2,1)S(1)}, u32[]{:S(2)}, u32[]{:S(2)}) collective-permute-start(bf16[256,768]{1,0:T(8,128)(2,1)} %get-tuple-element.810), channel_id=1, source_target_pairs={{0,0},{1,1},{2,4},{3,5},{4,2},{5,3},{6,6},{7,7},{8,8},{9,9},{10,12... | collective-permute-start | bytes 1179656 | tf_op jit(solution)/shard_map/ppermute | solution.py:420
  22.2 30.3 %collective-permute-start.9 = (bf16[256,768]{1,0:T(8,128)(2,1)}, bf16[256,768]{1,0:T(8,128)(2,1)S(1)}, u32[]{:S(2)}, u32[]{:S(2)}) collective-permute-start(bf16[256,768]{1,0:T(8,128)(2,1)} %get-tuple-element.809), channel_id=1, source_target_pairs={{0,1},{1,0},{2,5},{3,4},{4,3},{5,2},{6,7},{7,6},{8,9},{9,8},{10,13... | collective-permute-start | bytes 1179656 | tf_op jit(solution)/shard_map/ppermute | solution.py:420
  23.5 34.6 %collective-permute-start.10 = (bf16[256,768]{1,0:T(8,128)(2,1)}, bf16[256,768]{1,0:T(8,128)(2,1)S(1)}, u32[]{:S(2)}, u32[]{:S(2)}) collective-permute-start(bf16[256,768]{1,0:T(8,128)(2,1)} %get-tuple-element.808), channel_id=1, source_target_pairs={{0,4},{1,5},{2,0},{3,1},{4,6},{5,7},{6,2},{7,3},{8,12},{9,13},{10,... | collective-permute-start | bytes 1179656 | tf_op jit(solution)/shard_map/ppermute | solution.py:420
  26.7 32.2 %collective-permute-start.11 = (bf16[256,768]{1,0:T(8,128)(2,1)S(1)}, bf16[256,768]{1,0:T(8,128)(2,1)S(1)}, u32[]{:S(2)}, u32[]{:S(2)}) collective-permute-start(bf16[256,768]{1,0:T(8,128)(2,1)S(1)} %get-tuple-element.807), channel_id=1, source_target_pairs={{0,5},{1,4},{2,1},{3,0},{4,7},{5,6},{6,3},{7,2},{8,13},{9,12},{10,... | collective-permute-start | bytes 1179656 | tf_op jit(solution)/shard_map/ppermute | solution.py:420
  81.4 50.2 %collective-permute-start.16 = (bf16[256,768]{1,0:T(8,128)(2,1)S(1)}, bf16[256,768]{1,0:T(8,128)(2,1)S(1)}, u32[]{:S(2)}, u32[]{:S(2)}) collective-permute-start(bf16[256,768]{1,0:T(8,128)(2,1)S(1)} %get-tuple-element.806), channel_id=1, source_target_pairs={{0,0},{1,1},{2,4},{3,5},{4,2},{5,3},{6,6},{7,7},{8,8},{9,9},{10,12... | collective-permute-start | bytes 1179656 | tf_op jit(solution)/shard_map/ppermute | solution.py:420
  82.2 49.4 %collective-permute-start.17 = (bf16[256,768]{1,0:T(8,128)(2,1)S(1)}, bf16[256,768]{1,0:T(8,128)(2,1)S(1)}, u32[]{:S(2)}, u32[]{:S(2)}) collective-permute-start(bf16[256,768]{1,0:T(8,128)(2,1)S(1)} %get-tuple-element.805), channel_id=1, source_target_pairs={{0,1},{1,0},{2,5},{3,4},{4,3},{5,2},{6,7},{7,6},{8,9},{9,8},{10,13... | collective-permute-start | bytes 1179656 | tf_op jit(solution)/shard_map/ppermute | solution.py:420
  85.8 45.8 %collective-permute-start.18 = (bf16[256,768]{1,0:T(8,128)(2,1)S(1)}, bf16[256,768]{1,0:T(8,128)(2,1)S(1)}, u32[]{:S(2)}, u32[]{:S(2)}) collective-permute-start(bf16[256,768]{1,0:T(8,128)(2,1)S(1)} %get-tuple-element.804), channel_id=1, source_target_pairs={{0,4},{1,5},{2,0},{3,1},{4,6},{5,7},{6,2},{7,3},{8,12},{9,13},{10,... | collective-permute-start | bytes 1179656 | tf_op jit(solution)/shard_map/ppermute | solution.py:420
  89.7 41.9 %collective-permute-start.19 = (bf16[256,768]{1,0:T(8,128)(2,1)S(1)}, bf16[256,768]{1,0:T(8,128)(2,1)S(1)}, u32[]{:S(2)}, u32[]{:S(2)}) collective-permute-start(bf16[256,768]{1,0:T(8,128)(2,1)S(1)} %get-tuple-element.803), channel_id=1, source_target_pairs={{0,5},{1,4},{2,1},{3,0},{4,7},{5,6},{6,3},{7,2},{8,13},{9,12},{10,... | collective-permute-start | bytes 1179656 | tf_op jit(solution)/shard_map/ppermute | solution.py:420
  226.8 44.7 %collective-permute-start.25 = (bf16[4,256,768]{2,1,0:T(8,128)(2,1)}, bf16[4,256,768]{2,1,0:T(8,128)(2,1)}, u32[]{:S(2)}, u32[]{:S(2)}) collective-permute-start(bf16[4,256,768]{2,1,0:T(8,128)(2,1)} %bitcast.28), channel_id=1, source_target_pairs={{0,4},{4,0},{8,12},{12,8},{16,20},{20,16},{24,28},{28,24},{1,5},{5... | collective-permute-start | bytes 4718600 | tf_op jit(solution)/shard_map/ppermute | solution.py:302
  275.9 33.2 %collective-permute-start.28 = (bf16[4,480,768]{2,1,0:T(8,128)(2,1)}, bf16[4,480,768]{2,1,0:T(8,128)(2,1)}, u32[]{:S(2)}, u32[]{:S(2)}) collective-permute-start(bf16[4,480,768]{2,1,0:T(8,128)(2,1)} %get-tuple-element.415), channel_id=1, source_target_pairs={{0,4},{4,0},{8,12},{12,8},{16,20},{20,16},{24,28},{28,24},{1,5},{5... | collective-permute-start | bytes 8847368 | tf_op jit(solution)/shard_map/ppermute | solution.py:302
  276.1 29.9 %collective-permute-start.29 = (bf16[4,384,768]{2,1,0:T(8,128)(2,1)}, bf16[4,384,768]{2,1,0:T(8,128)(2,1)}, u32[]{:S(2)}, u32[]{:S(2)}) collective-permute-start(bf16[4,384,768]{2,1,0:T(8,128)(2,1)} %bitcast.30), channel_id=1, source_target_pairs={{0,4},{4,0},{8,12},{12,8},{16,20},{20,16},{24,28},{28,24},{1,5},{5... | collective-permute-start | bytes 7077896 | tf_op jit(solution)/shard_map/ppermute | solution.py:302
  276.5 35.6 %collective-permute-start.26 = (bf16[256,768]{1,0:T(8,128)(2,1)}, bf16[256,768]{1,0:T(8,128)(2,1)S(1)}, u32[]{:S(2)}, u32[]{:S(2)}) collective-permute-start(bf16[256,768]{1,0:T(8,128)(2,1)} %get-tuple-element.410), channel_id=1, source_target_pairs={{0,0},{1,1},{4,2},{5,3},{2,4},{3,5},{6,6},{7,7},{8,8},{9,9},{12,10... | collective-permute-start | bytes 1179656 | tf_op jit(solution)/shard_map/ppermute | solution.py:465
  278.1 34.0 %collective-permute-start.27 = (bf16[256,768]{1,0:T(8,128)(2,1)}, bf16[256,768]{1,0:T(8,128)(2,1)S(1)}, u32[]{:S(2)}, u32[]{:S(2)}) collective-permute-start(bf16[256,768]{1,0:T(8,128)(2,1)} %get-tuple-element.411), channel_id=1, source_target_pairs={{1,0},{0,1},{5,2},{4,3},{3,4},{2,5},{7,6},{6,7},{9,8},{8,9},{13,10... | collective-permute-start | bytes 1179656 | tf_op jit(solution)/shard_map/ppermute | solution.py:465
  312.5 41.7 %collective-permute-start.33 = (bf16[1,2,1,384,768]{4,3,2,1,0:T(8,128)(2,1)S(1)}, bf16[1,2,1,384,768]{4,3,2,1,0:T(8,128)(2,1)S(1)}, u32[]{:S(2)}, u32[]{:S(2)}) collective-permute-start(bf16[1,2,1,384,768]{4,3,2,1,0:T(8,128)(2,1)S(1)} %get-tuple-element.439), channel_id=1, source_target_pairs={{0,16},{4,20},{8,24},{12,28},{16,0},{20,4},{24,8},{28,12},{1,17},{... | collective-permute-start | bytes 3538952 | tf_op jit(solution)/shard_map/ppermute | solution.py:302
  314.1 40.5 %collective-permute-start.32 = (bf16[2,1,1,480,768]{4,3,2,1,0:T(8,128)(2,1)S(1)}, bf16[2,1,1,480,768]{4,3,2,1,0:T(8,128)(2,1)S(1)}, u32[]{:S(2)}, u32[]{:S(2)}) collective-permute-start(bf16[2,1,1,480,768]{4,3,2,1,0:T(8,128)(2,1)S(1)} %get-tuple-element.437), channel_id=1, source_target_pairs={{0,8},{4,12},{8,0},{12,4},{16,24},{20,28},{24,16},{28,20},{1,9},{5... | collective-permute-start | bytes 4423688 | tf_op jit(solution)/shard_map/ppermute | solution.py:302
  314.1 41.8 %collective-permute-start.30 = (bf16[256,768]{1,0:T(8,128)(2,1)S(1)}, bf16[256,768]{1,0:T(8,128)(2,1)S(1)}, u32[]{:S(2)}, u32[]{:S(2)}) collective-permute-start(bf16[256,768]{1,0:T(8,128)(2,1)S(1)} %copy-done.97), channel_id=1, source_target_pairs={{4,0},{5,1},{0,2},{1,3},{6,4},{7,5},{2,6},{3,7},{12,8},{13,9},{8,1... | collective-permute-start | bytes 1179656 | tf_op jit(solution)/shard_map/ppermute | solution.py:465
  319.9 36.0 %collective-permute-start.31 = (bf16[256,768]{1,0:T(8,128)(2,1)S(1)}, bf16[256,768]{1,0:T(8,128)(2,1)S(1)}, u32[]{:S(2)}, u32[]{:S(2)}) collective-permute-start(bf16[256,768]{1,0:T(8,128)(2,1)S(1)} %copy-done.96), channel_id=1, source_target_pairs={{5,0},{4,1},{1,2},{0,3},{7,4},{6,5},{3,6},{2,7},{13,8},{12,9},{9,1... | collective-permute-start | bytes 1179656 | tf_op jit(solution)/shard_map/ppermute | solution.py:465
  448.2 30.0 %collective-permute-start.45 = (bf16[4,480,768]{2,1,0:T(8,128)(2,1)S(1)}, bf16[4,480,768]{2,1,0:T(8,128)(2,1)}, u32[]{:S(2)}, u32[]{:S(2)}) collective-permute-start(bf16[4,480,768]{2,1,0:T(8,128)(2,1)S(1)} %get-tuple-element.545), channel_id=1, source_target_pairs={{0,4},{4,0},{8,12},{12,8},{16,20},{20,16},{24,28},{28,24},{1,5},{5... | collective-permute-start | bytes 8847368 | tf_op jit(solution)/shard_map/ppermute | solution.py:302
  448.3 28.9 %collective-permute-start.46 = (bf16[4,384,768]{2,1,0:T(8,128)(2,1)S(1)}, bf16[4,384,768]{2,1,0:T(8,128)(2,1)S(1)}, u32[]{:S(2)}, u32[]{:S(2)}) collective-permute-start(bf16[4,384,768]{2,1,0:T(8,128)(2,1)S(1)} %bitcast.165), channel_id=1, source_target_pairs={{0,4},{4,0},{8,12},{12,8},{16,20},{20,16},{24,28},{28,24},{1,5},{5... | collective-permute-start | bytes 7077896 | tf_op jit(solution)/shard_map/ppermute | solution.py:302
  481.3 29.4 %collective-permute-start.51 = (f32[16,768]{1,0:T(8,128)S(1)}, f32[16,768]{1,0:T(8,128)S(1)}, u32[]{:S(2)}, u32[]{:S(2)}) collective-permute-start(f32[16,768]{1,0:T(8,128)S(1)} %add.513), channel_id=1, source_target_pairs={{0,2},{1,3},{2,0},{3,1},{4,6},{5,7},{6,4},{7,5},{8,10},{9,11},{10,... | collective-permute-start | bytes 147464 | tf_op jit(solution)/shard_map/ppermute | solution.py:302
  481.3 29.3 %collective-permute-start.50 = (bf16[1,2,1,384,768]{4,3,2,1,0:T(8,128)(2,1)S(1)}, bf16[1,2,1,384,768]{4,3,2,1,0:T(8,128)(2,1)S(1)}, u32[]{:S(2)}, u32[]{:S(2)}) collective-permute-start(bf16[1,2,1,384,768]{4,3,2,1,0:T(8,128)(2,1)S(1)} %get-tuple-element.567), channel_id=1, source_target_pairs={{0,16},{4,20},{8,24},{12,28},{16,0},{20,4},{24,8},{28,12},{1,17},{... | collective-permute-start | bytes 3538952 | tf_op jit(solution)/shard_map/ppermute | solution.py:302
  484.5 33.1 %collective-permute-start.49 = (bf16[2,1,1,480,768]{4,3,2,1,0:T(8,128)(2,1)S(1)}, bf16[2,1,1,480,768]{4,3,2,1,0:T(8,128)(2,1)S(1)}, u32[]{:S(2)}, u32[]{:S(2)}) collective-permute-start(bf16[2,1,1,480,768]{4,3,2,1,0:T(8,128)(2,1)S(1)} %get-tuple-element.565), channel_id=1, source_target_pairs={{0,8},{4,12},{8,0},{12,4},{16,24},{20,28},{24,16},{28,20},{1,9},{5... | collective-permute-start | bytes 4423688 | tf_op jit(solution)/shard_map/ppermute | solution.py:302
  486.2 31.9 %collective-permute-start.48 = (bf16[1,144,384]{2,1,0:T(8,128)(2,1)S(1)}, bf16[1,144,384]{2,1,0:T(8,128)(2,1)S(1)}, u32[]{:S(2)}, u32[]{:S(2)}) collective-permute-start(bf16[1,144,384]{2,1,0:T(8,128)(2,1)S(1)} %get-tuple-element.563), channel_id=1, source_target_pairs={{0,2},{1,3},{2,0},{3,1},{4,6},{5,7},{6,4},{7,5},{8,10},{9,11},{10,... | collective-permute-start | bytes 331784 | tf_op jit(solution)/shard_map/ppermute | solution.py:302
  622.4 30.7 %collective-permute-start.72 = (bf16[256,768]{1,0:T(8,128)(2,1)}, bf16[256,768]{1,0:T(8,128)(2,1)S(1)}, u32[]{:S(2)}, u32[]{:S(2)}) collective-permute-start(bf16[256,768]{1,0:T(8,128)(2,1)} %get-tuple-element.665), channel_id=1, source_target_pairs={{5,0},{4,1},{1,2},{0,3},{7,4},{6,5},{3,6},{2,7},{13,8},{12,9},{9,1... | collective-permute-start | bytes 1179656 | tf_op jit(solution)/shard_map/ppermute | solution.py:465
  (168 other events, 2030.0 us)
